TPU v7x, 256 devices: a whole 4x4x8 slice. The times are simulated.
256 devices in a mesh: dp: 32 (over x, z_hi, y), tensor: 8 (over z_lo, core).
Axes of the slice: x: 4, y: 4, z: 8 (z_hi: 2, z_lo: 4; z = z_hi * 4 + z_lo), core: 2. Of those that a mesh axis runs over, the one named last changes fastest.
Arguments:
- context: bfloat16 [8192, 3072], P('dp', 'tensor'), may hold values from -6 to 6
- residual: bfloat16 [8192, 6144], P(('dp', 'tensor')), may hold values from -6 to 6
- out_proj: bfloat16 [6144, 3072], P('dp', 'tensor'), may hold values from -0.109375 to 0.109375
- norm_gain: float32 [6144], replicated, may hold values from 0.25 to 1.75
- cotangent: bfloat16 [8192, 6144], P(('dp', 'tensor')), may hold values from -0.75 to 0.75
- probe_seed: int32 [2], replicated, may hold values from 0 to 999999999
Outputs:
- hess_diag: float32 [6144, 3072], P('dp', 'tensor')
All inputs are finite; a program needn't handle non-finite values.
Results may differ from a plain program's by a relative error of at most 0.0029.
Values may be sent and summed in bfloat16 or wider, within the bound.
No kernel may reach another device: no remote copies, remote signals or barrier semaphores. Data moves between devices by JAX's collectives and lax.ppermute only.
A program may use at most 128 MiB of HBM per device.

v0:
```python
import jax
import jax.numpy as jnp
from jax import lax
from jax.sharding import PartitionSpec as P


def probe_signs(seed_pair, row_ids, col_ids, full_width):
    flat_index = row_ids[:, None] * jnp.int32(full_width) + col_ids[None, :]
    mixed = flat_index * jnp.int32(747796405) + seed_pair[0]
    mixed = mixed ^ lax.shift_right_logical(mixed, jnp.int32(16))
    mixed = mixed * jnp.int32(73244475)
    mixed = mixed ^ seed_pair[1]
    mixed = mixed ^ lax.shift_right_logical(mixed, jnp.int32(15))
    parity = lax.shift_right_logical(mixed, jnp.int32(9)) & jnp.int32(1)
    return (jnp.int32(1) - jnp.int32(2) * parity).astype(jnp.bfloat16)


def norm_gradient(stream, norm_gain, cotangent):

    def linear_loss(values):
        row_mean = jnp.mean(values, axis=-1, keepdims=True)
        centered = values - row_mean
        variance = jnp.mean(centered * centered, axis=-1, keepdims=True)
        normed = centered * lax.rsqrt(variance + 1e-05)
        return jnp.sum(cotangent.astype(jnp.float32) * norm_gain * normed)

    return jax.grad(linear_loss)(stream)


def on_device(context, residual, out_proj, norm_gain, cotangent, probe_seed):
    heads_local = context.shape[1]
    owned_count = out_proj.shape[0]
    model_width = owned_count * lax.axis_size("dp")
    feature_count = heads_local * lax.axis_size("tensor")
    head_ids = lax.axis_index("tensor") * heads_local + jnp.arange(heads_local)
    probe = probe_signs(probe_seed, jnp.arange(model_width), head_ids, feature_count)
    primal_part = jnp.dot(
        context,
        lax.all_gather(out_proj, "dp", axis=0, tiled=True).T,
        preferred_element_type=jnp.float32,
    )
    primal = lax.psum_scatter(primal_part, "tensor", scatter_dimension=0, tiled=True)
    tangent = lax.psum_scatter(
        jnp.dot(context, probe.T, preferred_element_type=jnp.float32),
        "tensor",
        scatter_dimension=0,
        tiled=True,
    )
    stream = residual.astype(jnp.float32) + primal
    tangent_grad = jax.jvp(
        lambda values: norm_gradient(values, norm_gain, cotangent), (stream,), (tangent,)
    )[1]
    tangent_grad = tangent_grad.astype(jnp.bfloat16)
    full_tangent = lax.all_gather(tangent_grad, "tensor", axis=0, tiled=True)
    own_probe = lax.dynamic_slice_in_dim(probe, lax.axis_index("dp") * owned_count, owned_count, 0)
    curvature = lax.psum_scatter(
        lax.dot_general(
            full_tangent, context, (((0,), (0,)), ((), ())), preferred_element_type=jnp.float32
        ),
        "dp",
        scatter_dimension=0,
        tiled=True,
    )
    return own_probe.astype(jnp.float32) * curvature


def solution(mesh):
    in_specs = (
        P("dp", "tensor"),
        P(("dp", "tensor"), None),
        P("dp", "tensor"),
        P(),
        P(("dp", "tensor"), None),
        P(),
    )
    out_specs = P("dp", "tensor")
    return jax.shard_map(
        on_device, mesh=mesh, in_specs=in_specs, out_specs=out_specs, check_vma=False
    )
```

profile of v0, /device:TPU:32, one launch (start us, length us, event | category | flops | bytes accessed | tf_op | source)
XLA Modules:
  0.0 574.6 jit_solution(3135948826300439928)
XLA Ops:
  7.4 0.0 copy-start
  7.4 0.7 all-gather.3.cloned.1.call-update
  8.1 0.0 reduce-scatter.10.cloned.1.call-start
  8.2 1.3 fusion.20
  9.5 8.5 %convolution_bitcast_fusion = f32[256,6144]{0,1:T(8,128)} fusion(bf16[256,384]{1,0:T(8,128)(2,1)S(1)} %copy-done, s32[]{:T(128)} %bitcast.1, s32[]{:T(128)} %bitcast, s32[384]{0:T(512)S(1)} %iota_add_fusion, s32[6144]{0:T(1024)S(1)} %iota_multiply_fusion), kind=kOutput, calls=%fused_computation.9 | convolution fusion | flops 1240989696 | bytes 6514184 | tf_op jit(solution)/shard_map/dot_general | solution.py:44
  18.0 6.6 %copy.18 = f32[256,6144]{1,0:T(8,128)} copy(f32[256,6144]{0,1:T(8,128)} %convolution_bitcast_fusion) | data formatting | bytes 12582912
  24.6 0.0 reduce-scatter.10.cloned.1.call-update
  24.6 0.0 copy-start.1
  24.7 0.0 copy-start.2
  24.7 0.0 copy-start.3
  24.7 0.0 reduce-scatter.12.cloned.1.call-start
  24.7 112.5 %all-gather.3.cloned.1.call-done = bf16[6144,384]{1,0:T(8,128)(2,1)} async-done(((bf16[192,384]{1,0:T(8,128)(2,1)}), bf16[6144,384]{1,0:T(8,128)(2,1)}) %all-gather.3.cloned.1.call-update) | async-done | bytes 4718608 | tf_op jit(solution)/shard_map/all_gather | solution.py:39
  137.3 6.9 %fusion.21 = f32[256,6144]{1,0:T(8,128)} fusion(bf16[256,384]{1,0:T(8,128)(2,1)S(1)} %copy-done, bf16[6144,384]{1,0:T(8,128)(2,1)} %all-gather.3.cloned.1.call-done), kind=kOutput, calls=%fused_computation.43 | convolution fusion | flops 1207959552 | bytes 11206656
  144.2 0.0 reduce-scatter.12.cloned.1.call-update
  144.2 0.0 all-gather.5.cloned.1.call-start
  144.2 0.0 reduce-scatter.10.cloned.1.call-done
  144.3 1.3 reduce_sum.62
  145.6 71.1 %reduce-scatter.12.cloned.1.call-done = f32[32,6144]{1,0:T(8,128)} async-done(((f32[256,6144]{1,0:T(8,128)}), f32[32,6144]{1,0:T(8,128)}) %reduce-scatter.12.cloned.1.call-update) | async-done | bytes 786448 | tf_op jit(solution)/shard_map/reduce_scatter | solution.py:42
  216.6 1.3 fusion.17
  217.9 0.0 copy-done.2
  218.0 0.0 copy-done.3
  218.0 1.9 multiply_reduce_fusion
  219.9 1.9 fusion.18
  221.8 0.9 add_convert_fusion
  222.7 0.0 all-gather.5.cloned.1.call-update
  222.7 0.0 reduce-scatter.8.cloned.1.call-start
  222.7 43.0 %all-gather.5.cloned.1.call-done = bf16[256,6144]{1,0:T(8,128)(2,1)} async-done(((bf16[32,6144]{1,0:T(8,128)(2,1)}), bf16[256,6144]{1,0:T(8,128)(2,1)}) %all-gather.5.cloned.1.call-update) | async-done | bytes 3145744 | tf_op jit(solution)/shard_map/all_gather | solution.py:54
  265.7 7.4 %fusion.22 = f32[6144,384]{1,0:T(8,128)} fusion(bf16[256,6144]{1,0:T(8,128)(2,1)} %all-gather.5.cloned.1.call-done, bf16[256,384]{1,0:T(8,128)(2,1)S(1)} %copy-done), kind=kOutput, calls=%fused_computation.44 | convolution fusion | flops 1207959552 | bytes 12779520 | tf_op jit(solution)/shard_map/dot_general | solution.py:57
  273.1 0.0 reduce-scatter.8.cloned.1.call-update
  273.1 7.2 %fusion.6 = bf16[6144,384]{1,0:T(8,128)(2,1)} fusion(s32[]{:T(128)} %bitcast.1, s32[]{:T(128)} %bitcast, s32[384]{0:T(512)S(1)} %iota_add_fusion, s32[6144]{0:T(1024)S(1)} %iota_multiply_fusion), kind=kLoop, calls=%fused_computation.8 | loop fusion | flops 33030144 | bytes 4744712 | tf_op jit(solution)/shard_map/convert_element_type | solution.py:15
  280.4 284.9 %reduce-scatter.8.cloned.1.call-done = f32[192,384]{1,0:T(8,128)} async-done(((f32[6144,384]{1,0:T(8,128)}), f32[192,384]{1,0:T(8,128)}) %reduce-scatter.8.cloned.1.call-update) | async-done | bytes 294928 | tf_op jit(solution)/shard_map/reduce_scatter | solution.py:56
  565.3 1.7 convert_multiply_fusion.1
  (10 shorter events, 0.1 us)
Async XLA Ops:
  7.4 2.1 copy-start
  7.4 129.9 %all-gather.3.cloned.1.call-start = ((), (), s32[]{:S(2)}) async-start(), calls=%async_computation.3 | async-start | bytes 4866048 | tf_op jit(solution)/shard_map/all_gather | solution.py:39
  8.1 136.2 %reduce-scatter.10.cloned.1.call-start = ((), (), s32[]{:S(2)}) async-start(), calls=%async_computation.6 | async-start | bytes 7077888 | tf_op jit(solution)/shard_map/reduce_scatter | solution.py:43
  24.6 192.0 %copy-start.1 = (bf16[32,6144]{1,0:T(8,128)(2,1)S(1)}, bf16[32,6144]{1,0:T(8,128)(2,1)}, u32[]{:S(2)}) copy-start(bf16[32,6144]{1,0:T(8,128)(2,1)} %param.7) | copy-start | bytes 1179652
  24.7 193.3 %copy-start.2 = (bf16[32,6144]{1,0:T(8,128)(2,1)S(1)}, bf16[32,6144]{1,0:T(8,128)(2,1)}, u32[]{:S(2)}) copy-start(bf16[32,6144]{1,0:T(8,128)(2,1)} %param.10) | copy-start | bytes 1179652
  24.7 193.3 %copy-start.3 = (f32[6144]{0:T(1024)S(1)}, f32[6144]{0:T(1024)}, u32[]{:S(2)}) copy-start(f32[6144]{0:T(1024)} %param.9) | copy-start | bytes 73732
  24.7 191.9 %reduce-scatter.12.cloned.1.call-start = ((), (), s32[]{:S(2)}) async-start(), calls=%async_computation.7 | async-start | bytes 7077888 | tf_op jit(solution)/shard_map/reduce_scatter | solution.py:42
  144.2 121.6 %all-gather.5.cloned.1.call-start = ((), (), s32[]{:S(2)}) async-start(), calls=%async_computation.4 | async-start | bytes 3538944 | tf_op jit(solution)/shard_map/all_gather | solution.py:54
  222.7 342.6 %reduce-scatter.8.cloned.1.call-start = ((), (), s32[]{:S(2)}) async-start(), calls=%async_computation.5 | async-start | bytes 9732096 | tf_op jit(solution)/shard_map/reduce_scatter | solution.py:56
Sparse Core Ops, SparseCore 0:
  11.7 125.5 all-gather.2
  273.2 291.9 reduce-scatter.7
Sparse Core Ops, SparseCore 1:
  24.7 115.8 reduce-scatter.9
  144.3 72.3 reduce-scatter.11
  222.8 42.9 all-gather.4
where the time goes:
time: 577 us; the launch traced here: 575 us
  waiting for transfers between devices  512 us (89%)
  matrix products  22.7 us (4%)
  other arithmetic  16.3 us (3%)
  between operations  15.1 us (3%)
  local copies, waits for them, and re-layouts  7.96 us (1%)
    reduce_scatter x1, waiting for transfers between devices, on_device(): lax.psum_scatter(lax.dot_general(full_tangent, context, (((0,), (0,)), ((...  285 us
    all_gather x1, waiting for transfers between devices, on_device(): lax.all_gather(out_proj, 'dp', axis=0, tiled=True)  113 us
    reduce_scatter x1, waiting for transfers between devices, on_device(): lax.psum_scatter(primal_part, 'tensor', scatter_dimension=0, tiled=True)  71.1 us
    all_gather x1, waiting for transfers between devices, on_device(): full_tangent = lax.all_gather(tangent_grad, 'tensor', axis=0, tiled=True)  43 us
  transfers between devices with their start and end apart: 5, of which 4 were waited for; matrix products, arithmetic and copies ran while one was open for 6% of the time, Pallas kernels for 0%

commit v1 on v0

v1 whole, which is shorter than its diff:
```python
import jax
import jax.numpy as jnp
from jax import lax
from jax.experimental import pallas as pl
from jax.experimental.pallas import tpu as pltpu
from jax.sharding import Mesh
from jax.sharding import PartitionSpec as P

AXES = ("x", "zh", "y", "zl", "c")
GRID = (4, 2, 4, 4, 2)
Z = ("zh", "zl")
XY = ("x", "y")
T = ("zl", "c")
R = 192
F = 384
W = 8 * F
OWN = 32
HALF = OWN // 2
TOK = 16 * OWN
D = 2 * R
N = 32 * R
VMEM = 48 * 1024 * 1024
MULT = 747796405
INT = jnp.int32
F32 = jnp.float32
BF16 = jnp.bfloat16
NT = (((1,), (1,)), ((), ()))


def shift(v, axis, k):
    n = 8 if axis == Z else 4
    return lax.ppermute(v, axis, [(s, (s + k) % n) for s in range(n)])


def probe_kernel(info, out):
    x, y, seed0, seed1 = info[0], info[1], info[4], info[5]
    cols = lax.broadcasted_iota(INT, (1, F), 1) + pl.program_id(0) * F
    rows = lax.broadcasted_iota(INT, (R, 1), 0)
    for zh in range(2):
        d = rows + (x * 8 + zh * 4 + y) * R
        m = (d * W * INT(MULT) + seed0) + cols * INT(MULT)
        m = m ^ lax.shift_right_logical(m, INT(16))
        m = m * INT(73244475)
        m = m ^ seed1
        m = m ^ lax.shift_right_logical(m, INT(15))
        parity = lax.shift_right_logical(m, INT(9)) & INT(1)
        out[zh * R : (zh + 1) * R, :] = (1 - 2 * parity).astype(F32).astype(BF16)


def make_probe(info):
    return pl.pallas_call(
        probe_kernel,
        grid=(8,),
        in_specs=[pl.BlockSpec(memory_space=pltpu.SMEM)],
        out_specs=pl.BlockSpec((D, F), lambda j: (0, j)),
        out_shape=jax.ShapeDtypeStruct((D, W), BF16),
        compiler_params=pltpu.CompilerParams(vmem_limit_bytes=VMEM),
        cost_estimate=pl.CostEstimate(flops=14 * D * W, bytes_accessed=2 * D * W, transcendentals=0),
    )(info)


def chip_of(i, zr):
    k = (i % 2) * 4 + i // 2
    return k, (zr - k + 8) % 8


def forward_kernel(info, *refs):
    pieces, (own, other, probe, rc, gain), (context, s_out, u_out, w_out, stats), (acc_p, acc_u) = (
        refs[:8],
        refs[8:13],
        refs[13:18],
        refs[18:],
    )
    i = pl.program_id(0)
    x, y, zr, c = info[0], info[1], info[2], info[3]
    zh = chip_of(i, zr)[1] // 4

    @pl.when(i == 0)
    def _():
        acc_p[...] = jnp.zeros_like(acc_p)
        acc_u[...] = jnp.zeros_like(acc_u)

    @pl.when(i % 2 == 0)
    def _():
        for first in range(4):
            for second in range(4):
                ax, ay = (x - second + 4) % 4, (y - first + 4) % 4
                row = pl.multiple_of((ax * 4 + ay) * OWN, OWN)
                context[pl.ds(row, HALF), :] = pieces[first][second]
                ax, ay = (x - first + 4) % 4, (y - second + 4) % 4
                row = pl.multiple_of((ax * 4 + ay) * OWN + HALF, HALF)
                context[pl.ds(row, HALF), :] = pieces[4 + first][second]

    mine = context[:, pl.ds(pl.multiple_of(c * F, F), F)]
    theirs = context[:, pl.ds(pl.multiple_of((1 - c) * F, F), F)]
    acc_p[zh] += lax.dot_general(own[0], mine, NT, preferred_element_type=F32) + lax.dot_general(
        other[0], theirs, NT, preferred_element_type=F32
    )
    acc_u[zh] += lax.dot_general(probe[...], context[...], NT, preferred_element_type=F32)

    @pl.when(i == 7)
    def _():
        eye = (lax.broadcasted_iota(INT, (D, D), 0) == lax.broadcasted_iota(INT, (D, D), 1)).astype(F32).astype(BF16)
        residual = rc[:, 0].reshape(TOK, D)
        cotangent = rc[:, 1].reshape(TOK, D)
        s = lax.dot_general(eye, residual, NT, preferred_element_type=F32) + acc_p[...].reshape(D, TOK)
        u = acc_u[...].reshape(D, TOK)
        w = lax.dot_general(eye, cotangent, NT, preferred_element_type=F32) * gain[...]
        s_out[...] = s
        u_out[...] = u
        w_out[...] = w
        mean = lambda v: jnp.sum(v, axis=0, keepdims=True) * (1.0 / D)
        ms, mu, mw = mean(s), mean(u), mean(w)
        sc, uc, wc = s - ms, u - mu, w - mw
        stats[0:1] = ms
        stats[1:2] = mu
        stats[2:3] = mw
        stats[3:4] = mean(sc * sc)
        stats[4:5] = mean(sc * uc)
        stats[5:6] = mean(sc * wc)
        stats[6:7] = mean(uc * wc)
        stats[7:8] = jnp.zeros_like(ms)


def forward(info, pieces, own, other, probe, rc, gain):
    whole = lambda *shape: pl.BlockSpec(shape, lambda i, info: (0,) * len(shape))
    zl = lambda i, info: chip_of(i, info[2])[1] % 4
    zh = lambda i, info: chip_of(i, info[2])[1] // 4
    return pl.pallas_call(
        forward_kernel,
        grid_spec=pltpu.PrefetchScalarGridSpec(
            num_scalar_prefetch=1,
            grid=(8,),
            in_specs=[pl.BlockSpec((4, HALF, 2 * F), lambda i, info: (0, 0, zl(i, info)))] * 8
            + [pl.BlockSpec((1, R, F), lambda i, info: (chip_of(i, info[2])[0], 0, 0))] * 2
            + [
                pl.BlockSpec((R, 2 * F), lambda i, info: (zh(i, info), zl(i, info))),
                whole(16, 2, OWN, D),
                whole(D, 1),
            ],
            out_specs=[pl.BlockSpec((TOK, 2 * F), lambda i, info: (0, zl(i, info)))]
            + [whole(D, TOK)] * 3
            + [whole(8, TOK)],
            scratch_shapes=[pltpu.VMEM((2, R, TOK), F32)] * 2,
        ),
        out_shape=[jax.ShapeDtypeStruct((TOK, W), BF16)]
        + [jax.ShapeDtypeStruct((D, TOK), F32)] * 3
        + [jax.ShapeDtypeStruct((8, TOK), F32)],
        compiler_params=pltpu.CompilerParams(vmem_limit_bytes=VMEM),
        cost_estimate=pl.CostEstimate(flops=4 * D * TOK * W, bytes_accessed=12 * TOK * W, transcendentals=0),
    )(info, *pieces, own, other, probe, rc, gain)


def curvature_kernel(info, stats, s, u, w, context, send, keep, grad):
    c = info[3]

    @pl.when(pl.program_id(0) == 0)
    def _():
        parts = [stats[j] for j in range(16)]
        total = parts[0]
        for part in parts[1:]:
            total = total + part
        mean = total * (1.0 / 16)
        ms, mu, mw = mean[0:1], mean[1:2], mean[2:3]
        css, csu, csw, cuw = mean[3:4], mean[4:5], mean[5:6], mean[6:7]
        for part in parts:
            ds, du, dw = part[0:1] - ms, part[1:2] - mu, part[2:3] - mw
            css = css + ds * ds * (1.0 / 16)
            csu = csu + ds * du * (1.0 / 16)
            csw = csw + ds * dw * (1.0 / 16)
            cuw = cuw + du * dw * (1.0 / 16)
        r2 = 1.0 / (css + 1e-05)
        r = lax.rsqrt(css + 1e-05)
        k = -(r * r2)
        gamma = cuw - 3.0 * r2 * csu * csw
        value = k * (csu * (w[...] - mw) + csw * (u[...] - mu) + gamma * (s[...] - ms))
        grad[...] = value.astype(BF16)

    mine = context[:, pl.ds(pl.multiple_of(c * F, F), F)]
    theirs = context[:, pl.ds(pl.multiple_of((1 - c) * F, F), F)]
    send[:, 0] = jnp.dot(grad[...], theirs, preferred_element_type=F32).astype(BF16).reshape(2, R, F)
    keep[:, 0] = jnp.dot(grad[...], mine, preferred_element_type=F32).reshape(2, R, F)


def curvature_parts(info, stats, s, u, w, context):
    whole = lambda *shape: pl.BlockSpec(shape, lambda i, info: (0,) * len(shape))
    out = pl.BlockSpec((2, 1, R, F), lambda i, info: (0, i, 0, 0))
    return pl.pallas_call(
        curvature_kernel,
        grid_spec=pltpu.PrefetchScalarGridSpec(
            num_scalar_prefetch=1,
            grid=(4,),
            in_specs=[whole(16, 8, TOK)]
            + [whole(D, TOK)] * 3
            + [pl.BlockSpec((TOK, 2 * F), lambda i, info: (0, i))],
            out_specs=[out, out],
            scratch_shapes=[pltpu.VMEM((D, TOK), BF16)],
        ),
        out_shape=[
            jax.ShapeDtypeStruct((2, 4, R, F), BF16),
            jax.ShapeDtypeStruct((2, 4, R, F), F32),
        ],
        compiler_params=pltpu.CompilerParams(vmem_limit_bytes=VMEM),
        cost_estimate=pl.CostEstimate(flops=2 * D * TOK * W, bytes_accessed=8 * TOK * W, transcendentals=0),
    )(info, stats, s, u, w, context)


def ring_blocks(block):
    behind, ahead = [block], [block]
    for _ in range(3):
        behind.append(shift(behind[-1], Z, 1))
        ahead.append(shift(ahead[-1], Z, -1))
    h = R // 2
    far = jnp.concatenate([shift(behind[-1][:h], Z, 1), shift(ahead[-1][h:], Z, -1)], 0)
    return jnp.stack(behind + [far] + ahead[:0:-1])


def plane_blocks(blocks, axes):
    near = [(shift(v, a, 1), shift(v, a, -1)) for v, a in zip(blocks, axes)]
    out = []
    for (behind, ahead), v, a in zip(near, blocks, axes):
        h = v.shape[0] // 2
        far = jnp.concatenate([shift(behind[:h], a, 1), shift(ahead[h:], a, -1)], 0)
        out.append((v, behind, far, ahead))
    return out


def on_device(context, residual, out_proj, norm_gain, cotangent, probe_seed):
    x, zh, y, zl, c = (lax.axis_index(a).astype(INT) for a in AXES)
    info = jnp.concatenate([jnp.stack([x, y, zh * 4 + zl, c]), probe_seed])

    probe = make_probe(info)
    own = ring_blocks(out_proj)
    other = lax.ppermute(own, "c", [(0, 1), (1, 0)])

    rows = lax.all_to_all(context, T, 0, 1, tiled=True)
    a, b = plane_blocks([rows[:HALF], rows[HALF:]], ["x", "y"])
    a, b = plane_blocks([jnp.stack(a), jnp.stack(b)], ["y", "x"])

    rc = jnp.stack([residual, cotangent]).reshape(2, OWN, 4, 2, 4, R)
    rc = rc.transpose(2, 4, 0, 1, 3, 5).reshape(16, 2, OWN, D)
    rc = lax.all_to_all(rc, XY, 0, 0, tiled=True)
    gain = norm_gain.reshape(4, 2, 4, R)
    gain = lax.dynamic_index_in_dim(lax.dynamic_index_in_dim(gain, x, 0, False), y, 1, False).reshape(D, 1)

    rows, s, u, w, stats = forward(info, [*a, *b], own, other, probe, rc, gain)
    stats = lax.all_to_all(jnp.broadcast_to(stats[None], (16, 8, TOK)), XY, 0, 0, tiled=True)
    send, keep = curvature_parts(info, stats, s, u, w, rows)
    total = (keep + lax.ppermute(send, "c", [(0, 1), (1, 0)]).astype(F32)).astype(BF16)
    total = lax.all_to_all(total.reshape(8, R, F), Z, 0, 0, tiled=True)
    curvature = jnp.sum(total.astype(F32), axis=0)
    signs = lax.dynamic_slice(probe, (zh * R, (zl * 2 + c) * F), (R, F))
    return signs.astype(F32) * curvature


def solution(mesh):
    split = Mesh(mesh.devices.reshape(GRID), AXES)
    dp, tensor = ("x", "zh", "y"), T
    in_specs = (
        P(dp, tensor),
        P((*dp, *tensor), None),
        P(dp, tensor),
        P(),
        P((*dp, *tensor), None),
        P(),
    )
    return jax.shard_map(on_device, mesh=split, in_specs=in_specs, out_specs=P(dp, tensor), check_vma=False)
```

time: 577 us -> 160 us (0.28)
  waiting for transfers between devices: 512 us -> 48.5 us
  starting transfers between devices: 0.18 us -> 53.7 us
  matrix products: 22.7 us -> 0 us
  Pallas kernels: 0 us -> 21 us
  between operations: 15.1 us -> 0.37 us
  blocking collectives: 0 us -> 13 us
  other arithmetic: 16.3 us -> 6.56 us
    reduce_scatter x3 -> x0, waiting for transfers between devices: 356 us -> none  [the longest x1 285 us: on_device(): lax.psum_scatter(lax.dot_general(full_tangent, context, (((0,), (0,)), ((...]
    all_gather x2 -> x0, waiting for transfers between devices: 156 us -> none  [the longest x1 113 us: on_device(): lax.all_gather(out_proj, 'dp', axis=0, tiled=True)]
    ppermute x0 -> x26, starting transfers between devices: none -> 32.8 us  [the longest x24 32.8 us: shift(): return lax.ppermute(v, axis, [(s, (s + k) % n) for s in range(n)])]
    all_to_all x0 -> x3, waiting for transfers between devices: none -> 30.4 us  [the longest x1 30.4 us: on_device(): total = lax.all_to_all(total.reshape(8, R, F), Z, 0, 0, tiled=True)]
    pallas_call x0 -> x3, Pallas kernels: none -> 21 us  [the longest x1 12.6 us: forward(): pl.pallas_call(forward_kernel, grid_spec=pltpu.PrefetchScalarGridSpec(num...]
    all_to_all x0 -> x3, starting transfers between devices: none -> 20.8 us  [the longest x1 7.37 us: on_device(): total = lax.all_to_all(total.reshape(8, R, F), Z, 0, 0, tiled=True)]
    ppermute x0 -> x26, waiting for transfers between devices: none -> 18.1 us  [the longest x24 15.3 us: shift(): return lax.ppermute(v, axis, [(s, (s + k) % n) for s in range(n)])]
    dot_general x2 -> x0, matrix products: 15.9 us -> none  [the longest x1 8.51 us: on_device(): jnp.dot(context, probe.T, preferred_element_type=jnp.float32)]
  transfers between devices with their start and end apart: 5 -> 29, of which waited for: 4 -> 9; matrix products, arithmetic and copies ran while one was open for 6% -> 10% of each run, Pallas kernels for 0% -> 2%
where the time goes in v1:
time: 160 us; the launch traced here: 157 us
  starting transfers between devices  53.7 us (34%)
  waiting for transfers between devices  48.5 us (30%)
  Pallas kernels  21 us (13%)
  local copies, waits for them, and re-layouts  13.5 us (8%)
  blocking collectives  13 us (8%)
  other arithmetic  6.56 us (4%)
    ppermute x24, starting transfers between devices, shift(): return lax.ppermute(v, axis, [(s, (s + k) % n) for s in range(n)])  32.8 us
    all_to_all x1, waiting for transfers between devices, on_device(): total = lax.all_to_all(total.reshape(8, R, F), Z, 0, 0, tiled=True)  30.4 us
    ppermute x24, waiting for transfers between devices, shift(): return lax.ppermute(v, axis, [(s, (s + k) % n) for s in range(n)])  15.3 us
    all_to_all x1, blocking collectives, on_device(): lax.all_to_all(jnp.broadcast_to(stats[None], (16, 8, TOK)), XY, 0, 0, til...  13 us
    pallas_call x1, Pallas kernels, forward(): pl.pallas_call(forward_kernel, grid_spec=pltpu.PrefetchScalarGridSpec(num...  12.6 us
    all_to_all x1, starting transfers between devices, on_device(): total = lax.all_to_all(total.reshape(8, R, F), Z, 0, 0, tiled=True)  7.37 us
    all_to_all x1, starting transfers between devices, on_device(): rows = lax.all_to_all(context, T, 0, 1, tiled=True)  7.24 us
    unnamed x18, local copies, waits for them, and re-layouts  6.39 us
  transfers between devices with their start and end apart: 29, of which 9 were waited for; matrix products, arithmetic and copies ran while one was open for 10% of the time, Pallas kernels for 2%

profile of v1, /device:TPU:32, one launch (start us, length us, event | category | flops | bytes accessed | tf_op | source)
XLA Modules:
  0.0 156.7 jit_solution(3715910955319427133)
XLA Ops:
  0.0 1.8 %collective-permute-start.20 = (bf16[192,384]{1,0:T(8,128)(2,1)}, bf16[192,384]{1,0:T(8,128)(2,1)S(1)}, u32[]{:S(2)}, u32[]{:S(2)}) collective-permute-start(bf16[192,384]{1,0:T(8,128)(2,1)} %param.8), channel_id=1, source_target_pairs={{0,38},{2,0},{4,2},{6,4},{32,6},{34,32},{36,34},{38,36},{1,39},{3,... | collective-permute-start | bytes 442376 | tf_op jit(solution)/shard_map/ppermute | solution.py:32
  2.0 7.2 %all-to-all-start = ((bf16[8,32,384]{2,1,0:T(8,128)(2,1)}), bf16[8,32,384]{2,1,0:T(8,128)(2,1)S(1)}, u32[]{:S(2)}, u32[]{:S(2)}) async-start(bf16[8,32,384]{2,1,0:T(8,128)(2,1)} %bitcast.46), calls=%async_computation | async-start | bytes 393216 | tf_op jit(solution)/shard_map/all_to_all | solution.py:236
  9.3 1.6 %bitcast_dynamic-update-slice_fusion.6 = bf16[8,192,384]{2,1,0:T(8,128)(2,1)} fusion(bf16[192,384]{1,0:T(8,128)(2,1)} %param.8), kind=kLoop, calls=%fused_computation.16 | loop fusion | bytes 294912
  11.0 1.9 %collective-permute-start.17 = (bf16[192,384]{1,0:T(8,128)(2,1)S(1)}, bf16[192,384]{1,0:T(8,128)(2,1)S(1)}, u32[]{:S(2)}, u32[]{:S(2)}) collective-permute-start(bf16[192,384]{1,0:T(8,128)(2,1)S(1)} %collective-permute-done.16), channel_id=1, source_target_pairs={{0,2},{2,4},{4,6},{6,32},{32,34},{34,36},{36,38},{38,0},{1,3},{3,5... | collective-permute-start | bytes 442376 | tf_op jit(solution)/shard_map/ppermute | solution.py:32
  13.6 5.8 %collective-permute-done.21 = bf16[192,384]{1,0:T(8,128)(2,1)S(1)} collective-permute-done((bf16[192,384]{1,0:T(8,128)(2,1)S(1)}, bf16[192,384]{1,0:T(8,128)(2,1)S(1)}, u32[]{:S(2)}, u32[]{:S(2)}) %collective-permute-start.21) | collective-permute-done | bytes 147488 | tf_op jit(solution)/shard_map/ppermute | solution.py:32
  19.8 1.6 %collective-permute-start.18 = (bf16[192,384]{1,0:T(8,128)(2,1)S(1)}, bf16[192,384]{1,0:T(8,128)(2,1)S(1)}, u32[]{:S(2)}, u32[]{:S(2)}) collective-permute-start(bf16[192,384]{1,0:T(8,128)(2,1)S(1)} %collective-permute-done.17), channel_id=1, source_target_pairs={{0,2},{2,4},{4,6},{6,32},{32,34},{34,36},{36,38},{38,0},{1,3},{3,5... | collective-permute-start | bytes 442376 | tf_op jit(solution)/shard_map/ppermute | solution.py:32
  21.4 2.8 %collective-permute-start.2 = (bf16[16,3072]{1,0:T(8,128)(2,1)S(1)}, bf16[16,3072]{1,0:T(8,128)(2,1)S(1)}, u32[]{:S(2)}, u32[]{:S(2)}) collective-permute-start(bf16[16,3072]{1,0:T(8,128)(2,1)S(1)} %bitcast.49), channel_id=1, source_target_pairs={{0,192},{64,0},{128,64},{192,128},{1,193},{65,1},{129,65},{193,129... | collective-permute-start | bytes 294920 | tf_op jit(solution)/shard_map/ppermute | solution.py:32
  25.1 3.1 %collective-permute-start.10 = (bf16[16,3072]{1,0:T(8,128)(2,1)S(1)}, bf16[16,3072]{1,0:T(8,128)(2,1)S(1)}, u32[]{:S(2)}, u32[]{:S(2)}) collective-permute-start(bf16[16,3072]{1,0:T(8,128)(2,1)S(1)} %bitcast.47), channel_id=1, source_target_pairs={{0,24},{8,0},{16,8},{24,16},{1,25},{9,1},{17,9},{25,17},{2,26},{10... | collective-permute-start | bytes 294920 | tf_op jit(solution)/shard_map/ppermute | solution.py:32
  28.2 1.7 %collective-permute-start.23 = (bf16[96,384]{1,0:T(8,128)(2,1)S(1)}, bf16[96,384]{1,0:T(8,128)(2,1)S(1)}, u32[]{:S(2)}, u32[]{:S(2)}) collective-permute-start(bf16[96,384]{1,0:T(8,128)(2,1)S(1)} %slice.67), channel_id=1, source_target_pairs={{0,38},{2,0},{4,2},{6,4},{32,6},{34,32},{36,34},{38,36},{1,39},{3,... | collective-permute-start | bytes 221192 | tf_op jit(solution)/shard_map/ppermute | solution.py:32
  30.1 3.2 %collective-permute-start.3 = (bf16[8,3072]{1,0:T(8,128)(2,1)S(1)}, bf16[8,3072]{1,0:T(8,128)(2,1)S(1)}, u32[]{:S(2)}, u32[]{:S(2)}) collective-permute-start(bf16[8,3072]{1,0:T(8,128)(2,1)S(1)} %slice.58), channel_id=1, source_target_pairs={{0,192},{64,0},{128,64},{192,128},{1,193},{65,1},{129,65},{193,129... | collective-permute-start | bytes 147464 | tf_op jit(solution)/shard_map/ppermute | solution.py:32
  34.5 3.3 %collective-permute-start.11 = (bf16[8,3072]{1,0:T(8,128)(2,1)S(1)}, bf16[8,3072]{1,0:T(8,128)(2,1)S(1)}, u32[]{:S(2)}, u32[]{:S(2)}) collective-permute-start(bf16[8,3072]{1,0:T(8,128)(2,1)S(1)} %slice.63), channel_id=1, source_target_pairs={{0,24},{8,0},{16,8},{24,16},{1,25},{9,1},{17,9},{25,17},{2,26},{10... | collective-permute-start | bytes 147464 | tf_op jit(solution)/shard_map/ppermute | solution.py:32
  38.8 3.3 %collective-permute-start.6 = (bf16[4,16,3072]{2,1,0:T(8,128)(2,1)S(1)}, bf16[4,16,3072]{2,1,0:T(8,128)(2,1)S(1)}, u32[]{:S(2)}, u32[]{:S(2)}) collective-permute-start(bf16[4,16,3072]{2,1,0:T(8,128)(2,1)S(1)} %pad_maximum_fusion.refs_0_), channel_id=1, source_target_pairs={{0,24},{8,0},{16,8},{24,16},{1,25},{9,1},{17,9},{25,17},{2,26},{10... | collective-permute-start | bytes 1179656 | tf_op jit(solution)/shard_map/ppermute | solution.py:32
  42.1 1.8 %collective-permute-done.9 = bf16[8,3072]{1,0:T(8,128)(2,1)S(1)} collective-permute-done((bf16[8,3072]{1,0:T(8,128)(2,1)S(1)}, bf16[8,3072]{1,0:T(8,128)(2,1)S(1)}, u32[]{:S(2)}, u32[]{:S(2)}) %collective-permute-start.9) | collective-permute-done | bytes 49184 | tf_op jit(solution)/shard_map/ppermute | solution.py:32
  46.7 3.4 %collective-permute-start.14 = (bf16[4,16,3072]{2,1,0:T(8,128)(2,1)S(1)}, bf16[4,16,3072]{2,1,0:T(8,128)(2,1)S(1)}, u32[]{:S(2)}, u32[]{:S(2)}) collective-permute-start(bf16[4,16,3072]{2,1,0:T(8,128)(2,1)S(1)} %pad_maximum_fusion.2.refs_4_), channel_id=1, source_target_pairs={{0,192},{64,0},{128,64},{192,128},{1,193},{65,1},{129,65},{193,129... | collective-permute-start | bytes 1179656 | tf_op jit(solution)/shard_map/ppermute | solution.py:32
  50.8 1.2 copy.18
  55.2 1.3 collective-permute-start.5
  56.5 1.5 maximum_bitcast_fusion
  58.0 1.4 reshape.28
  59.5 6.2 %all-to-all-start.1 = ((bf16[16,2,32,384]{3,2,1,0:T(8,128)(2,1)}), bf16[16,2,32,384]{3,2,1,0:T(8,128)(2,1)}, u32[]{:S(2)}, u32[]{:S(2)}) async-start(bf16[16,2,32,384]{3,2,1,0:T(8,128)(2,1)} %reshape.28), calls=%async_computation.1 | async-start | bytes 1572864 | tf_op jit(solution)/shard_map/all_to_all | solution.py:242
  66.1 3.2 %shard_map.64.refs_10_ = bf16[384,3072]{1,0:T(8,128)(2,1)S(1)} custom-call(s32[6]{0:T(128)S(1)} %concatenate.19.info), custom_call_target="tpu_custom_call" | custom-call | flops 16515072 | bytes 2359296 | tf_op jit(solution)/shard_map/pallas_call | solution.py:51
  69.4 1.4 copy-done
  70.8 3.1 %collective-permute-start.15 = (bf16[2,16,3072]{2,1,0:T(8,128)(2,1)S(1)}, bf16[2,16,3072]{2,1,0:T(8,128)(2,1)S(1)}, u32[]{:S(2)}, u32[]{:S(2)}) collective-permute-start(bf16[2,16,3072]{2,1,0:T(8,128)(2,1)S(1)} %slice.65), channel_id=1, source_target_pairs={{0,192},{64,0},{128,64},{192,128},{1,193},{65,1},{129,65},{193,129... | collective-permute-start | bytes 589832 | tf_op jit(solution)/shard_map/ppermute | solution.py:32
  75.4 4.8 %collective-permute-done.15 = bf16[2,16,3072]{2,1,0:T(8,128)(2,1)S(1)} collective-permute-done((bf16[2,16,3072]{2,1,0:T(8,128)(2,1)S(1)}, bf16[2,16,3072]{2,1,0:T(8,128)(2,1)S(1)}, u32[]{:S(2)}, u32[]{:S(2)}) %collective-permute-start.15) | collective-permute-done | bytes 196640 | tf_op jit(solution)/shard_map/ppermute | solution.py:32
  80.1 1.8 %collective-permute-done.13 = bf16[2,16,3072]{2,1,0:T(8,128)(2,1)S(1)} collective-permute-done((bf16[2,16,3072]{2,1,0:T(8,128)(2,1)S(1)}, bf16[2,16,3072]{2,1,0:T(8,128)(2,1)S(1)}, u32[]{:S(2)}, u32[]{:S(2)}) %collective-permute-start.13) | collective-permute-done | bytes 196640 | tf_op jit(solution)/shard_map/ppermute | solution.py:32
  82.0 12.6 %shard_map.65 = (bf16[512,3072]{1,0:T(8,128)(2,1)}, f32[384,512]{1,0:T(8,128)S(1)}, f32[384,512]{1,0:T(8,128)S(1)}, f32[384,512]{1,0:T(8,128)S(1)}, f32[8,512]{1,0:T(8,128)S(1)}) custom-call(s32[6]{0:T(128)S(1)} %concatenate.19.info, bf16[4,16,3072]{2,1,0:T(8,128)(2,1)S(1)} %pad_maximum_fusion.refs_0_, ...), custom_call_target="tpu_custom_call" | custom-call | flops 2415919104 | bytes 18874368 | tf_op jit(solution)/shard_map/pallas_call | solution.py:129
  94.6 13.0 %all_to_all.31.stats = f32[16,8,512]{2,1,0:T(8,128)S(1)} all-to-all(f32[16,8,512]{2,1,0:T(8,128)S(1)} %broadcast_in_dim.2), channel_id=1, replica_groups=mesh['x'=4,'zh'=2,'y'=4,'zl'=4,'c'=2] {'x','y'}, dimensions={0} | all-to-all | bytes 524288 | tf_op jit(solution)/shard_map/all_to_all | solution.py:247
  107.6 5.2 %shard_map.66 = (bf16[2,4,192,384]{3,2,1,0:T(8,128)(2,1)S(1)}, f32[2,4,192,384]{3,2,1,0:T(8,128)S(1)}) custom-call(s32[6]{0:T(128)S(1)} %concatenate.19.info, f32[16,8,512]{2,1,0:T(8,128)S(1)} %all_to_all.31.stats, f32[384,512]{1,0:T(8,128)S(1)} %get-tuple-element.13.s, f32[384,512]{1,0:T(8,128)S(1)} %get-tuple-element.14.u, ...), custom_call_target="tpu_custom_call" | custom-call | flops 1207959552 | bytes 12582912 | tf_op jit(solution)/shard_map/pallas_call | solution.py:188
  112.9 2.8 %collective-permute-done.25 = bf16[2,4,192,384]{3,2,1,0:T(8,128)(2,1)S(1)} collective-permute-done((bf16[2,4,192,384]{3,2,1,0:T(8,128)(2,1)S(1)}, bf16[2,4,192,384]{3,2,1,0:T(8,128)(2,1)S(1)}, u32[]{:S(2)}, u32[]{:S(2)}) %collective-permute-start.25) | collective-permute-done | bytes 1179680 | tf_op jit(solution)/shard_map/ppermute | solution.py:249
  115.8 1.3 add_convert_fusion
  117.1 7.4 %all-to-all-start.3 = ((bf16[8,192,384]{2,1,0:T(8,128)(2,1)}), bf16[8,192,384]{2,1,0:T(8,128)(2,1)S(1)}, u32[]{:S(2)}, u32[]{:S(2)}) async-start(bf16[8,192,384]{2,1,0:T(8,128)(2,1)} %bitcast.21), calls=%async_computation.3 | async-start | bytes 2359296 | tf_op jit(solution)/shard_map/all_to_all | solution.py:250
  124.5 30.4 %all-to-all-done.3 = bf16[8,192,384]{2,1,0:T(8,128)(2,1)S(1)} async-done(((bf16[8,192,384]{2,1,0:T(8,128)(2,1)}), bf16[8,192,384]{2,1,0:T(8,128)(2,1)S(1)}, u32[]{:S(2)}, u32[]{:S(2)}) %all-to-all-start.3) | async-done | bytes 1179680 | tf_op jit(solution)/shard_map/all_to_all | solution.py:250
  155.0 1.7 %convert_multiply_fusion = f32[192,384]{1,0:T(8,128)} fusion(f32[192,384]{1,0:T(8,128)S(1)} %convert_reduce_fusion, bf16[384,3072]{1,0:T(8,128)(2,1)} %copy-done, s32[]{:T(128)S(6)} %select_n.18, s32[]{:T(128)S(6)} %select_n.19), kind=kLoop, calls=%fused_computation.7 | loop fusion | flops 147456 | bytes 737288 | tf_op jit(solution)/shard_map/mul | solution.py:253
  (87 shorter events, 13.3 us)
Async XLA Ops:
  0.0 10.9 %collective-permute-start.20 = (bf16[192,384]{1,0:T(8,128)(2,1)}, bf16[192,384]{1,0:T(8,128)(2,1)S(1)}, u32[]{:S(2)}, u32[]{:S(2)}) collective-permute-start(bf16[192,384]{1,0:T(8,128)(2,1)} %param.8), channel_id=1, source_target_pairs={{0,38},{2,0},{4,2},{6,4},{32,6},{34,32},{36,34},{38,36},{1,39},{3,... | collective-permute-start | bytes 442376 | tf_op jit(solution)/shard_map/ppermute | solution.py:32
  1.8 9.1 %collective-permute-start.16 = (bf16[192,384]{1,0:T(8,128)(2,1)}, bf16[192,384]{1,0:T(8,128)(2,1)S(1)}, u32[]{:S(2)}, u32[]{:S(2)}) collective-permute-start(bf16[192,384]{1,0:T(8,128)(2,1)} %param.8), channel_id=1, source_target_pairs={{0,2},{2,4},{4,6},{6,32},{32,34},{34,36},{36,38},{38,0},{1,3},{3,5... | collective-permute-start | bytes 442376 | tf_op jit(solution)/shard_map/ppermute | solution.py:32
  2.0 19.3 %all-to-all-start = ((bf16[8,32,384]{2,1,0:T(8,128)(2,1)}), bf16[8,32,384]{2,1,0:T(8,128)(2,1)S(1)}, u32[]{:S(2)}, u32[]{:S(2)}) async-start(bf16[8,32,384]{2,1,0:T(8,128)(2,1)} %bitcast.46), calls=%async_computation | async-start | bytes 393216 | tf_op jit(solution)/shard_map/all_to_all | solution.py:236
  10.9 8.5 %collective-permute-start.21 = (bf16[192,384]{1,0:T(8,128)(2,1)S(1)}, bf16[192,384]{1,0:T(8,128)(2,1)S(1)}, u32[]{:S(2)}, u32[]{:S(2)}) collective-permute-start(bf16[192,384]{1,0:T(8,128)(2,1)S(1)} %collective-permute-done.20), channel_id=1, source_target_pairs={{0,38},{2,0},{4,2},{6,4},{32,6},{34,32},{36,34},{38,36},{1,39},{3,... | collective-permute-start | bytes 442376 | tf_op jit(solution)/shard_map/ppermute | solution.py:32
  11.0 8.8 %collective-permute-start.17 = (bf16[192,384]{1,0:T(8,128)(2,1)S(1)}, bf16[192,384]{1,0:T(8,128)(2,1)S(1)}, u32[]{:S(2)}, u32[]{:S(2)}) collective-permute-start(bf16[192,384]{1,0:T(8,128)(2,1)S(1)} %collective-permute-done.16), channel_id=1, source_target_pairs={{0,2},{2,4},{4,6},{6,32},{32,34},{34,36},{36,38},{38,0},{1,3},{3,5... | collective-permute-start | bytes 442376 | tf_op jit(solution)/shard_map/ppermute | solution.py:32
  19.3 8.9 %collective-permute-start.22 = (bf16[192,384]{1,0:T(8,128)(2,1)S(1)}, bf16[192,384]{1,0:T(8,128)(2,1)S(1)}, u32[]{:S(2)}, u32[]{:S(2)}) collective-permute-start(bf16[192,384]{1,0:T(8,128)(2,1)S(1)} %collective-permute-done.21), channel_id=1, source_target_pairs={{0,38},{2,0},{4,2},{6,4},{32,6},{34,32},{36,34},{38,36},{1,39},{3,... | collective-permute-start | bytes 442376 | tf_op jit(solution)/shard_map/ppermute | solution.py:32
  19.8 13.5 %collective-permute-start.18 = (bf16[192,384]{1,0:T(8,128)(2,1)S(1)}, bf16[192,384]{1,0:T(8,128)(2,1)S(1)}, u32[]{:S(2)}, u32[]{:S(2)}) collective-permute-start(bf16[192,384]{1,0:T(8,128)(2,1)S(1)} %collective-permute-done.17), channel_id=1, source_target_pairs={{0,2},{2,4},{4,6},{6,32},{32,34},{34,36},{36,38},{38,0},{1,3},{3,5... | collective-permute-start | bytes 442376 | tf_op jit(solution)/shard_map/ppermute | solution.py:32
  21.4 6.8 %collective-permute-start.2 = (bf16[16,3072]{1,0:T(8,128)(2,1)S(1)}, bf16[16,3072]{1,0:T(8,128)(2,1)S(1)}, u32[]{:S(2)}, u32[]{:S(2)}) collective-permute-start(bf16[16,3072]{1,0:T(8,128)(2,1)S(1)} %bitcast.49), channel_id=1, source_target_pairs={{0,192},{64,0},{128,64},{192,128},{1,193},{65,1},{129,65},{193,129... | collective-permute-start | bytes 294920 | tf_op jit(solution)/shard_map/ppermute | solution.py:32
  24.3 5.8 %collective-permute-start = (bf16[16,3072]{1,0:T(8,128)(2,1)S(1)}, bf16[16,3072]{1,0:T(8,128)(2,1)S(1)}, u32[]{:S(2)}, u32[]{:S(2)}) collective-permute-start(bf16[16,3072]{1,0:T(8,128)(2,1)S(1)} %bitcast.50), channel_id=1, source_target_pairs={{0,64},{64,128},{128,192},{192,0},{1,65},{65,129},{129,193},{193,1... | collective-permute-start | bytes 294920 | tf_op jit(solution)/shard_map/ppermute | solution.py:32
  25.1 9.0 %collective-permute-start.10 = (bf16[16,3072]{1,0:T(8,128)(2,1)S(1)}, bf16[16,3072]{1,0:T(8,128)(2,1)S(1)}, u32[]{:S(2)}, u32[]{:S(2)}) collective-permute-start(bf16[16,3072]{1,0:T(8,128)(2,1)S(1)} %bitcast.47), channel_id=1, source_target_pairs={{0,24},{8,0},{16,8},{24,16},{1,25},{9,1},{17,9},{25,17},{2,26},{10... | collective-permute-start | bytes 294920 | tf_op jit(solution)/shard_map/ppermute | solution.py:32
  28.2 6.3 %collective-permute-start.8 = (bf16[16,3072]{1,0:T(8,128)(2,1)S(1)}, bf16[16,3072]{1,0:T(8,128)(2,1)S(1)}, u32[]{:S(2)}, u32[]{:S(2)}) collective-permute-start(bf16[16,3072]{1,0:T(8,128)(2,1)S(1)} %bitcast.48), channel_id=1, source_target_pairs={{0,8},{8,16},{16,24},{24,0},{1,9},{9,17},{17,25},{25,1},{2,10},{10... | collective-permute-start | bytes 294920 | tf_op jit(solution)/shard_map/ppermute | solution.py:32
  28.2 15.7 %collective-permute-start.23 = (bf16[96,384]{1,0:T(8,128)(2,1)S(1)}, bf16[96,384]{1,0:T(8,128)(2,1)S(1)}, u32[]{:S(2)}, u32[]{:S(2)}) collective-permute-start(bf16[96,384]{1,0:T(8,128)(2,1)S(1)} %slice.67), channel_id=1, source_target_pairs={{0,38},{2,0},{4,2},{6,4},{32,6},{34,32},{36,34},{38,36},{1,39},{3,... | collective-permute-start | bytes 221192 | tf_op jit(solution)/shard_map/ppermute | solution.py:32
  30.1 7.8 %collective-permute-start.3 = (bf16[8,3072]{1,0:T(8,128)(2,1)S(1)}, bf16[8,3072]{1,0:T(8,128)(2,1)S(1)}, u32[]{:S(2)}, u32[]{:S(2)}) collective-permute-start(bf16[8,3072]{1,0:T(8,128)(2,1)S(1)} %slice.58), channel_id=1, source_target_pairs={{0,192},{64,0},{128,64},{192,128},{1,193},{65,1},{129,65},{193,129... | collective-permute-start | bytes 147464 | tf_op jit(solution)/shard_map/ppermute | solution.py:32
  33.3 5.4 %collective-permute-start.1 = (bf16[8,3072]{1,0:T(8,128)(2,1)S(1)}, bf16[8,3072]{1,0:T(8,128)(2,1)S(1)}, u32[]{:S(2)}, u32[]{:S(2)}) collective-permute-start(bf16[8,3072]{1,0:T(8,128)(2,1)S(1)} %slice.57), channel_id=1, source_target_pairs={{0,64},{64,128},{128,192},{192,0},{1,65},{65,129},{129,193},{193,1... | collective-permute-start | bytes 147464 | tf_op jit(solution)/shard_map/ppermute | solution.py:32
  34.1 9.9 %collective-permute-start.19 = (bf16[96,384]{1,0:T(8,128)(2,1)S(1)}, bf16[96,384]{1,0:T(8,128)(2,1)S(1)}, u32[]{:S(2)}, u32[]{:S(2)}) collective-permute-start(bf16[96,384]{1,0:T(8,128)(2,1)S(1)} %slice.66), channel_id=1, source_target_pairs={{0,2},{2,4},{4,6},{6,32},{32,34},{34,36},{36,38},{38,0},{1,3},{3,5... | collective-permute-start | bytes 221192 | tf_op jit(solution)/shard_map/ppermute | solution.py:32
  34.5 7.6 %collective-permute-start.11 = (bf16[8,3072]{1,0:T(8,128)(2,1)S(1)}, bf16[8,3072]{1,0:T(8,128)(2,1)S(1)}, u32[]{:S(2)}, u32[]{:S(2)}) collective-permute-start(bf16[8,3072]{1,0:T(8,128)(2,1)S(1)} %slice.63), channel_id=1, source_target_pairs={{0,24},{8,0},{16,8},{24,16},{1,25},{9,1},{17,9},{25,17},{2,26},{10... | collective-permute-start | bytes 147464 | tf_op jit(solution)/shard_map/ppermute | solution.py:32
  37.8 6.1 %collective-permute-start.9 = (bf16[8,3072]{1,0:T(8,128)(2,1)S(1)}, bf16[8,3072]{1,0:T(8,128)(2,1)S(1)}, u32[]{:S(2)}, u32[]{:S(2)}) collective-permute-start(bf16[8,3072]{1,0:T(8,128)(2,1)S(1)} %slice.62), channel_id=1, source_target_pairs={{0,8},{8,16},{16,24},{24,0},{1,9},{9,17},{17,25},{25,1},{2,10},{10... | collective-permute-start | bytes 147464 | tf_op jit(solution)/shard_map/ppermute | solution.py:32
  38.8 11.3 %copy-start.2 = (bf16[32,6144]{1,0:T(8,128)(2,1)S(1)}, bf16[32,6144]{1,0:T(8,128)(2,1)}, u32[]{:S(2)}) copy-start(bf16[32,6144]{1,0:T(8,128)(2,1)} %param.7) | copy-start | bytes 1179652
  38.8 14.3 %collective-permute-start.6 = (bf16[4,16,3072]{2,1,0:T(8,128)(2,1)S(1)}, bf16[4,16,3072]{2,1,0:T(8,128)(2,1)S(1)}, u32[]{:S(2)}, u32[]{:S(2)}) collective-permute-start(bf16[4,16,3072]{2,1,0:T(8,128)(2,1)S(1)} %pad_maximum_fusion.refs_0_), channel_id=1, source_target_pairs={{0,24},{8,0},{16,8},{24,16},{1,25},{9,1},{17,9},{25,17},{2,26},{10... | collective-permute-start | bytes 1179656 | tf_op jit(solution)/shard_map/ppermute | solution.py:32
  42.1 12.5 %collective-permute-start.4 = (bf16[4,16,3072]{2,1,0:T(8,128)(2,1)S(1)}, bf16[4,16,3072]{2,1,0:T(8,128)(2,1)S(1)}, u32[]{:S(2)}, u32[]{:S(2)}) collective-permute-start(bf16[4,16,3072]{2,1,0:T(8,128)(2,1)S(1)} %pad_maximum_fusion.refs_0_), channel_id=1, source_target_pairs={{0,8},{8,16},{16,24},{24,0},{1,9},{9,17},{17,25},{25,1},{2,10},{10... | collective-permute-start | bytes 1179656 | tf_op jit(solution)/shard_map/ppermute | solution.py:32
  46.7 35.3 %collective-permute-start.24 = (bf16[8,192,384]{2,1,0:T(8,128)(2,1)}, bf16[8,192,384]{2,1,0:T(8,128)(2,1)}, u32[]{:S(2)}, u32[]{:S(2)}) collective-permute-start(bf16[8,192,384]{2,1,0:T(8,128)(2,1)} %bitcast_dynamic-update-slice_fusion.refs_8_), channel_id=1, source_target_pairs={{0,1},{1,0},{2,3},{3,2},{4,5},{5,4},{6,7},{7,6},{8,9},{9,8},{10,11... | collective-permute-start | bytes 3538952 | tf_op jit(solution)/shard_map/ppermute | solution.py:234
  46.7 24.1 %collective-permute-start.14 = (bf16[4,16,3072]{2,1,0:T(8,128)(2,1)S(1)}, bf16[4,16,3072]{2,1,0:T(8,128)(2,1)S(1)}, u32[]{:S(2)}, u32[]{:S(2)}) collective-permute-start(bf16[4,16,3072]{2,1,0:T(8,128)(2,1)S(1)} %pad_maximum_fusion.2.refs_4_), channel_id=1, source_target_pairs={{0,192},{64,0},{128,64},{192,128},{1,193},{65,1},{129,65},{193,129... | collective-permute-start | bytes 1179656 | tf_op jit(solution)/shard_map/ppermute | solution.py:32
  50.1 23.9 %collective-permute-start.12 = (bf16[4,16,3072]{2,1,0:T(8,128)(2,1)S(1)}, bf16[4,16,3072]{2,1,0:T(8,128)(2,1)S(1)}, u32[]{:S(2)}, u32[]{:S(2)}) collective-permute-start(bf16[4,16,3072]{2,1,0:T(8,128)(2,1)S(1)} %pad_maximum_fusion.2.refs_4_), channel_id=1, source_target_pairs={{0,64},{64,128},{128,192},{192,0},{1,65},{65,129},{129,193},{193,1... | collective-permute-start | bytes 1179656 | tf_op jit(solution)/shard_map/ppermute | solution.py:32
  53.8 20.5 %collective-permute-start.7 = (bf16[2,16,3072]{2,1,0:T(8,128)(2,1)}, bf16[2,16,3072]{2,1,0:T(8,128)(2,1)}, u32[]{:S(2)}, u32[]{:S(2)}) collective-permute-start(bf16[2,16,3072]{2,1,0:T(8,128)(2,1)} %slice.60), channel_id=1, source_target_pairs={{0,24},{8,0},{16,8},{24,16},{1,25},{9,1},{17,9},{25,17},{2,26},{10... | collective-permute-start | bytes 589832 | tf_op jit(solution)/shard_map/ppermute | solution.py:32
  55.2 19.1 %collective-permute-start.5 = (bf16[2,16,3072]{2,1,0:T(8,128)(2,1)}, bf16[2,16,3072]{2,1,0:T(8,128)(2,1)}, u32[]{:S(2)}, u32[]{:S(2)}) collective-permute-start(bf16[2,16,3072]{2,1,0:T(8,128)(2,1)} %slice.59), channel_id=1, source_target_pairs={{0,8},{8,16},{16,24},{24,0},{1,9},{9,17},{17,25},{25,1},{2,10},{10... | collective-permute-start | bytes 589832 | tf_op jit(solution)/shard_map/ppermute | solution.py:32
  59.5 6.2 %copy-start.4 = (f32[6144]{0:T(1024)S(1)}, f32[6144]{0:T(1024)}, u32[]{:S(2)}) copy-start(f32[6144]{0:T(1024)} %param.9) | copy-start | bytes 73732
  59.5 6.6 %copy-start.5 = (s32[2]{0:T(128)S(1)}, s32[2]{0:T(128)}, u32[]{:S(2)}) copy-start(s32[2]{0:T(128)} %param.11) | copy-start | bytes 28
  59.5 22.5 %all-to-all-start.1 = ((bf16[16,2,32,384]{3,2,1,0:T(8,128)(2,1)}), bf16[16,2,32,384]{3,2,1,0:T(8,128)(2,1)}, u32[]{:S(2)}, u32[]{:S(2)}) async-start(bf16[16,2,32,384]{3,2,1,0:T(8,128)(2,1)} %reshape.28), calls=%async_computation.1 | async-start | bytes 1572864 | tf_op jit(solution)/shard_map/all_to_all | solution.py:242
  70.8 9.3 %collective-permute-start.15 = (bf16[2,16,3072]{2,1,0:T(8,128)(2,1)S(1)}, bf16[2,16,3072]{2,1,0:T(8,128)(2,1)S(1)}, u32[]{:S(2)}, u32[]{:S(2)}) collective-permute-start(bf16[2,16,3072]{2,1,0:T(8,128)(2,1)S(1)} %slice.65), channel_id=1, source_target_pairs={{0,192},{64,0},{128,64},{192,128},{1,193},{65,1},{129,65},{193,129... | collective-permute-start | bytes 589832 | tf_op jit(solution)/shard_map/ppermute | solution.py:32
  74.0 7.9 %collective-permute-start.13 = (bf16[2,16,3072]{2,1,0:T(8,128)(2,1)S(1)}, bf16[2,16,3072]{2,1,0:T(8,128)(2,1)S(1)}, u32[]{:S(2)}, u32[]{:S(2)}) collective-permute-start(bf16[2,16,3072]{2,1,0:T(8,128)(2,1)S(1)} %slice.64), channel_id=1, source_target_pairs={{0,64},{64,128},{128,192},{192,0},{1,65},{65,129},{129,193},{193,1... | collective-permute-start | bytes 589832 | tf_op jit(solution)/shard_map/ppermute | solution.py:32
  112.8 2.9 %collective-permute-start.25 = (bf16[2,4,192,384]{3,2,1,0:T(8,128)(2,1)S(1)}, bf16[2,4,192,384]{3,2,1,0:T(8,128)(2,1)S(1)}, u32[]{:S(2)}, u32[]{:S(2)}) collective-permute-start(bf16[2,4,192,384]{3,2,1,0:T(8,128)(2,1)S(1)} %get-tuple-element.18), channel_id=1, source_target_pairs={{0,1},{1,0},{2,3},{3,2},{4,5},{5,4},{6,7},{7,6},{8,9},{9,8},{10,11... | collective-permute-start | bytes 3538952 | tf_op jit(solution)/shard_map/ppermute | solution.py:249
  117.1 37.8 %all-to-all-start.3 = ((bf16[8,192,384]{2,1,0:T(8,128)(2,1)}), bf16[8,192,384]{2,1,0:T(8,128)(2,1)S(1)}, u32[]{:S(2)}, u32[]{:S(2)}) async-start(bf16[8,192,384]{2,1,0:T(8,128)(2,1)} %bitcast.21), calls=%async_computation.3 | async-start | bytes 2359296 | tf_op jit(solution)/shard_map/all_to_all | solution.py:250
  (3 other events, 6.5 us)

commit v2 on v0

v2 whole, which is shorter than its diff:
```python
import jax
import jax.numpy as jnp
from jax import lax
from jax.experimental import pallas as pl
from jax.experimental.pallas import tpu as pltpu
from jax.sharding import Mesh
from jax.sharding import PartitionSpec as P

AXES = ("x", "zh", "y", "zl", "c")
GRID = (4, 2, 4, 4, 2)
Z = ("zh", "zl")
XY = ("x", "y")
T = ("zl", "c")
R = 192
F = 384
W = 8 * F
OWN = 32
TOK = 16 * OWN
D = 2 * R
N = 32 * R
E = W + 2 * D
XYC = ("x", "y", "c")
MIB = 1024 * 1024
MULT = 747796405
INT = jnp.int32
F32 = jnp.float32
BF16 = jnp.bfloat16
NT = (((1,), (1,)), ((), ()))


def shift(v, axis, k):
    n = 8 if axis == Z else 4
    return lax.ppermute(v, axis, [(s, (s + k) % n) for s in range(n)])


def probe_kernel(info, out):
    x, y, seed0, seed1 = info[0], info[1], info[4], info[5]
    cols = lax.broadcasted_iota(INT, (1, F), 1) + pl.program_id(0) * F
    rows = lax.broadcasted_iota(INT, (R, 1), 0)
    for zh in range(2):
        d = rows + (x * 8 + zh * 4 + y) * R
        m = (d * W * INT(MULT) + seed0) + cols * INT(MULT)
        m = m ^ lax.shift_right_logical(m, INT(16))
        m = m * INT(73244475)
        m = m ^ seed1
        m = m ^ lax.shift_right_logical(m, INT(15))
        parity = lax.shift_right_logical(m, INT(9)) & INT(1)
        out[zh * R : (zh + 1) * R, :] = (1 - 2 * parity).astype(F32).astype(BF16)


def make_probe(info):
    return pl.pallas_call(
        probe_kernel,
        grid=(8,),
        in_specs=[pl.BlockSpec(memory_space=pltpu.SMEM)],
        out_specs=pl.BlockSpec((D, F), lambda j: (0, j)),
        out_shape=jax.ShapeDtypeStruct((D, W), BF16),
        compiler_params=pltpu.CompilerParams(vmem_limit_bytes=16 * MIB),
        cost_estimate=pl.CostEstimate(flops=14 * D * W, bytes_accessed=2 * D * W, transcendentals=0),
    )(info)


def regroup_kernel(info, residual, cotangent, gains, out, gain):
    x, y, c = info[0], info[1], info[3]
    eye = lax.broadcasted_iota(INT, (R, R), 0) == lax.broadcasted_iota(INT, (R, R), 1)
    for zh in range(2):
        row = gains[pl.ds(x * 8 + zh * 4 + y, 1), :]
        gain[zh * R : (zh + 1) * R, :] = jnp.sum(jnp.where(eye, row, 0.0), axis=1, keepdims=True)

    @pl.when(c == 0)
    def _():
        for n, v in enumerate((residual, cotangent)):
            for k in range(4):
                part = v[:, pl.ds(pl.multiple_of((x + k) % 4 * (8 * R), 8 * R), 8 * R)]
                for at in range(4):
                    for zh in range(2):
                        first = at * 2 * D + n * D + zh * R
                        out[k, :, first : first + R] = part[:, (zh * 4 + at) * R : (zh * 4 + at + 1) * R]

    @pl.when(c == 1)
    def _():
        for n, v in enumerate((residual, cotangent)):
            for at in range(4):
                part = v[:, at * 8 * R : (at + 1) * 8 * R]
                for to in range(4):
                    k = (to - y + 4) % 4
                    for zh in range(2):
                        first = at * 2 * D + n * D + zh * R
                        out[k, :, first : first + R] = part[:, (zh * 4 + to) * R : (zh * 4 + to + 1) * R]


def regroup(info, residual, cotangent, norm_gain):
    return pl.pallas_call(
        regroup_kernel,
        in_specs=[pl.BlockSpec(memory_space=pltpu.SMEM)] + [pl.BlockSpec(memory_space=pltpu.VMEM)] * 3,
        out_shape=[jax.ShapeDtypeStruct((4, OWN, 8 * D), BF16), jax.ShapeDtypeStruct((D, 1), F32)],
        compiler_params=pltpu.CompilerParams(vmem_limit_bytes=16 * MIB),
        cost_estimate=pl.CostEstimate(flops=0, bytes_accessed=8 * OWN * N, transcendentals=0),
    )(info, residual, cotangent, norm_gain.reshape(32, R))


def first_kernel(rows, rest, *out):
    for k in range(4):
        for t in range(8):
            out[k][:OWN, t * F : (t + 1) * F] = rows[t]
        out[k][OWN:] = rest[k]


def first_leg(rows, rest):
    return pl.pallas_call(
        first_kernel,
        out_shape=[jax.ShapeDtypeStruct((2 * OWN, W), BF16)] * 4,
        compiler_params=pltpu.CompilerParams(vmem_limit_bytes=16 * MIB),
        cost_estimate=pl.CostEstimate(flops=0, bytes_accessed=32 * OWN * W, transcendentals=0),
    )(rows, rest)


def second_kernel(info, *refs):
    came, out = refs[:4], refs[4:]
    place = jnp.where(info[3] == 0, info[1], info[0])
    for j in range(4):
        columns = pl.ds(pl.multiple_of((place + j) % 4 * 2 * D, 2 * D), 2 * D)
        for k in range(4):
            out[j][k, :, :W] = came[k][:OWN]
            out[j][k, :, W:] = came[k][OWN:, columns]


def second_leg(info, came):
    return pl.pallas_call(
        second_kernel,
        in_specs=[pl.BlockSpec(memory_space=pltpu.SMEM)] + [pl.BlockSpec(memory_space=pltpu.VMEM)] * 4,
        out_shape=[jax.ShapeDtypeStruct((4, OWN, E), BF16)] * 4,
        compiler_params=pltpu.CompilerParams(vmem_limit_bytes=16 * MIB),
        cost_estimate=pl.CostEstimate(flops=0, bytes_accessed=64 * OWN * E, transcendentals=0),
    )(info, *came)


def tangent_kernel(info, *refs):
    pieces, (probe, gain), (context, residual, u_out, w_out), cotangent = refs[:4], refs[4:6], refs[6:10], refs[10]
    x, y, c = info[0], info[1], info[3]
    for j in range(4):
        for k in range(4):
            ax = (x - jnp.where(c == 0, k, j) + 4) % 4
            ay = (y - jnp.where(c == 0, j, k) + 4) % 4
            row = pl.ds(pl.multiple_of((ax * 4 + ay) * OWN, OWN), OWN)
            context[row, :] = pieces[j][k, :, :W]
            residual[row, :] = pieces[j][k, :, W : W + D]
            cotangent[row, :] = pieces[j][k, :, W + D :]
    u_out[...] = lax.dot_general(probe[...], context[...], NT, preferred_element_type=F32)
    w_out[...] = turned(cotangent[...]) * gain[...]


def turned(v):
    eye = (lax.broadcasted_iota(INT, (D, D), 0) == lax.broadcasted_iota(INT, (D, D), 1)).astype(F32).astype(BF16)
    return lax.dot_general(eye, v, NT, preferred_element_type=F32)


def tangent_of(info, pieces, probe, gain):
    return pl.pallas_call(
        tangent_kernel,
        in_specs=[pl.BlockSpec(memory_space=pltpu.SMEM)] + [pl.BlockSpec(memory_space=pltpu.VMEM)] * 6,
        out_shape=[jax.ShapeDtypeStruct((TOK, W), BF16), jax.ShapeDtypeStruct((TOK, D), BF16)]
        + [jax.ShapeDtypeStruct((D, TOK), F32)] * 2,
        scratch_shapes=[pltpu.VMEM((TOK, D), BF16)],
        compiler_params=pltpu.CompilerParams(vmem_limit_bytes=16 * MIB),
        cost_estimate=pl.CostEstimate(flops=2 * D * TOK * W, bytes_accessed=8 * TOK * W, transcendentals=0),
    )(info, *pieces, probe, gain)


def stream_kernel(info, own, other, context, residual, u_in, w_in, s_out, stats, weight):
    zr, c = info[2], info[3]
    for zh in range(2):
        for zl in range(4):
            at = (zr - (zh * 4 + zl) + 8) % 8
            rows = slice(zh * R, (zh + 1) * R)
            weight[rows, pl.ds(pl.multiple_of((zl * 2 + c) * F, F), F)] = own[at]
            weight[rows, pl.ds(pl.multiple_of((zl * 2 + 1 - c) * F, F), F)] = other[at]
    s = turned(residual[...]) + lax.dot_general(weight[...], context[...], NT, preferred_element_type=F32)
    s_out[...] = s
    u, w = u_in[...], w_in[...]
    mean = lambda v: jnp.sum(v, axis=0, keepdims=True) * (1.0 / D)
    ms, mu, mw = mean(s), mean(u), mean(w)
    sc, uc, wc = s - ms, u - mu, w - mw
    stats[0:1] = ms
    stats[1:2] = mu
    stats[2:3] = mw
    stats[3:4] = mean(sc * sc)
    stats[4:5] = mean(sc * uc)
    stats[5:6] = mean(sc * wc)
    stats[6:7] = mean(uc * wc)
    stats[7:8] = jnp.zeros_like(ms)


def stream_of(info, own, other, context, residual, u, w):
    return pl.pallas_call(
        stream_kernel,
        in_specs=[pl.BlockSpec(memory_space=pltpu.SMEM)] + [pl.BlockSpec(memory_space=pltpu.VMEM)] * 6,
        out_shape=[jax.ShapeDtypeStruct((D, TOK), F32), jax.ShapeDtypeStruct((8, TOK), F32)],
        scratch_shapes=[pltpu.VMEM((D, W), BF16)],
        compiler_params=pltpu.CompilerParams(vmem_limit_bytes=16 * MIB),
        cost_estimate=pl.CostEstimate(flops=2 * D * TOK * W, bytes_accessed=8 * TOK * W, transcendentals=0),
    )(info, own, other, context, residual, u, w)


def gradient(stats, s, u, w):
    parts = [stats[j] for j in range(16)]
    total = parts[0]
    for part in parts[1:]:
        total = total + part
    mean = total * (1.0 / 16)
    ms, mu, mw = mean[0:1], mean[1:2], mean[2:3]
    css, csu, csw, cuw = mean[3:4], mean[4:5], mean[5:6], mean[6:7]
    for part in parts:
        ds, du, dw = part[0:1] - ms, part[1:2] - mu, part[2:3] - mw
        css = css + ds * ds * (1.0 / 16)
        csu = csu + ds * du * (1.0 / 16)
        csw = csw + ds * dw * (1.0 / 16)
        cuw = cuw + du * dw * (1.0 / 16)
    r2 = 1.0 / (css + 1e-05)
    r = lax.rsqrt(css + 1e-05)
    k = -(r * r2)
    gamma = cuw - 3.0 * r2 * csu * csw
    value = k * (csu * (w[...] - mw) + csw * (u[...] - mu) + gamma * (s[...] - ms))
    return value.astype(BF16)


def owner(info, k):
    chip = (info[2] + k) % 8
    return pl.ds(pl.multiple_of(chip // 4 * R, R), R), chip % 4 * 2


def away_kernel(info, stats, s, u, w, context, grad, send):
    grad[...] = gradient(stats, s, u, w)
    for k in range(8):
        rows, feature = owner(info, k)
        columns = context[:, pl.ds(pl.multiple_of((feature + 1 - info[3]) * F, F), F)]
        send[k] = jnp.dot(grad[rows, :], columns, preferred_element_type=F32).astype(BF16)


def away(info, stats, s, u, w, context):
    return pl.pallas_call(
        away_kernel,
        in_specs=[pl.BlockSpec(memory_space=pltpu.SMEM)] + [pl.BlockSpec(memory_space=pltpu.VMEM)] * 5,
        out_shape=[jax.ShapeDtypeStruct((D, TOK), BF16), jax.ShapeDtypeStruct((8, R, F), BF16)],
        compiler_params=pltpu.CompilerParams(vmem_limit_bytes=16 * MIB),
        cost_estimate=pl.CostEstimate(flops=D * TOK * W, bytes_accessed=8 * TOK * W, transcendentals=0),
    )(info, stats, s, u, w, context)


def home_kernel(info, grad, context, received, near_up, near_down, three_up, three_down, four_up, four_down, kept):
    def part(k):
        rows, feature = owner(info, k)
        columns = context[:, pl.ds(pl.multiple_of((feature + info[3]) * F, F), F)]
        return jnp.dot(grad[rows, :], columns, preferred_element_type=F32) + received[k].astype(F32)

    three_up[...] = part(3).astype(BF16)
    three_down[...] = part(5).astype(BF16)
    four = part(4).astype(BF16)
    four_up[...] = four[: R // 2]
    four_down[...] = four[R // 2 :]
    near_up[...] = part(1).astype(BF16)
    near_down[...] = part(7).astype(BF16)
    for n, k in enumerate((0, 2, 6)):
        kept[n] = part(k)


def home(info, grad, context, received):
    return pl.pallas_call(
        home_kernel,
        in_specs=[pl.BlockSpec(memory_space=pltpu.SMEM)] + [pl.BlockSpec(memory_space=pltpu.VMEM)] * 3,
        out_shape=[jax.ShapeDtypeStruct((R, F), BF16)] * 4
        + [jax.ShapeDtypeStruct((R // 2, F), BF16)] * 2
        + [jax.ShapeDtypeStruct((3, R, F), F32)],
        compiler_params=pltpu.CompilerParams(vmem_limit_bytes=16 * MIB),
        cost_estimate=pl.CostEstimate(flops=D * TOK * W, bytes_accessed=8 * TOK * W, transcendentals=0),
    )(info, grad, context, received)


def swap(v):
    return lax.ppermute(v, "c", [(0, 1), (1, 0)])


def after(v, *others):
    return lax.optimization_barrier((v, *others))[0]


def leg(blocks, axes):
    out = [blocks[0]]
    for k in range(1, 4):
        pairs = []
        for x in range(4):
            for y in range(4):
                for c in range(2):
                    to = ((x + k) % 4, y) if axes[c] == "x" else (x, (y + k) % 4)
                    pairs.append(((x * 4 + y) * 2 + c, (to[0] * 4 + to[1]) * 2 + c))
        out.append(lax.ppermute(blocks[k], XYC, pairs))
    return out


def on_device(context, residual, out_proj, norm_gain, cotangent, probe_seed):
    x, zh, y, zl, c = (lax.axis_index(a).astype(INT) for a in AXES)
    info = jnp.concatenate([jnp.stack([x, y, zh * 4 + zl, c]), probe_seed])

    rest, gain = regroup(info, residual, cotangent, norm_gain)
    rows = lax.all_to_all(context.reshape(8, OWN, F), T, 0, 0, tiled=True)
    rows, rest, gain = lax.optimization_barrier((rows, rest, gain))

    came = lax.optimization_barrier(leg(first_leg(rows, rest), "xy"))
    behind, ahead = shift(out_proj, Z, 1), shift(out_proj, Z, -1)
    two, ahead2 = after(jnp.stack([out_proj, behind]), rows), after(jnp.stack([out_proj, ahead]), rows)
    behind2, ahead2 = shift(two, Z, 2), shift(ahead2, Z, -2)
    far = shift(after(ahead2[1], *came), Z, -1)
    own = jnp.concatenate([two, behind2, far[None], ahead2[::-1], ahead[None]])

    probe = make_probe(after(info, *came))
    *pieces, probe, own = lax.optimization_barrier((*leg(second_leg(info, came), "yx"), probe, own))
    other = swap(own)
    rows, res, u, w = tangent_of(info, pieces, probe, gain)
    s, stats = stream_of(info, own, other, rows, res, u, w)
    stats = lax.all_to_all(jnp.broadcast_to(stats[None], (16, 8, TOK)), XY, 0, 0, tiled=True)
    grad, send = away(info, stats, s, u, w, rows)
    near_up, near_down, three_up, three_down, four_up, four_down, kept = home(info, grad, rows, swap(send))

    near_up, near_down, three_up, three_down, four_up, four_down = lax.optimization_barrier(
        (
            shift(near_up, Z, 1),
            shift(near_down, Z, -1),
            shift(three_up, Z, 1),
            shift(three_down, Z, -1),
            shift(four_up, Z, 2),
            shift(four_down, Z, -2),
        )
    )
    none = jnp.zeros((R // 2, F), F32)
    up = kept[1] + three_up.astype(F32) + jnp.concatenate([four_up.astype(F32), none])
    down = kept[2] + three_down.astype(F32) + jnp.concatenate([none, four_down.astype(F32)])
    up, down = shift(up.astype(BF16), Z, 2), shift(down.astype(BF16), Z, -2)
    total = kept[0] + near_up.astype(F32) + near_down.astype(F32) + up.astype(F32) + down.astype(F32)
    signs = lax.dynamic_slice(probe, (zh * R, (zl * 2 + c) * F), (R, F))
    return signs.astype(F32) * total


def solution(mesh):
    split = Mesh(mesh.devices.reshape(GRID), AXES)
    dp, tensor = ("x", "zh", "y"), T
    in_specs = (
        P(dp, tensor),
        P((*dp, *tensor), None),
        P(dp, tensor),
        P(),
        P((*dp, *tensor), None),
        P(),
    )
    return jax.shard_map(on_device, mesh=split, in_specs=in_specs, out_specs=P(dp, tensor), check_vma=False)
```

time: 577 us -> 115 us (0.20)
  waiting for transfers between devices: 512 us -> 37.9 us
  starting transfers between devices: 0.18 us -> 40.6 us
  matrix products: 22.7 us -> 0 us
  blocking collectives: 0 us -> 15.2 us
  between operations: 15.1 us -> 0.14 us
  Pallas kernels: 0 us -> 14.6 us
  other arithmetic: 16.3 us -> 2.66 us
    reduce_scatter x3 -> x0, waiting for transfers between devices: 356 us -> none  [the longest x1 285 us: on_device(): lax.psum_scatter(lax.dot_general(full_tangent, context, (((0,), (0,)), ((...]
    all_gather x2 -> x0, waiting for transfers between devices: 156 us -> none  [the longest x1 113 us: on_device(): lax.all_gather(out_proj, 'dp', axis=0, tiled=True)]
    ppermute x0 -> x21, waiting for transfers between devices: none -> 37.5 us  [the longest x13 18.7 us: shift(): return lax.ppermute(v, axis, [(s, (s + k) % n) for s in range(n)])]
    ppermute x0 -> x21, starting transfers between devices: none -> 34.5 us  [the longest x13 22.8 us: shift(): return lax.ppermute(v, axis, [(s, (s + k) % n) for s in range(n)])]
    dot_general x2 -> x0, matrix products: 15.9 us -> none  [the longest x1 8.51 us: on_device(): jnp.dot(context, probe.T, preferred_element_type=jnp.float32)]
    all_to_all x0 -> x1, blocking collectives: none -> 15.2 us  [on_device(): lax.all_to_all(jnp.broadcast_to(stats[None], (16, 8, TOK)), XY, 0, 0, til...]
    pallas_call x0 -> x8, Pallas kernels: none -> 14.6 us  [the longest x1 3.22 us: make_probe(): pl.pallas_call(probe_kernel, grid=(8,), in_specs=[pl.BlockSpec(memory_spa...]
    convert_element_type x2 -> x1, other arithmetic: 8.09 us -> 0.78 us  [on_device(): up, down = (shift(up.astype(BF16), Z, 2), shift(down.astype(BF16), Z, -2))]
  transfers between devices with their start and end apart: 5 -> 22, of which waited for: 4 -> 13; matrix products, arithmetic and copies ran while one was open for 6% -> 2% of each run, Pallas kernels for 0% -> 7%
where the time goes in v2:
time: 115 us
  starting transfers between devices  40.6 us (35%)
  waiting for transfers between devices  37.9 us (33%)
  blocking collectives  15.2 us (13%)
  Pallas kernels  14.6 us (13%)
  local copies, waits for them, and re-layouts  3.76 us (3%)
  other arithmetic  2.66 us (2%)
    ppermute x13, starting transfers between devices, shift(): return lax.ppermute(v, axis, [(s, (s + k) % n) for s in range(n)])  22.8 us
    ppermute x13, waiting for transfers between devices, shift(): return lax.ppermute(v, axis, [(s, (s + k) % n) for s in range(n)])  18.7 us
    ppermute x6, waiting for transfers between devices, leg(): out.append(lax.ppermute(blocks[k], XYC, pairs))  15.6 us
    all_to_all x1, blocking collectives, on_device(): lax.all_to_all(jnp.broadcast_to(stats[None], (16, 8, TOK)), XY, 0, 0, til...  15.2 us
    ppermute x6, starting transfers between devices, leg(): out.append(lax.ppermute(blocks[k], XYC, pairs))  11.6 us
    all_to_all x1, starting transfers between devices, on_device(): rows = lax.all_to_all(context.reshape(8, OWN, F), T, 0, 0, tiled=True)  6.14 us
    pallas_call x1, Pallas kernels, make_probe(): pl.pallas_call(probe_kernel, grid=(8,), in_specs=[pl.BlockSpec(memory_spa...  3.22 us
    ppermute x2, waiting for transfers between devices, swap(): return lax.ppermute(v, 'c', [(0, 1), (1, 0)])  3.19 us
  transfers between devices with their start and end apart: 22, of which 13 were waited for; matrix products, arithmetic and copies ran while one was open for 2% of the time, Pallas kernels for 7%

profile of v2, /device:TPU:32, one launch (start us, length us, event | category | flops | bytes accessed | tf_op | source)
XLA Modules:
  0.0 114.9 jit_solution(15786073210592825529)
XLA Ops:
  0.0 6.1 %all-to-all-start = ((bf16[8,32,384]{2,1,0:T(8,128)(2,1)}), bf16[8,32,384]{2,1,0:T(8,128)(2,1)S(1)}, u32[]{:S(2)}, u32[]{:S(2)}) async-start(bf16[8,32,384]{2,1,0:T(8,128)(2,1)} %bitcast.36), calls=%async_computation | async-start | bytes 393216 | tf_op jit(solution)/shard_map/all_to_all | solution.py:305
  6.2 2.0 %collective-permute-start.6 = (bf16[192,384]{1,0:T(8,128)(2,1)}, bf16[192,384]{1,0:T(8,128)(2,1)S(1)}, u32[]{:S(2)}, u32[]{:S(2)}) collective-permute-start(bf16[192,384]{1,0:T(8,128)(2,1)} %param.8), channel_id=1, source_target_pairs={{0,2},{2,4},{4,6},{6,32},{32,34},{34,36},{36,38},{38,0},{1,3},{3,5... | collective-permute-start | bytes 442376 | tf_op jit(solution)/shard_map/ppermute | solution.py:33
  9.7 1.0 copy-done
  11.7 1.2 %shard_map.64 = (bf16[4,32,3072]{2,1,0:T(8,128)(2,1)S(1)}, f32[384,1]{1,0:T(8,128)S(1)}) custom-call(s32[6]{0:T(128)S(1)} %concatenate.16.info, bf16[32,6144]{1,0:T(8,128)(2,1)S(1)} %copy-done, bf16[32,6144]{1,0:T(8,128)(2,1)S(1)} %copy-done.1, f32[32,192]{1,0:T(8,128)S(1)} %reshape.8.gains), custom_call_target="tpu_custom_call" | custom-call | bytes 1572864 | tf_op jit(solution)/shard_map/pallas_call | solution.py:93
  13.5 1.6 %collective-permute-start = (bf16[64,3072]{1,0:T(8,128)(2,1)S(1)}, bf16[64,3072]{1,0:T(8,128)(2,1)S(1)}, u32[]{:S(2)}, u32[]{:S(2)}) collective-permute-start(bf16[64,3072]{1,0:T(8,128)(2,1)S(1)} %get-tuple-element.58), channel_id=1, source_target_pairs={{0,64},{1,9},{8,72},{9,17},{16,80},{17,25},{24,88},{25,1},{64,128}... | collective-permute-start | bytes 1179656 | tf_op jit(solution)/shard_map/ppermute | solution.py:296
  15.0 2.7 %collective-permute-start.1 = (bf16[64,3072]{1,0:T(8,128)(2,1)S(1)}, bf16[64,3072]{1,0:T(8,128)(2,1)S(1)}, u32[]{:S(2)}, u32[]{:S(2)}) collective-permute-start(bf16[64,3072]{1,0:T(8,128)(2,1)S(1)} %get-tuple-element.59), channel_id=1, source_target_pairs={{0,128},{1,17},{8,136},{9,25},{16,144},{17,1},{24,152},{25,9},{64,... | collective-permute-start | bytes 1179656 | tf_op jit(solution)/shard_map/ppermute | solution.py:296
  17.8 1.4 %collective-permute-start.2 = (bf16[64,3072]{1,0:T(8,128)(2,1)S(1)}, bf16[64,3072]{1,0:T(8,128)(2,1)S(1)}, u32[]{:S(2)}, u32[]{:S(2)}) collective-permute-start(bf16[64,3072]{1,0:T(8,128)(2,1)S(1)} %get-tuple-element.60), channel_id=1, source_target_pairs={{0,192},{1,25},{8,200},{9,1},{16,208},{17,9},{24,216},{25,17},{64,... | collective-permute-start | bytes 1179656 | tf_op jit(solution)/shard_map/ppermute | solution.py:296
  19.3 5.5 %collective-permute-start.9 = (bf16[2,192,384]{2,1,0:T(8,128)(2,1)S(1)}, bf16[2,192,384]{2,1,0:T(8,128)(2,1)S(1)}, u32[]{:S(2)}, u32[]{:S(2)}) collective-permute-start(bf16[2,192,384]{2,1,0:T(8,128)(2,1)S(1)} %get-tuple-element.71), channel_id=1, source_target_pairs={{0,36},{2,38},{4,0},{6,2},{32,4},{34,6},{36,32},{38,34},{1,37},{3,... | collective-permute-start | bytes 884744 | tf_op jit(solution)/shard_map/ppermute | solution.py:33
  24.8 2.9 %collective-permute-done.1.refs_2_ = bf16[64,3072]{1,0:T(8,128)(2,1)S(1)} collective-permute-done((bf16[64,3072]{1,0:T(8,128)(2,1)S(1)}, bf16[64,3072]{1,0:T(8,128)(2,1)S(1)}, u32[]{:S(2)}, u32[]{:S(2)}) %collective-permute-start.1) | collective-permute-done | bytes 393248 | tf_op jit(solution)/shard_map/ppermute | solution.py:296
  28.5 1.7 %collective-permute-start.3 = (bf16[4,32,3840]{2,1,0:T(8,128)(2,1)S(1)}, bf16[4,32,3840]{2,1,0:T(8,128)(2,1)S(1)}, u32[]{:S(2)}, u32[]{:S(2)}) collective-permute-start(bf16[4,32,3840]{2,1,0:T(8,128)(2,1)S(1)} %get-tuple-element.66), channel_id=1, source_target_pairs={{0,8},{1,65},{8,16},{9,73},{16,24},{17,81},{24,0},{25,89},{64,72},... | collective-permute-start | bytes 2949128 | tf_op jit(solution)/shard_map/ppermute | solution.py:296
  30.2 2.9 %collective-permute-start.4 = (bf16[4,32,3840]{2,1,0:T(8,128)(2,1)S(1)}, bf16[4,32,3840]{2,1,0:T(8,128)(2,1)S(1)}, u32[]{:S(2)}, u32[]{:S(2)}) collective-permute-start(bf16[4,32,3840]{2,1,0:T(8,128)(2,1)S(1)} %get-tuple-element.67), channel_id=1, source_target_pairs={{0,16},{1,129},{8,24},{9,137},{16,0},{17,145},{24,8},{25,153},{64,... | collective-permute-start | bytes 2949128 | tf_op jit(solution)/shard_map/ppermute | solution.py:296
  33.1 1.3 %collective-permute-start.5 = (bf16[4,32,3840]{2,1,0:T(8,128)(2,1)S(1)}, bf16[4,32,3840]{2,1,0:T(8,128)(2,1)S(1)}, u32[]{:S(2)}, u32[]{:S(2)}) collective-permute-start(bf16[4,32,3840]{2,1,0:T(8,128)(2,1)S(1)} %get-tuple-element.68), channel_id=1, source_target_pairs={{0,24},{1,193},{8,0},{9,201},{16,8},{17,209},{24,16},{25,217},{64,... | collective-permute-start | bytes 2949128 | tf_op jit(solution)/shard_map/ppermute | solution.py:296
  35.3 2.0 %collective-permute-start.10 = (bf16[192,384]{1,0:T(8,128)(2,1)S(1)}, bf16[192,384]{1,0:T(8,128)(2,1)S(1)}, u32[]{:S(2)}, u32[]{:S(2)}) collective-permute-start(bf16[192,384]{1,0:T(8,128)(2,1)S(1)} %slice_bitcast_fusion), channel_id=1, source_target_pairs={{0,38},{2,0},{4,2},{6,4},{32,6},{34,32},{36,34},{38,36},{1,39},{3,... | collective-permute-start | bytes 442376 | tf_op jit(solution)/shard_map/ppermute | solution.py:33
  37.3 2.3 %collective-permute-done.7 = bf16[2,192,384]{2,1,0:T(8,128)(2,1)S(1)} collective-permute-done((bf16[2,192,384]{2,1,0:T(8,128)(2,1)S(1)}, bf16[2,192,384]{2,1,0:T(8,128)(2,1)S(1)}, u32[]{:S(2)}, u32[]{:S(2)}) %collective-permute-start.7) | collective-permute-done | bytes 294944 | tf_op jit(solution)/shard_map/ppermute | solution.py:33
  39.7 3.2 %shard_map.67.refs_4_ = bf16[384,3072]{1,0:T(8,128)(2,1)S(1)} custom-call(s32[6]{0:T(128)S(1)} %concatenate.16.info), custom_call_target="tpu_custom_call" | custom-call | flops 16515072 | bytes 2359296 | tf_op jit(solution)/shard_map/pallas_call | solution.py:52
  43.9 11.8 %collective-permute-done.4.refs_2_ = bf16[4,32,3840]{2,1,0:T(8,128)(2,1)S(1)} collective-permute-done((bf16[4,32,3840]{2,1,0:T(8,128)(2,1)S(1)}, bf16[4,32,3840]{2,1,0:T(8,128)(2,1)S(1)}, u32[]{:S(2)}, u32[]{:S(2)}) %collective-permute-start.4) | collective-permute-done | bytes 983072 | tf_op jit(solution)/shard_map/ppermute | solution.py:296
  55.7 2.5 %shard_map.68 = (bf16[512,3072]{1,0:T(8,128)(2,1)S(1)}, bf16[512,384]{1,0:T(8,128)(2,1)S(1)}, f32[384,512]{1,0:T(8,128)S(1)}, f32[384,512]{1,0:T(8,128)S(1)}) custom-call(s32[6]{0:T(128)S(1)} %concatenate.16.info, bf16[4,32,3840]{2,1,0:T(8,128)(2,1)S(1)} %get-tuple-element.75.refs_0_, bf16[4,32,3840]{2,1,0:T(8,128)(2,1)S(1)} %collective-permute-done.3.refs_1_, ...), custom_call_target="tpu_custom_call" | custom-call | flops 1207959552 | bytes 12582912 | tf_op jit(solution)/shard_map/pallas_call | solution.py:159
  58.5 2.9 %shard_map.69 = (f32[384,512]{1,0:T(8,128)S(1)}, f32[8,512]{1,0:T(8,128)S(1)}) custom-call(s32[6]{0:T(128)S(1)} %concatenate.16.info, bf16[8,192,384]{2,1,0:T(8,128)(2,1)S(1)} %constant_dynamic-update-slice_fusion.own, bf16[8,192,384]{2,1,0:T(8,128)(2,1)S(1)} %collective-permute-done.11.other, bf16[512,3072]{1,0:T(8,128)(2,1)S(1)} %get-tuple-element.80.context, ...), custom_call_target="tpu_custom_call" | custom-call | flops 1207959552 | bytes 12582912 | tf_op jit(solution)/shard_map/pallas_call | solution.py:195
  61.5 15.2 %all_to_all.10.stats = f32[16,8,512]{2,1,0:T(8,128)S(1)} all-to-all(f32[16,8,512]{2,1,0:T(8,128)S(1)} %broadcast_in_dim.5), channel_id=1, replica_groups=mesh['x'=4,'zh'=2,'y'=4,'zl'=4,'c'=2] {'x','y'}, dimensions={0} | all-to-all | bytes 524288 | tf_op jit(solution)/shard_map/all_to_all | solution.py:320
  76.7 2.3 %shard_map.70 = (bf16[384,512]{1,0:T(8,128)(2,1)S(1)}, bf16[8,192,384]{2,1,0:T(8,128)(2,1)S(1)}) custom-call(s32[6]{0:T(128)S(1)} %concatenate.16.info, f32[16,8,512]{2,1,0:T(8,128)S(1)} %all_to_all.10.stats, f32[384,512]{1,0:T(8,128)S(1)} %get-tuple-element.85.s, f32[384,512]{1,0:T(8,128)S(1)} %get-tuple-element.82.u_in.u, ...), custom_call_target="tpu_custom_call" | custom-call | flops 603979776 | bytes 12582912 | tf_op jit(solution)/shard_map/pallas_call | solution.py:241
  79.1 2.8 %collective-permute-done.12.received = bf16[8,192,384]{2,1,0:T(8,128)(2,1)S(1)} collective-permute-done((bf16[8,192,384]{2,1,0:T(8,128)(2,1)S(1)}, bf16[8,192,384]{2,1,0:T(8,128)(2,1)S(1)}, u32[]{:S(2)}, u32[]{:S(2)}) %collective-permute-start.12) | collective-permute-done | bytes 1179680 | tf_op jit(solution)/shard_map/ppermute | solution.py:280
  81.9 1.6 %shard_map.71 = (bf16[192,384]{1,0:T(8,128)(2,1)S(1)}, bf16[192,384]{1,0:T(8,128)(2,1)S(1)}, bf16[192,384]{1,0:T(8,128)(2,1)S(1)}, bf16[192,384]{1,0:T(8,128)(2,...) custom-call(s32[6]{0:T(128)S(1)} %concatenate.16.info, ...), custom_call_target="tpu_custom_call" | custom-call | flops 603979776 | bytes 12582912 | tf_op jit(solution)/shard_map/pallas_call | solution.py:268
  83.5 3.2 %collective-permute-start.17 = (bf16[96,384]{1,0:T(8,128)(2,1)S(1)}, bf16[96,384]{1,0:T(8,128)(2,1)S(1)}, u32[]{:S(2)}, u32[]{:S(2)}) collective-permute-start(bf16[96,384]{1,0:T(8,128)(2,1)S(1)} %get-tuple-element.93), channel_id=1, source_target_pairs={{0,4},{2,6},{4,32},{6,34},{32,36},{34,38},{36,0},{38,2},{1,5},{3,7... | collective-permute-start | bytes 221192 | tf_op jit(solution)/shard_map/ppermute | solution.py:33
  86.7 2.1 %collective-permute-start.13 = (bf16[192,384]{1,0:T(8,128)(2,1)S(1)}, bf16[192,384]{1,0:T(8,128)(2,1)S(1)}, u32[]{:S(2)}, u32[]{:S(2)}) collective-permute-start(bf16[192,384]{1,0:T(8,128)(2,1)S(1)} %get-tuple-element.89), channel_id=1, source_target_pairs={{0,2},{2,4},{4,6},{6,32},{32,34},{34,36},{36,38},{38,0},{1,3},{3,5... | collective-permute-start | bytes 442376 | tf_op jit(solution)/shard_map/ppermute | solution.py:33
  88.9 2.0 %collective-permute-start.15 = (bf16[192,384]{1,0:T(8,128)(2,1)S(1)}, bf16[192,384]{1,0:T(8,128)(2,1)S(1)}, u32[]{:S(2)}, u32[]{:S(2)}) collective-permute-start(bf16[192,384]{1,0:T(8,128)(2,1)S(1)} %get-tuple-element.91), channel_id=1, source_target_pairs={{0,2},{2,4},{4,6},{6,32},{32,34},{34,36},{36,38},{38,0},{1,3},{3,5... | collective-permute-start | bytes 442376 | tf_op jit(solution)/shard_map/ppermute | solution.py:33
  90.9 2.5 %collective-permute-done.17 = bf16[96,384]{1,0:T(8,128)(2,1)S(1)} collective-permute-done((bf16[96,384]{1,0:T(8,128)(2,1)S(1)}, bf16[96,384]{1,0:T(8,128)(2,1)S(1)}, u32[]{:S(2)}, u32[]{:S(2)}) %collective-permute-start.17) | collective-permute-done | bytes 73760 | tf_op jit(solution)/shard_map/ppermute | solution.py:33
  93.4 1.6 %collective-permute-start.18 = (bf16[96,384]{1,0:T(8,128)(2,1)S(1)}, bf16[96,384]{1,0:T(8,128)(2,1)S(1)}, u32[]{:S(2)}, u32[]{:S(2)}) collective-permute-start(bf16[96,384]{1,0:T(8,128)(2,1)S(1)} %get-tuple-element.94), channel_id=1, source_target_pairs={{0,36},{2,38},{4,0},{6,2},{32,4},{34,6},{36,32},{38,34},{1,37},{3,... | collective-permute-start | bytes 221192 | tf_op jit(solution)/shard_map/ppermute | solution.py:33
  95.1 4.5 %collective-permute-done.18 = bf16[96,384]{1,0:T(8,128)(2,1)S(1)} collective-permute-done((bf16[96,384]{1,0:T(8,128)(2,1)S(1)}, bf16[96,384]{1,0:T(8,128)(2,1)S(1)}, u32[]{:S(2)}, u32[]{:S(2)}) %collective-permute-start.18) | collective-permute-done | bytes 73760 | tf_op jit(solution)/shard_map/ppermute | solution.py:33
  100.5 3.8 %collective-permute-start.19 = (bf16[192,384]{1,0:T(8,128)(2,1)}, bf16[192,384]{1,0:T(8,128)(2,1)}, u32[]{:S(2)}, u32[]{:S(2)}) collective-permute-start(bf16[192,384]{1,0:T(8,128)(2,1)} %get-tuple-element.101), channel_id=1, source_target_pairs={{0,4},{2,6},{4,32},{6,34},{32,36},{34,38},{36,0},{38,2},{1,5},{3,7... | collective-permute-start | bytes 442376 | tf_op jit(solution)/shard_map/ppermute | solution.py:33
  104.7 5.0 %collective-permute-done.19 = bf16[192,384]{1,0:T(8,128)(2,1)} collective-permute-done((bf16[192,384]{1,0:T(8,128)(2,1)}, bf16[192,384]{1,0:T(8,128)(2,1)}, u32[]{:S(2)}, u32[]{:S(2)}) %collective-permute-start.19) | collective-permute-done | bytes 147488 | tf_op jit(solution)/shard_map/ppermute | solution.py:33
  109.7 3.5 %collective-permute-done.20 = bf16[192,384]{1,0:T(8,128)(2,1)} collective-permute-done((bf16[192,384]{1,0:T(8,128)(2,1)}, bf16[192,384]{1,0:T(8,128)(2,1)}, u32[]{:S(2)}, u32[]{:S(2)}) %collective-permute-start.20) | collective-permute-done | bytes 147488 | tf_op jit(solution)/shard_map/ppermute | solution.py:33
  113.1 1.8 %fusion.7 = f32[192,384]{1,0:T(8,128)} fusion(bf16[192,384]{1,0:T(8,128)(2,1)} %collective-permute-done.20, bf16[192,384]{1,0:T(8,128)(2,1)} %collective-permute-done.19, bf16[192,384]{1,0:T(8,128)(2,1)S(1)} %collective-permute-done.14, bf16[192,384]{1,0:T(8,128)(2,1)S(1)} %collective-permute-done.13, f32[3,192,384]{2,1,0:T(8,128)S(1)} %get-tuple-element.88, ...), kind=kLoop, calls=%fused_computation.12 | loop fusion | flops 737280 | bytes 1327112 | tf_op jit(solution)/shard_map/mul | solution.py:340
  (39 shorter events, 7.6 us)
Async XLA Ops:
  0.0 19.2 %copy-start.2 = (bf16[192,384]{1,0:T(8,128)(2,1)S(1)}, bf16[192,384]{1,0:T(8,128)(2,1)}, u32[]{:S(2)}) copy-start(bf16[192,384]{1,0:T(8,128)(2,1)} %param.8) | copy-start | bytes 442372
  0.0 13.3 %all-to-all-start = ((bf16[8,32,384]{2,1,0:T(8,128)(2,1)}), bf16[8,32,384]{2,1,0:T(8,128)(2,1)S(1)}, u32[]{:S(2)}, u32[]{:S(2)}) async-start(bf16[8,32,384]{2,1,0:T(8,128)(2,1)} %bitcast.36), calls=%async_computation | async-start | bytes 393216 | tf_op jit(solution)/shard_map/all_to_all | solution.py:305
  6.1 13.1 %collective-permute-start.8 = (bf16[192,384]{1,0:T(8,128)(2,1)}, bf16[192,384]{1,0:T(8,128)(2,1)S(1)}, u32[]{:S(2)}, u32[]{:S(2)}) collective-permute-start(bf16[192,384]{1,0:T(8,128)(2,1)} %param.8), channel_id=1, source_target_pairs={{0,38},{2,0},{4,2},{6,4},{32,6},{34,32},{36,34},{38,36},{1,39},{3,... | collective-permute-start | bytes 442376 | tf_op jit(solution)/shard_map/ppermute | solution.py:33
  6.2 13.0 %collective-permute-start.6 = (bf16[192,384]{1,0:T(8,128)(2,1)}, bf16[192,384]{1,0:T(8,128)(2,1)S(1)}, u32[]{:S(2)}, u32[]{:S(2)}) collective-permute-start(bf16[192,384]{1,0:T(8,128)(2,1)} %param.8), channel_id=1, source_target_pairs={{0,2},{2,4},{4,6},{6,32},{32,34},{34,36},{36,38},{38,0},{1,3},{3,5... | collective-permute-start | bytes 442376 | tf_op jit(solution)/shard_map/ppermute | solution.py:33
  9.7 1.0 copy-start
  10.7 1.0 copy-start.1
  13.5 11.3 %collective-permute-start = (bf16[64,3072]{1,0:T(8,128)(2,1)S(1)}, bf16[64,3072]{1,0:T(8,128)(2,1)S(1)}, u32[]{:S(2)}, u32[]{:S(2)}) collective-permute-start(bf16[64,3072]{1,0:T(8,128)(2,1)S(1)} %get-tuple-element.58), channel_id=1, source_target_pairs={{0,64},{1,9},{8,72},{9,17},{16,80},{17,25},{24,88},{25,1},{64,128}... | collective-permute-start | bytes 1179656 | tf_op jit(solution)/shard_map/ppermute | solution.py:296
  15.0 12.7 %collective-permute-start.1 = (bf16[64,3072]{1,0:T(8,128)(2,1)S(1)}, bf16[64,3072]{1,0:T(8,128)(2,1)S(1)}, u32[]{:S(2)}, u32[]{:S(2)}) collective-permute-start(bf16[64,3072]{1,0:T(8,128)(2,1)S(1)} %get-tuple-element.59), channel_id=1, source_target_pairs={{0,128},{1,17},{8,136},{9,25},{16,144},{17,1},{24,152},{25,9},{64,... | collective-permute-start | bytes 1179656 | tf_op jit(solution)/shard_map/ppermute | solution.py:296
  17.8 10.0 %collective-permute-start.2 = (bf16[64,3072]{1,0:T(8,128)(2,1)S(1)}, bf16[64,3072]{1,0:T(8,128)(2,1)S(1)}, u32[]{:S(2)}, u32[]{:S(2)}) collective-permute-start(bf16[64,3072]{1,0:T(8,128)(2,1)S(1)} %get-tuple-element.60), channel_id=1, source_target_pairs={{0,192},{1,25},{8,200},{9,1},{16,208},{17,9},{24,216},{25,17},{64,... | collective-permute-start | bytes 1179656 | tf_op jit(solution)/shard_map/ppermute | solution.py:296
  19.3 16.0 %collective-permute-start.9 = (bf16[2,192,384]{2,1,0:T(8,128)(2,1)S(1)}, bf16[2,192,384]{2,1,0:T(8,128)(2,1)S(1)}, u32[]{:S(2)}, u32[]{:S(2)}) collective-permute-start(bf16[2,192,384]{2,1,0:T(8,128)(2,1)S(1)} %get-tuple-element.71), channel_id=1, source_target_pairs={{0,36},{2,38},{4,0},{6,2},{32,4},{34,6},{36,32},{38,34},{1,37},{3,... | collective-permute-start | bytes 884744 | tf_op jit(solution)/shard_map/ppermute | solution.py:33
  24.8 14.8 %collective-permute-start.7 = (bf16[2,192,384]{2,1,0:T(8,128)(2,1)S(1)}, bf16[2,192,384]{2,1,0:T(8,128)(2,1)S(1)}, u32[]{:S(2)}, u32[]{:S(2)}) collective-permute-start(bf16[2,192,384]{2,1,0:T(8,128)(2,1)S(1)} %get-tuple-element.70), channel_id=1, source_target_pairs={{0,4},{2,6},{4,32},{6,34},{32,36},{34,38},{36,0},{38,2},{1,5},{3,7... | collective-permute-start | bytes 884744 | tf_op jit(solution)/shard_map/ppermute | solution.py:33
  28.5 15.4 %collective-permute-start.3 = (bf16[4,32,3840]{2,1,0:T(8,128)(2,1)S(1)}, bf16[4,32,3840]{2,1,0:T(8,128)(2,1)S(1)}, u32[]{:S(2)}, u32[]{:S(2)}) collective-permute-start(bf16[4,32,3840]{2,1,0:T(8,128)(2,1)S(1)} %get-tuple-element.66), channel_id=1, source_target_pairs={{0,8},{1,65},{8,16},{9,73},{16,24},{17,81},{24,0},{25,89},{64,72},... | collective-permute-start | bytes 2949128 | tf_op jit(solution)/shard_map/ppermute | solution.py:296
  30.2 25.5 %collective-permute-start.4 = (bf16[4,32,3840]{2,1,0:T(8,128)(2,1)S(1)}, bf16[4,32,3840]{2,1,0:T(8,128)(2,1)S(1)}, u32[]{:S(2)}, u32[]{:S(2)}) collective-permute-start(bf16[4,32,3840]{2,1,0:T(8,128)(2,1)S(1)} %get-tuple-element.67), channel_id=1, source_target_pairs={{0,16},{1,129},{8,24},{9,137},{16,0},{17,145},{24,8},{25,153},{64,... | collective-permute-start | bytes 2949128 | tf_op jit(solution)/shard_map/ppermute | solution.py:296
  33.1 22.6 %collective-permute-start.5 = (bf16[4,32,3840]{2,1,0:T(8,128)(2,1)S(1)}, bf16[4,32,3840]{2,1,0:T(8,128)(2,1)S(1)}, u32[]{:S(2)}, u32[]{:S(2)}) collective-permute-start(bf16[4,32,3840]{2,1,0:T(8,128)(2,1)S(1)} %get-tuple-element.68), channel_id=1, source_target_pairs={{0,24},{1,193},{8,0},{9,201},{16,8},{17,209},{24,16},{25,217},{64,... | collective-permute-start | bytes 2949128 | tf_op jit(solution)/shard_map/ppermute | solution.py:296
  35.3 7.6 %collective-permute-start.10 = (bf16[192,384]{1,0:T(8,128)(2,1)S(1)}, bf16[192,384]{1,0:T(8,128)(2,1)S(1)}, u32[]{:S(2)}, u32[]{:S(2)}) collective-permute-start(bf16[192,384]{1,0:T(8,128)(2,1)S(1)} %slice_bitcast_fusion), channel_id=1, source_target_pairs={{0,38},{2,0},{4,2},{6,4},{32,6},{34,32},{36,34},{38,36},{1,39},{3,... | collective-permute-start | bytes 442376 | tf_op jit(solution)/shard_map/ppermute | solution.py:33
  55.7 2.8 %collective-permute-start.11 = (bf16[8,192,384]{2,1,0:T(8,128)(2,1)S(1)}, bf16[8,192,384]{2,1,0:T(8,128)(2,1)S(1)}, u32[]{:S(2)}, u32[]{:S(2)}) collective-permute-start(bf16[8,192,384]{2,1,0:T(8,128)(2,1)S(1)} %constant_dynamic-update-slice_fusion.own), channel_id=1, source_target_pairs={{0,1},{1,0},{2,3},{3,2},{4,5},{5,4},{6,7},{7,6},{8,9},{9,8},{10,11... | collective-permute-start | bytes 3538952 | tf_op jit(solution)/shard_map/ppermute | solution.py:280
  79.0 2.9 %collective-permute-start.12 = (bf16[8,192,384]{2,1,0:T(8,128)(2,1)S(1)}, bf16[8,192,384]{2,1,0:T(8,128)(2,1)S(1)}, u32[]{:S(2)}, u32[]{:S(2)}) collective-permute-start(bf16[8,192,384]{2,1,0:T(8,128)(2,1)S(1)} %get-tuple-element.87), channel_id=1, source_target_pairs={{0,1},{1,0},{2,3},{3,2},{4,5},{5,4},{6,7},{7,6},{8,9},{9,8},{10,11... | collective-permute-start | bytes 3538952 | tf_op jit(solution)/shard_map/ppermute | solution.py:280
  83.5 9.9 %collective-permute-start.17 = (bf16[96,384]{1,0:T(8,128)(2,1)S(1)}, bf16[96,384]{1,0:T(8,128)(2,1)S(1)}, u32[]{:S(2)}, u32[]{:S(2)}) collective-permute-start(bf16[96,384]{1,0:T(8,128)(2,1)S(1)} %get-tuple-element.93), channel_id=1, source_target_pairs={{0,4},{2,6},{4,32},{6,34},{32,36},{34,38},{36,0},{38,2},{1,5},{3,7... | collective-permute-start | bytes 221192 | tf_op jit(solution)/shard_map/ppermute | solution.py:33
  86.7 12.9 %collective-permute-start.13 = (bf16[192,384]{1,0:T(8,128)(2,1)S(1)}, bf16[192,384]{1,0:T(8,128)(2,1)S(1)}, u32[]{:S(2)}, u32[]{:S(2)}) collective-permute-start(bf16[192,384]{1,0:T(8,128)(2,1)S(1)} %get-tuple-element.89), channel_id=1, source_target_pairs={{0,2},{2,4},{4,6},{6,32},{32,34},{34,36},{36,38},{38,0},{1,3},{3,5... | collective-permute-start | bytes 442376 | tf_op jit(solution)/shard_map/ppermute | solution.py:33
  88.9 10.7 %collective-permute-start.14 = (bf16[192,384]{1,0:T(8,128)(2,1)S(1)}, bf16[192,384]{1,0:T(8,128)(2,1)S(1)}, u32[]{:S(2)}, u32[]{:S(2)}) collective-permute-start(bf16[192,384]{1,0:T(8,128)(2,1)S(1)} %get-tuple-element.90), channel_id=1, source_target_pairs={{0,38},{2,0},{4,2},{6,4},{32,6},{34,32},{36,34},{38,36},{1,39},{3,... | collective-permute-start | bytes 442376 | tf_op jit(solution)/shard_map/ppermute | solution.py:33
  88.9 10.7 %collective-permute-start.15 = (bf16[192,384]{1,0:T(8,128)(2,1)S(1)}, bf16[192,384]{1,0:T(8,128)(2,1)S(1)}, u32[]{:S(2)}, u32[]{:S(2)}) collective-permute-start(bf16[192,384]{1,0:T(8,128)(2,1)S(1)} %get-tuple-element.91), channel_id=1, source_target_pairs={{0,2},{2,4},{4,6},{6,32},{32,34},{34,36},{36,38},{38,0},{1,3},{3,5... | collective-permute-start | bytes 442376 | tf_op jit(solution)/shard_map/ppermute | solution.py:33
  90.9 8.8 %collective-permute-start.16 = (bf16[192,384]{1,0:T(8,128)(2,1)S(1)}, bf16[192,384]{1,0:T(8,128)(2,1)S(1)}, u32[]{:S(2)}, u32[]{:S(2)}) collective-permute-start(bf16[192,384]{1,0:T(8,128)(2,1)S(1)} %get-tuple-element.92), channel_id=1, source_target_pairs={{0,38},{2,0},{4,2},{6,4},{32,6},{34,32},{36,34},{38,36},{1,39},{3,... | collective-permute-start | bytes 442376 | tf_op jit(solution)/shard_map/ppermute | solution.py:33
  93.4 6.2 %collective-permute-start.18 = (bf16[96,384]{1,0:T(8,128)(2,1)S(1)}, bf16[96,384]{1,0:T(8,128)(2,1)S(1)}, u32[]{:S(2)}, u32[]{:S(2)}) collective-permute-start(bf16[96,384]{1,0:T(8,128)(2,1)S(1)} %get-tuple-element.94), channel_id=1, source_target_pairs={{0,36},{2,38},{4,0},{6,2},{32,4},{34,6},{36,32},{38,34},{1,37},{3,... | collective-permute-start | bytes 221192 | tf_op jit(solution)/shard_map/ppermute | solution.py:33
  100.5 9.1 %collective-permute-start.19 = (bf16[192,384]{1,0:T(8,128)(2,1)}, bf16[192,384]{1,0:T(8,128)(2,1)}, u32[]{:S(2)}, u32[]{:S(2)}) collective-permute-start(bf16[192,384]{1,0:T(8,128)(2,1)} %get-tuple-element.101), channel_id=1, source_target_pairs={{0,4},{2,6},{4,32},{6,34},{32,36},{34,38},{36,0},{38,2},{1,5},{3,7... | collective-permute-start | bytes 442376 | tf_op jit(solution)/shard_map/ppermute | solution.py:33
  104.4 8.7 %collective-permute-start.20 = (bf16[192,384]{1,0:T(8,128)(2,1)}, bf16[192,384]{1,0:T(8,128)(2,1)}, u32[]{:S(2)}, u32[]{:S(2)}) collective-permute-start(bf16[192,384]{1,0:T(8,128)(2,1)} %get-tuple-element.102), channel_id=1, source_target_pairs={{0,36},{2,38},{4,0},{6,2},{32,4},{34,6},{36,32},{38,34},{1,37},{3,... | collective-permute-start | bytes 442376 | tf_op jit(solution)/shard_map/ppermute | solution.py:33

commit v3 on v2

--- a/solution.py
+++ b/solution.py
@@ -33,19 +33,22 @@
     return lax.ppermute(v, axis, [(s, (s + k) % n) for s in range(n)])
 
 
+def parity(info, rows, cols):
+    m = (rows * W * INT(MULT) + info[4]) + cols * INT(MULT)
+    m = m ^ lax.shift_right_logical(m, INT(16))
+    m = m * INT(73244475)
+    m = m ^ info[5]
+    m = m ^ lax.shift_right_logical(m, INT(15))
+    return lax.shift_right_logical(m, INT(9)) & INT(1)
+
+
 def probe_kernel(info, out):
-    x, y, seed0, seed1 = info[0], info[1], info[4], info[5]
+    x, y = info[0], info[1]
     cols = lax.broadcasted_iota(INT, (1, F), 1) + pl.program_id(0) * F
     rows = lax.broadcasted_iota(INT, (R, 1), 0)
     for zh in range(2):
         d = rows + (x * 8 + zh * 4 + y) * R
-        m = (d * W * INT(MULT) + seed0) + cols * INT(MULT)
-        m = m ^ lax.shift_right_logical(m, INT(16))
-        m = m * INT(73244475)
-        m = m ^ seed1
-        m = m ^ lax.shift_right_logical(m, INT(15))
-        parity = lax.shift_right_logical(m, INT(9)) & INT(1)
-        out[zh * R : (zh + 1) * R, :] = (1 - 2 * parity).astype(F32).astype(BF16)
+        out[zh * R : (zh + 1) * R, :] = (1 - 2 * parity(info, d, cols)).astype(F32).astype(BF16)
 
 
 def make_probe(info):
@@ -276,6 +279,40 @@
     )(info, grad, context, received)
 
 
+def last_kernel(info, kept, a, b, up, down, out):
+    rows = lax.broadcasted_iota(INT, (R, 1), 0) + (info[0] * 8 + info[2] // 4 * 4 + info[1]) * R
+    cols = lax.broadcasted_iota(INT, (1, F), 1) + (info[2] % 4 * 2 + info[3]) * F
+    total = kept[0] + a[...].astype(F32) + b[...].astype(F32) + up[...].astype(F32) + down[...].astype(F32)
+    out[...] = jnp.where(parity(info, rows, cols) == 0, total, -total)
+
+
+def last(info, kept, *parts):
+    return pl.pallas_call(
+        last_kernel,
+        in_specs=[pl.BlockSpec(memory_space=pltpu.SMEM)] + [pl.BlockSpec(memory_space=pltpu.VMEM)] * 5,
+        out_shape=jax.ShapeDtypeStruct((R, F), F32),
+        compiler_params=pltpu.CompilerParams(vmem_limit_bytes=16 * MIB),
+        cost_estimate=pl.CostEstimate(flops=20 * R * F, bytes_accessed=20 * R * F, transcendentals=0),
+    )(info, kept, *parts)
+
+
+def between_kernel(kept, three_up, three_down, four_up, four_down, up, down):
+    h = R // 2
+    up[:h] = (kept[1, :h] + three_up[:h].astype(F32) + four_up[...].astype(F32)).astype(BF16)
+    up[h:] = (kept[1, h:] + three_up[h:].astype(F32)).astype(BF16)
+    down[:h] = (kept[2, :h] + three_down[:h].astype(F32)).astype(BF16)
+    down[h:] = (kept[2, h:] + three_down[h:].astype(F32) + four_down[...].astype(F32)).astype(BF16)
+
+
+def between(*parts):
+    return pl.pallas_call(
+        between_kernel,
+        out_shape=[jax.ShapeDtypeStruct((R, F), BF16)] * 2,
+        compiler_params=pltpu.CompilerParams(vmem_limit_bytes=16 * MIB),
+        cost_estimate=pl.CostEstimate(flops=8 * R * F, bytes_accessed=20 * R * F, transcendentals=0),
+    )(*parts)
+
+
 def swap(v):
     return lax.ppermute(v, "c", [(0, 1), (1, 0)])
 
@@ -321,23 +358,12 @@
     grad, send = away(info, stats, s, u, w, rows)
     near_up, near_down, three_up, three_down, four_up, four_down, kept = home(info, grad, rows, swap(send))
 
-    near_up, near_down, three_up, three_down, four_up, four_down = lax.optimization_barrier(
-        (
-            shift(near_up, Z, 1),
-            shift(near_down, Z, -1),
-            shift(three_up, Z, 1),
-            shift(three_down, Z, -1),
-            shift(four_up, Z, 2),
-            shift(four_down, Z, -2),
-        )
-    )
-    none = jnp.zeros((R // 2, F), F32)
-    up = kept[1] + three_up.astype(F32) + jnp.concatenate([four_up.astype(F32), none])
-    down = kept[2] + three_down.astype(F32) + jnp.concatenate([none, four_down.astype(F32)])
-    up, down = shift(up.astype(BF16), Z, 2), shift(down.astype(BF16), Z, -2)
-    total = kept[0] + near_up.astype(F32) + near_down.astype(F32) + up.astype(F32) + down.astype(F32)
-    signs = lax.dynamic_slice(probe, (zh * R, (zl * 2 + c) * F), (R, F))
-    return signs.astype(F32) * total
+    near_up, near_down = shift(near_up, Z, 1), shift(near_down, Z, -1)
+    three_up, three_down = shift(three_up, Z, 1), shift(three_down, Z, -1)
+    four_up, four_down = shift(four_up, Z, 2), shift(four_down, Z, -2)
+    up, down = between(kept, three_up, three_down, four_up, four_down)
+    up, down = shift(up, Z, 2), shift(down, Z, -2)
+    return last(info, kept, near_up, near_down, up, down)
 
 
 def solution(mesh):

time: 115 us -> 110 us (0.957)
  waiting for transfers between devices: 37.9 us -> 31.2 us
  starting transfers between devices: 40.6 us -> 43.5 us
  other arithmetic: 2.66 us -> 0.06 us
  Pallas kernels: 14.6 us -> 16.1 us
    ppermute x13, waiting for transfers between devices: 18.7 us -> 11.9 us  [shift(): return lax.ppermute(v, axis, [(s, (s + k) % n) for s in range(n)])]
    ppermute x13, starting transfers between devices: 22.8 us -> 25.7 us  [shift(): return lax.ppermute(v, axis, [(s, (s + k) % n) for s in range(n)])]
    mul x1 -> x0, other arithmetic: 1.81 us -> none  [on_device(): return signs.astype(F32) * total]
    pallas_call x0 -> x2, Pallas kernels: none -> 1.56 us  [the longest x1 1.47 us: last(): pl.pallas_call(last_kernel, in_specs=[pl.BlockSpec(memory_space=pltpu.SME...]
  transfers between devices with their start and end apart: 22 -> 22, of which waited for: 13 -> 10; matrix products, arithmetic and copies ran while one was open for 2% -> 2% of each run, Pallas kernels for 7% -> 7%
where the time goes in v3:
time: 110 us
  starting transfers between devices  43.5 us (40%)
  waiting for transfers between devices  31.2 us (28%)
  Pallas kernels  16.1 us (15%)
  blocking collectives  15.2 us (14%)
  local copies, waits for them, and re-layouts  3.76 us (3%)
    ppermute x13, starting transfers between devices, shift(): return lax.ppermute(v, axis, [(s, (s + k) % n) for s in range(n)])  25.7 us
    ppermute x6, waiting for transfers between devices, leg(): out.append(lax.ppermute(blocks[k], XYC, pairs))  15.6 us
    all_to_all x1, blocking collectives, on_device(): lax.all_to_all(jnp.broadcast_to(stats[None], (16, 8, TOK)), XY, 0, 0, til...  15.2 us
    ppermute x13, waiting for transfers between devices, shift(): return lax.ppermute(v, axis, [(s, (s + k) % n) for s in range(n)])  11.9 us
    ppermute x6, starting transfers between devices, leg(): out.append(lax.ppermute(blocks[k], XYC, pairs))  11.6 us
    all_to_all x1, starting transfers between devices, on_device(): rows = lax.all_to_all(context.reshape(8, OWN, F), T, 0, 0, tiled=True)  6.14 us
    ppermute x2, waiting for transfers between devices, swap(): return lax.ppermute(v, 'c', [(0, 1), (1, 0)])  3.23 us
    pallas_call x1, Pallas kernels, make_probe(): pl.pallas_call(probe_kernel, grid=(8,), in_specs=[pl.BlockSpec(memory_spa...  3.21 us
  transfers between devices with their start and end apart: 22, of which 10 were waited for; matrix products, arithmetic and copies ran while one was open for 2% of the time, Pallas kernels for 7%

profile of v3, /device:TPU:32, one launch (start us, length us, event | category | flops | bytes accessed | tf_op | source)
XLA Modules:
  0.0 110.0 jit_solution(10120274703813014493)
XLA Ops:
  0.0 6.1 %all-to-all-start = ((bf16[8,32,384]{2,1,0:T(8,128)(2,1)}), bf16[8,32,384]{2,1,0:T(8,128)(2,1)S(1)}, u32[]{:S(2)}, u32[]{:S(2)}) async-start(bf16[8,32,384]{2,1,0:T(8,128)(2,1)} %bitcast.14), calls=%async_computation | async-start | bytes 393216 | tf_op jit(solution)/shard_map/all_to_all | solution.py:342
  6.2 2.0 %collective-permute-start.6 = (bf16[192,384]{1,0:T(8,128)(2,1)}, bf16[192,384]{1,0:T(8,128)(2,1)S(1)}, u32[]{:S(2)}, u32[]{:S(2)}) collective-permute-start(bf16[192,384]{1,0:T(8,128)(2,1)} %param.8), channel_id=1, source_target_pairs={{0,2},{2,4},{4,6},{6,32},{32,34},{34,36},{36,38},{38,0},{1,3},{3,5... | collective-permute-start | bytes 442376 | tf_op jit(solution)/shard_map/ppermute | solution.py:33
  9.7 1.0 copy-done
  11.7 1.2 %shard_map.64 = (bf16[4,32,3072]{2,1,0:T(8,128)(2,1)S(1)}, f32[384,1]{1,0:T(8,128)S(1)}) custom-call(s32[6]{0:T(128)S(1)} %concatenate.6.info, bf16[32,6144]{1,0:T(8,128)(2,1)S(1)} %copy-done, bf16[32,6144]{1,0:T(8,128)(2,1)S(1)} %copy-done.1, f32[32,192]{1,0:T(8,128)S(1)} %reshape.8.gains), custom_call_target="tpu_custom_call" | custom-call | bytes 1572864 | tf_op jit(solution)/shard_map/pallas_call | solution.py:96
  13.5 1.6 %collective-permute-start = (bf16[64,3072]{1,0:T(8,128)(2,1)S(1)}, bf16[64,3072]{1,0:T(8,128)(2,1)S(1)}, u32[]{:S(2)}, u32[]{:S(2)}) collective-permute-start(bf16[64,3072]{1,0:T(8,128)(2,1)S(1)} %get-tuple-element.54), channel_id=1, source_target_pairs={{0,64},{1,9},{8,72},{9,17},{16,80},{17,25},{24,88},{25,1},{64,128}... | collective-permute-start | bytes 1179656 | tf_op jit(solution)/shard_map/ppermute | solution.py:333
  15.0 2.7 %collective-permute-start.1 = (bf16[64,3072]{1,0:T(8,128)(2,1)S(1)}, bf16[64,3072]{1,0:T(8,128)(2,1)S(1)}, u32[]{:S(2)}, u32[]{:S(2)}) collective-permute-start(bf16[64,3072]{1,0:T(8,128)(2,1)S(1)} %get-tuple-element.55), channel_id=1, source_target_pairs={{0,128},{1,17},{8,136},{9,25},{16,144},{17,1},{24,152},{25,9},{64,... | collective-permute-start | bytes 1179656 | tf_op jit(solution)/shard_map/ppermute | solution.py:333
  17.8 1.4 %collective-permute-start.2 = (bf16[64,3072]{1,0:T(8,128)(2,1)S(1)}, bf16[64,3072]{1,0:T(8,128)(2,1)S(1)}, u32[]{:S(2)}, u32[]{:S(2)}) collective-permute-start(bf16[64,3072]{1,0:T(8,128)(2,1)S(1)} %get-tuple-element.56), channel_id=1, source_target_pairs={{0,192},{1,25},{8,200},{9,1},{16,208},{17,9},{24,216},{25,17},{64,... | collective-permute-start | bytes 1179656 | tf_op jit(solution)/shard_map/ppermute | solution.py:333
  19.3 5.5 %collective-permute-start.9 = (bf16[2,192,384]{2,1,0:T(8,128)(2,1)S(1)}, bf16[2,192,384]{2,1,0:T(8,128)(2,1)S(1)}, u32[]{:S(2)}, u32[]{:S(2)}) collective-permute-start(bf16[2,192,384]{2,1,0:T(8,128)(2,1)S(1)} %get-tuple-element.67), channel_id=1, source_target_pairs={{0,36},{2,38},{4,0},{6,2},{32,4},{34,6},{36,32},{38,34},{1,37},{3,... | collective-permute-start | bytes 884744 | tf_op jit(solution)/shard_map/ppermute | solution.py:33
  24.8 2.9 %collective-permute-done.1.refs_2_ = bf16[64,3072]{1,0:T(8,128)(2,1)S(1)} collective-permute-done((bf16[64,3072]{1,0:T(8,128)(2,1)S(1)}, bf16[64,3072]{1,0:T(8,128)(2,1)S(1)}, u32[]{:S(2)}, u32[]{:S(2)}) %collective-permute-start.1) | collective-permute-done | bytes 393248 | tf_op jit(solution)/shard_map/ppermute | solution.py:333
  28.5 1.7 %collective-permute-start.3 = (bf16[4,32,3840]{2,1,0:T(8,128)(2,1)S(1)}, bf16[4,32,3840]{2,1,0:T(8,128)(2,1)S(1)}, u32[]{:S(2)}, u32[]{:S(2)}) collective-permute-start(bf16[4,32,3840]{2,1,0:T(8,128)(2,1)S(1)} %get-tuple-element.62), channel_id=1, source_target_pairs={{0,8},{1,65},{8,16},{9,73},{16,24},{17,81},{24,0},{25,89},{64,72},... | collective-permute-start | bytes 2949128 | tf_op jit(solution)/shard_map/ppermute | solution.py:333
  30.2 2.9 %collective-permute-start.4 = (bf16[4,32,3840]{2,1,0:T(8,128)(2,1)S(1)}, bf16[4,32,3840]{2,1,0:T(8,128)(2,1)S(1)}, u32[]{:S(2)}, u32[]{:S(2)}) collective-permute-start(bf16[4,32,3840]{2,1,0:T(8,128)(2,1)S(1)} %get-tuple-element.63), channel_id=1, source_target_pairs={{0,16},{1,129},{8,24},{9,137},{16,0},{17,145},{24,8},{25,153},{64,... | collective-permute-start | bytes 2949128 | tf_op jit(solution)/shard_map/ppermute | solution.py:333
  33.1 1.3 %collective-permute-start.5 = (bf16[4,32,3840]{2,1,0:T(8,128)(2,1)S(1)}, bf16[4,32,3840]{2,1,0:T(8,128)(2,1)S(1)}, u32[]{:S(2)}, u32[]{:S(2)}) collective-permute-start(bf16[4,32,3840]{2,1,0:T(8,128)(2,1)S(1)} %get-tuple-element.64), channel_id=1, source_target_pairs={{0,24},{1,193},{8,0},{9,201},{16,8},{17,209},{24,16},{25,217},{64,... | collective-permute-start | bytes 2949128 | tf_op jit(solution)/shard_map/ppermute | solution.py:333
  35.3 2.0 %collective-permute-start.10 = (bf16[192,384]{1,0:T(8,128)(2,1)S(1)}, bf16[192,384]{1,0:T(8,128)(2,1)S(1)}, u32[]{:S(2)}, u32[]{:S(2)}) collective-permute-start(bf16[192,384]{1,0:T(8,128)(2,1)S(1)} %slice_bitcast_fusion), channel_id=1, source_target_pairs={{0,38},{2,0},{4,2},{6,4},{32,6},{34,32},{36,34},{38,36},{1,39},{3,... | collective-permute-start | bytes 442376 | tf_op jit(solution)/shard_map/ppermute | solution.py:33
  37.3 2.3 %collective-permute-done.7 = bf16[2,192,384]{2,1,0:T(8,128)(2,1)S(1)} collective-permute-done((bf16[2,192,384]{2,1,0:T(8,128)(2,1)S(1)}, bf16[2,192,384]{2,1,0:T(8,128)(2,1)S(1)}, u32[]{:S(2)}, u32[]{:S(2)}) %collective-permute-start.7) | collective-permute-done | bytes 294944 | tf_op jit(solution)/shard_map/ppermute | solution.py:33
  39.7 3.2 %shard_map.67.refs_4_ = bf16[384,3072]{1,0:T(8,128)(2,1)S(1)} custom-call(s32[6]{0:T(128)S(1)} %concatenate.6.info), custom_call_target="tpu_custom_call" | custom-call | flops 16515072 | bytes 2359296 | tf_op jit(solution)/shard_map/pallas_call | solution.py:55
  43.9 11.8 %collective-permute-done.4.refs_2_ = bf16[4,32,3840]{2,1,0:T(8,128)(2,1)S(1)} collective-permute-done((bf16[4,32,3840]{2,1,0:T(8,128)(2,1)S(1)}, bf16[4,32,3840]{2,1,0:T(8,128)(2,1)S(1)}, u32[]{:S(2)}, u32[]{:S(2)}) %collective-permute-start.4) | collective-permute-done | bytes 983072 | tf_op jit(solution)/shard_map/ppermute | solution.py:333
  55.7 2.4 %shard_map.68 = (bf16[512,3072]{1,0:T(8,128)(2,1)S(1)}, bf16[512,384]{1,0:T(8,128)(2,1)S(1)}, f32[384,512]{1,0:T(8,128)S(1)}, f32[384,512]{1,0:T(8,128)S(1)}) custom-call(s32[6]{0:T(128)S(1)} %concatenate.6.info, bf16[4,32,3840]{2,1,0:T(8,128)(2,1)S(1)} %get-tuple-element.70.refs_0_, bf16[4,32,3840]{2,1,0:T(8,128)(2,1)S(1)} %collective-permute-done.3.refs_1_, ...), custom_call_target="tpu_custom_call" | custom-call | flops 1207959552 | bytes 12582912 | tf_op jit(solution)/shard_map/pallas_call | solution.py:162
  58.6 2.9 %shard_map.69 = (f32[384,512]{1,0:T(8,128)S(1)}, f32[8,512]{1,0:T(8,128)S(1)}) custom-call(s32[6]{0:T(128)S(1)} %concatenate.6.info, bf16[8,192,384]{2,1,0:T(8,128)(2,1)S(1)} %constant_dynamic-update-slice_fusion.own, bf16[8,192,384]{2,1,0:T(8,128)(2,1)S(1)} %collective-permute-done.11.other, bf16[512,3072]{1,0:T(8,128)(2,1)S(1)} %get-tuple-element.76.context, ...), custom_call_target="tpu_custom_call" | custom-call | flops 1207959552 | bytes 12582912 | tf_op jit(solution)/shard_map/pallas_call | solution.py:198
  61.5 15.2 %all_to_all.10.stats = f32[16,8,512]{2,1,0:T(8,128)S(1)} all-to-all(f32[16,8,512]{2,1,0:T(8,128)S(1)} %broadcast_in_dim.5), channel_id=1, replica_groups=mesh['x'=4,'zh'=2,'y'=4,'zl'=4,'c'=2] {'x','y'}, dimensions={0} | all-to-all | bytes 524288 | tf_op jit(solution)/shard_map/all_to_all | solution.py:357
  76.7 2.3 %shard_map.70 = (bf16[384,512]{1,0:T(8,128)(2,1)S(1)}, bf16[8,192,384]{2,1,0:T(8,128)(2,1)S(1)}) custom-call(s32[6]{0:T(128)S(1)} %concatenate.6.info, f32[16,8,512]{2,1,0:T(8,128)S(1)} %all_to_all.10.stats, f32[384,512]{1,0:T(8,128)S(1)} %get-tuple-element.81.s, f32[384,512]{1,0:T(8,128)S(1)} %get-tuple-element.78.u_in.u, ...), custom_call_target="tpu_custom_call" | custom-call | flops 603979776 | bytes 12582912 | tf_op jit(solution)/shard_map/pallas_call | solution.py:244
  79.1 2.8 %collective-permute-done.12.received = bf16[8,192,384]{2,1,0:T(8,128)(2,1)S(1)} collective-permute-done((bf16[8,192,384]{2,1,0:T(8,128)(2,1)S(1)}, bf16[8,192,384]{2,1,0:T(8,128)(2,1)S(1)}, u32[]{:S(2)}, u32[]{:S(2)}) %collective-permute-start.12) | collective-permute-done | bytes 1179680 | tf_op jit(solution)/shard_map/ppermute | solution.py:317
  81.9 1.6 %shard_map.71 = (bf16[192,384]{1,0:T(8,128)(2,1)S(1)}, bf16[192,384]{1,0:T(8,128)(2,1)S(1)}, bf16[192,384]{1,0:T(8,128)(2,1)S(1)}, bf16[192,384]{1,0:T(8,128)(2,...) custom-call(s32[6]{0:T(128)S(1)} %concatenate.6.info, ...), custom_call_target="tpu_custom_call" | custom-call | flops 603979776 | bytes 12582912 | tf_op jit(solution)/shard_map/pallas_call | solution.py:271
  83.5 1.1 %collective-permute-start.15 = (bf16[192,384]{1,0:T(8,128)(2,1)S(1)}, bf16[192,384]{1,0:T(8,128)(2,1)S(1)}, u32[]{:S(2)}, u32[]{:S(2)}) collective-permute-start(bf16[192,384]{1,0:T(8,128)(2,1)S(1)} %get-tuple-element.87), channel_id=1, source_target_pairs={{0,2},{2,4},{4,6},{6,32},{32,34},{34,36},{36,38},{38,0},{1,3},{3,5... | collective-permute-start | bytes 442376 | tf_op jit(solution)/shard_map/ppermute | solution.py:33
  84.6 1.8 %collective-permute-start.16 = (bf16[192,384]{1,0:T(8,128)(2,1)S(1)}, bf16[192,384]{1,0:T(8,128)(2,1)S(1)}, u32[]{:S(2)}, u32[]{:S(2)}) collective-permute-start(bf16[192,384]{1,0:T(8,128)(2,1)S(1)} %get-tuple-element.88), channel_id=1, source_target_pairs={{0,38},{2,0},{4,2},{6,4},{32,6},{34,32},{36,34},{38,36},{1,39},{3,... | collective-permute-start | bytes 442376 | tf_op jit(solution)/shard_map/ppermute | solution.py:33
  86.4 2.5 %collective-permute-start.17 = (bf16[96,384]{1,0:T(8,128)(2,1)S(1)}, bf16[96,384]{1,0:T(8,128)(2,1)S(1)}, u32[]{:S(2)}, u32[]{:S(2)}) collective-permute-start(bf16[96,384]{1,0:T(8,128)(2,1)S(1)} %get-tuple-element.89), channel_id=1, source_target_pairs={{0,4},{2,6},{4,32},{6,34},{32,36},{34,38},{36,0},{38,2},{1,5},{3,7... | collective-permute-start | bytes 221192 | tf_op jit(solution)/shard_map/ppermute | solution.py:33
  88.9 2.1 %collective-permute-start.18 = (bf16[96,384]{1,0:T(8,128)(2,1)S(1)}, bf16[96,384]{1,0:T(8,128)(2,1)S(1)}, u32[]{:S(2)}, u32[]{:S(2)}) collective-permute-start(bf16[96,384]{1,0:T(8,128)(2,1)S(1)} %get-tuple-element.90), channel_id=1, source_target_pairs={{0,36},{2,38},{4,0},{6,2},{32,4},{34,6},{36,32},{38,34},{1,37},{3,... | collective-permute-start | bytes 221192 | tf_op jit(solution)/shard_map/ppermute | solution.py:33
  91.0 1.1 %collective-permute-start.13 = (bf16[192,384]{1,0:T(8,128)(2,1)S(1)}, bf16[192,384]{1,0:T(8,128)(2,1)S(1)}, u32[]{:S(2)}, u32[]{:S(2)}) collective-permute-start(bf16[192,384]{1,0:T(8,128)(2,1)S(1)} %get-tuple-element.85), channel_id=1, source_target_pairs={{0,2},{2,4},{4,6},{6,32},{32,34},{34,36},{36,38},{38,0},{1,3},{3,5... | collective-permute-start | bytes 442376 | tf_op jit(solution)/shard_map/ppermute | solution.py:33
  92.1 3.3 %collective-permute-done.17.four_up = bf16[96,384]{1,0:T(8,128)(2,1)S(1)} collective-permute-done((bf16[96,384]{1,0:T(8,128)(2,1)S(1)}, bf16[96,384]{1,0:T(8,128)(2,1)S(1)}, u32[]{:S(2)}, u32[]{:S(2)}) %collective-permute-start.17) | collective-permute-done | bytes 73760 | tf_op jit(solution)/shard_map/ppermute | solution.py:33
  95.4 3.3 %collective-permute-start.14 = (bf16[192,384]{1,0:T(8,128)(2,1)S(1)}, bf16[192,384]{1,0:T(8,128)(2,1)S(1)}, u32[]{:S(2)}, u32[]{:S(2)}) collective-permute-start(bf16[192,384]{1,0:T(8,128)(2,1)S(1)} %get-tuple-element.86), channel_id=1, source_target_pairs={{0,38},{2,0},{4,2},{6,4},{32,6},{34,32},{36,34},{38,36},{1,39},{3,... | collective-permute-start | bytes 442376 | tf_op jit(solution)/shard_map/ppermute | solution.py:33
  98.9 4.1 %collective-permute-start.20 = (bf16[192,384]{1,0:T(8,128)(2,1)S(1)}, bf16[192,384]{1,0:T(8,128)(2,1)S(1)}, u32[]{:S(2)}, u32[]{:S(2)}) collective-permute-start(bf16[192,384]{1,0:T(8,128)(2,1)S(1)} %get-tuple-element.92), channel_id=1, source_target_pairs={{0,36},{2,38},{4,0},{6,2},{32,4},{34,6},{36,32},{38,34},{1,37},{3,... | collective-permute-start | bytes 442376 | tf_op jit(solution)/shard_map/ppermute | solution.py:33
  103.0 5.5 %collective-permute-done.19.up = bf16[192,384]{1,0:T(8,128)(2,1)S(1)} collective-permute-done((bf16[192,384]{1,0:T(8,128)(2,1)S(1)}, bf16[192,384]{1,0:T(8,128)(2,1)S(1)}, u32[]{:S(2)}, u32[]{:S(2)}) %collective-permute-start.19) | collective-permute-done | bytes 147488 | tf_op jit(solution)/shard_map/ppermute | solution.py:33
  108.5 1.5 %shard_map.73 = f32[192,384]{1,0:T(8,128)} custom-call(s32[6]{0:T(128)S(1)} %concatenate.6.info, f32[3,192,384]{2,1,0:T(8,128)S(1)} %get-tuple-element.84.kept, bf16[192,384]{1,0:T(8,128)(2,1)S(1)} %collective-permute-done.13.a, bf16[192,384]{1,0:T(8,128)(2,1)S(1)} %collective-permute-done.14.b, bf16[192,384]{1,0:T(8,128)(2,1)S(1)} %collective-permute-done.19.up, ...), custom_call_target="tpu_custom_call" | custom-call | flops 1474560 | bytes 1474560 | tf_op jit(solution)/shard_map/pallas_call | solution.py:290
  (39 shorter events, 6.6 us)
Async XLA Ops:
  0.0 19.2 %copy-start.2 = (bf16[192,384]{1,0:T(8,128)(2,1)S(1)}, bf16[192,384]{1,0:T(8,128)(2,1)}, u32[]{:S(2)}) copy-start(bf16[192,384]{1,0:T(8,128)(2,1)} %param.8) | copy-start | bytes 442372
  0.0 13.3 %all-to-all-start = ((bf16[8,32,384]{2,1,0:T(8,128)(2,1)}), bf16[8,32,384]{2,1,0:T(8,128)(2,1)S(1)}, u32[]{:S(2)}, u32[]{:S(2)}) async-start(bf16[8,32,384]{2,1,0:T(8,128)(2,1)} %bitcast.14), calls=%async_computation | async-start | bytes 393216 | tf_op jit(solution)/shard_map/all_to_all | solution.py:342
  6.1 13.1 %collective-permute-start.8 = (bf16[192,384]{1,0:T(8,128)(2,1)}, bf16[192,384]{1,0:T(8,128)(2,1)S(1)}, u32[]{:S(2)}, u32[]{:S(2)}) collective-permute-start(bf16[192,384]{1,0:T(8,128)(2,1)} %param.8), channel_id=1, source_target_pairs={{0,38},{2,0},{4,2},{6,4},{32,6},{34,32},{36,34},{38,36},{1,39},{3,... | collective-permute-start | bytes 442376 | tf_op jit(solution)/shard_map/ppermute | solution.py:33
  6.2 13.0 %collective-permute-start.6 = (bf16[192,384]{1,0:T(8,128)(2,1)}, bf16[192,384]{1,0:T(8,128)(2,1)S(1)}, u32[]{:S(2)}, u32[]{:S(2)}) collective-permute-start(bf16[192,384]{1,0:T(8,128)(2,1)} %param.8), channel_id=1, source_target_pairs={{0,2},{2,4},{4,6},{6,32},{32,34},{34,36},{36,38},{38,0},{1,3},{3,5... | collective-permute-start | bytes 442376 | tf_op jit(solution)/shard_map/ppermute | solution.py:33
  9.7 1.0 copy-start
  10.7 1.0 copy-start.1
  13.5 11.3 %collective-permute-start = (bf16[64,3072]{1,0:T(8,128)(2,1)S(1)}, bf16[64,3072]{1,0:T(8,128)(2,1)S(1)}, u32[]{:S(2)}, u32[]{:S(2)}) collective-permute-start(bf16[64,3072]{1,0:T(8,128)(2,1)S(1)} %get-tuple-element.54), channel_id=1, source_target_pairs={{0,64},{1,9},{8,72},{9,17},{16,80},{17,25},{24,88},{25,1},{64,128}... | collective-permute-start | bytes 1179656 | tf_op jit(solution)/shard_map/ppermute | solution.py:333
  15.0 12.7 %collective-permute-start.1 = (bf16[64,3072]{1,0:T(8,128)(2,1)S(1)}, bf16[64,3072]{1,0:T(8,128)(2,1)S(1)}, u32[]{:S(2)}, u32[]{:S(2)}) collective-permute-start(bf16[64,3072]{1,0:T(8,128)(2,1)S(1)} %get-tuple-element.55), channel_id=1, source_target_pairs={{0,128},{1,17},{8,136},{9,25},{16,144},{17,1},{24,152},{25,9},{64,... | collective-permute-start | bytes 1179656 | tf_op jit(solution)/shard_map/ppermute | solution.py:333
  17.8 10.0 %collective-permute-start.2 = (bf16[64,3072]{1,0:T(8,128)(2,1)S(1)}, bf16[64,3072]{1,0:T(8,128)(2,1)S(1)}, u32[]{:S(2)}, u32[]{:S(2)}) collective-permute-start(bf16[64,3072]{1,0:T(8,128)(2,1)S(1)} %get-tuple-element.56), channel_id=1, source_target_pairs={{0,192},{1,25},{8,200},{9,1},{16,208},{17,9},{24,216},{25,17},{64,... | collective-permute-start | bytes 1179656 | tf_op jit(solution)/shard_map/ppermute | solution.py:333
  19.3 16.0 %collective-permute-start.9 = (bf16[2,192,384]{2,1,0:T(8,128)(2,1)S(1)}, bf16[2,192,384]{2,1,0:T(8,128)(2,1)S(1)}, u32[]{:S(2)}, u32[]{:S(2)}) collective-permute-start(bf16[2,192,384]{2,1,0:T(8,128)(2,1)S(1)} %get-tuple-element.67), channel_id=1, source_target_pairs={{0,36},{2,38},{4,0},{6,2},{32,4},{34,6},{36,32},{38,34},{1,37},{3,... | collective-permute-start | bytes 884744 | tf_op jit(solution)/shard_map/ppermute | solution.py:33
  24.8 14.8 %collective-permute-start.7 = (bf16[2,192,384]{2,1,0:T(8,128)(2,1)S(1)}, bf16[2,192,384]{2,1,0:T(8,128)(2,1)S(1)}, u32[]{:S(2)}, u32[]{:S(2)}) collective-permute-start(bf16[2,192,384]{2,1,0:T(8,128)(2,1)S(1)} %get-tuple-element.66), channel_id=1, source_target_pairs={{0,4},{2,6},{4,32},{6,34},{32,36},{34,38},{36,0},{38,2},{1,5},{3,7... | collective-permute-start | bytes 884744 | tf_op jit(solution)/shard_map/ppermute | solution.py:33
  28.5 15.4 %collective-permute-start.3 = (bf16[4,32,3840]{2,1,0:T(8,128)(2,1)S(1)}, bf16[4,32,3840]{2,1,0:T(8,128)(2,1)S(1)}, u32[]{:S(2)}, u32[]{:S(2)}) collective-permute-start(bf16[4,32,3840]{2,1,0:T(8,128)(2,1)S(1)} %get-tuple-element.62), channel_id=1, source_target_pairs={{0,8},{1,65},{8,16},{9,73},{16,24},{17,81},{24,0},{25,89},{64,72},... | collective-permute-start | bytes 2949128 | tf_op jit(solution)/shard_map/ppermute | solution.py:333
  30.2 25.5 %collective-permute-start.4 = (bf16[4,32,3840]{2,1,0:T(8,128)(2,1)S(1)}, bf16[4,32,3840]{2,1,0:T(8,128)(2,1)S(1)}, u32[]{:S(2)}, u32[]{:S(2)}) collective-permute-start(bf16[4,32,3840]{2,1,0:T(8,128)(2,1)S(1)} %get-tuple-element.63), channel_id=1, source_target_pairs={{0,16},{1,129},{8,24},{9,137},{16,0},{17,145},{24,8},{25,153},{64,... | collective-permute-start | bytes 2949128 | tf_op jit(solution)/shard_map/ppermute | solution.py:333
  33.1 22.6 %collective-permute-start.5 = (bf16[4,32,3840]{2,1,0:T(8,128)(2,1)S(1)}, bf16[4,32,3840]{2,1,0:T(8,128)(2,1)S(1)}, u32[]{:S(2)}, u32[]{:S(2)}) collective-permute-start(bf16[4,32,3840]{2,1,0:T(8,128)(2,1)S(1)} %get-tuple-element.64), channel_id=1, source_target_pairs={{0,24},{1,193},{8,0},{9,201},{16,8},{17,209},{24,16},{25,217},{64,... | collective-permute-start | bytes 2949128 | tf_op jit(solution)/shard_map/ppermute | solution.py:333
  35.3 7.6 %collective-permute-start.10 = (bf16[192,384]{1,0:T(8,128)(2,1)S(1)}, bf16[192,384]{1,0:T(8,128)(2,1)S(1)}, u32[]{:S(2)}, u32[]{:S(2)}) collective-permute-start(bf16[192,384]{1,0:T(8,128)(2,1)S(1)} %slice_bitcast_fusion), channel_id=1, source_target_pairs={{0,38},{2,0},{4,2},{6,4},{32,6},{34,32},{36,34},{38,36},{1,39},{3,... | collective-permute-start | bytes 442376 | tf_op jit(solution)/shard_map/ppermute | solution.py:33
  55.7 2.8 %collective-permute-start.11 = (bf16[8,192,384]{2,1,0:T(8,128)(2,1)S(1)}, bf16[8,192,384]{2,1,0:T(8,128)(2,1)S(1)}, u32[]{:S(2)}, u32[]{:S(2)}) collective-permute-start(bf16[8,192,384]{2,1,0:T(8,128)(2,1)S(1)} %constant_dynamic-update-slice_fusion.own), channel_id=1, source_target_pairs={{0,1},{1,0},{2,3},{3,2},{4,5},{5,4},{6,7},{7,6},{8,9},{9,8},{10,11... | collective-permute-start | bytes 3538952 | tf_op jit(solution)/shard_map/ppermute | solution.py:317
  79.0 2.9 %collective-permute-start.12 = (bf16[8,192,384]{2,1,0:T(8,128)(2,1)S(1)}, bf16[8,192,384]{2,1,0:T(8,128)(2,1)S(1)}, u32[]{:S(2)}, u32[]{:S(2)}) collective-permute-start(bf16[8,192,384]{2,1,0:T(8,128)(2,1)S(1)} %get-tuple-element.83), channel_id=1, source_target_pairs={{0,1},{1,0},{2,3},{3,2},{4,5},{5,4},{6,7},{7,6},{8,9},{9,8},{10,11... | collective-permute-start | bytes 3538952 | tf_op jit(solution)/shard_map/ppermute | solution.py:317
  83.5 15.2 %collective-permute-start.15 = (bf16[192,384]{1,0:T(8,128)(2,1)S(1)}, bf16[192,384]{1,0:T(8,128)(2,1)S(1)}, u32[]{:S(2)}, u32[]{:S(2)}) collective-permute-start(bf16[192,384]{1,0:T(8,128)(2,1)S(1)} %get-tuple-element.87), channel_id=1, source_target_pairs={{0,2},{2,4},{4,6},{6,32},{32,34},{34,36},{36,38},{38,0},{1,3},{3,5... | collective-permute-start | bytes 442376 | tf_op jit(solution)/shard_map/ppermute | solution.py:33
  84.6 14.1 %collective-permute-start.16 = (bf16[192,384]{1,0:T(8,128)(2,1)S(1)}, bf16[192,384]{1,0:T(8,128)(2,1)S(1)}, u32[]{:S(2)}, u32[]{:S(2)}) collective-permute-start(bf16[192,384]{1,0:T(8,128)(2,1)S(1)} %get-tuple-element.88), channel_id=1, source_target_pairs={{0,38},{2,0},{4,2},{6,4},{32,6},{34,32},{36,34},{38,36},{1,39},{3,... | collective-permute-start | bytes 442376 | tf_op jit(solution)/shard_map/ppermute | solution.py:33
  86.4 9.0 %collective-permute-start.17 = (bf16[96,384]{1,0:T(8,128)(2,1)S(1)}, bf16[96,384]{1,0:T(8,128)(2,1)S(1)}, u32[]{:S(2)}, u32[]{:S(2)}) collective-permute-start(bf16[96,384]{1,0:T(8,128)(2,1)S(1)} %get-tuple-element.89), channel_id=1, source_target_pairs={{0,4},{2,6},{4,32},{6,34},{32,36},{34,38},{36,0},{38,2},{1,5},{3,7... | collective-permute-start | bytes 221192 | tf_op jit(solution)/shard_map/ppermute | solution.py:33
  88.9 9.8 %collective-permute-start.18 = (bf16[96,384]{1,0:T(8,128)(2,1)S(1)}, bf16[96,384]{1,0:T(8,128)(2,1)S(1)}, u32[]{:S(2)}, u32[]{:S(2)}) collective-permute-start(bf16[96,384]{1,0:T(8,128)(2,1)S(1)} %get-tuple-element.90), channel_id=1, source_target_pairs={{0,36},{2,38},{4,0},{6,2},{32,4},{34,6},{36,32},{38,34},{1,37},{3,... | collective-permute-start | bytes 221192 | tf_op jit(solution)/shard_map/ppermute | solution.py:33
  91.0 12.0 %collective-permute-start.13 = (bf16[192,384]{1,0:T(8,128)(2,1)S(1)}, bf16[192,384]{1,0:T(8,128)(2,1)S(1)}, u32[]{:S(2)}, u32[]{:S(2)}) collective-permute-start(bf16[192,384]{1,0:T(8,128)(2,1)S(1)} %get-tuple-element.85), channel_id=1, source_target_pairs={{0,2},{2,4},{4,6},{6,32},{32,34},{34,36},{36,38},{38,0},{1,3},{3,5... | collective-permute-start | bytes 442376 | tf_op jit(solution)/shard_map/ppermute | solution.py:33
  95.4 7.6 %collective-permute-start.14 = (bf16[192,384]{1,0:T(8,128)(2,1)S(1)}, bf16[192,384]{1,0:T(8,128)(2,1)S(1)}, u32[]{:S(2)}, u32[]{:S(2)}) collective-permute-start(bf16[192,384]{1,0:T(8,128)(2,1)S(1)} %get-tuple-element.86), channel_id=1, source_target_pairs={{0,38},{2,0},{4,2},{6,4},{32,6},{34,32},{36,34},{38,36},{1,39},{3,... | collective-permute-start | bytes 442376 | tf_op jit(solution)/shard_map/ppermute | solution.py:33
  98.8 9.7 %collective-permute-start.19 = (bf16[192,384]{1,0:T(8,128)(2,1)S(1)}, bf16[192,384]{1,0:T(8,128)(2,1)S(1)}, u32[]{:S(2)}, u32[]{:S(2)}) collective-permute-start(bf16[192,384]{1,0:T(8,128)(2,1)S(1)} %get-tuple-element.91), channel_id=1, source_target_pairs={{0,4},{2,6},{4,32},{6,34},{32,36},{34,38},{36,0},{38,2},{1,5},{3,7... | collective-permute-start | bytes 442376 | tf_op jit(solution)/shard_map/ppermute | solution.py:33
  98.9 9.6 %collective-permute-start.20 = (bf16[192,384]{1,0:T(8,128)(2,1)S(1)}, bf16[192,384]{1,0:T(8,128)(2,1)S(1)}, u32[]{:S(2)}, u32[]{:S(2)}) collective-permute-start(bf16[192,384]{1,0:T(8,128)(2,1)S(1)} %get-tuple-element.92), channel_id=1, source_target_pairs={{0,36},{2,38},{4,0},{6,2},{32,4},{34,6},{36,32},{38,34},{1,37},{3,... | collective-permute-start | bytes 442376 | tf_op jit(solution)/shard_map/ppermute | solution.py:33

commit v4 on v3

--- a/solution.py
+++ b/solution.py
@@ -323,7 +323,7 @@
 
 def leg(blocks, axes):
     out = [blocks[0]]
-    for k in range(1, 4):
+    for k in (1, 3, 2):
         pairs = []
         for x in range(4):
             for y in range(4):
@@ -343,6 +343,7 @@
     rows, rest, gain = lax.optimization_barrier((rows, rest, gain))
 
     came = lax.optimization_barrier(leg(first_leg(rows, rest), "xy"))
+    came = [came[n] for n in (0, 1, 3, 2)]
     behind, ahead = shift(out_proj, Z, 1), shift(out_proj, Z, -1)
     two, ahead2 = after(jnp.stack([out_proj, behind]), rows), after(jnp.stack([out_proj, ahead]), rows)
     behind2, ahead2 = shift(two, Z, 2), shift(ahead2, Z, -2)
@@ -351,6 +352,7 @@
 
     probe = make_probe(after(info, *came))
     *pieces, probe, own = lax.optimization_barrier((*leg(second_leg(info, came), "yx"), probe, own))
+    pieces = [pieces[n] for n in (0, 1, 3, 2)]
     other = swap(own)
     rows, res, u, w = tangent_of(info, pieces, probe, gain)
     s, stats = stream_of(info, own, other, rows, res, u, w)
@@ -358,9 +360,9 @@
     grad, send = away(info, stats, s, u, w, rows)
     near_up, near_down, three_up, three_down, four_up, four_down, kept = home(info, grad, rows, swap(send))
 
-    near_up, near_down = shift(near_up, Z, 1), shift(near_down, Z, -1)
     three_up, three_down = shift(three_up, Z, 1), shift(three_down, Z, -1)
     four_up, four_down = shift(four_up, Z, 2), shift(four_down, Z, -2)
+    near_up, near_down = shift(near_up, Z, 1), shift(near_down, Z, -1)
     up, down = between(kept, three_up, three_down, four_up, four_down)
     up, down = shift(up, Z, 2), shift(down, Z, -2)
     return last(info, kept, near_up, near_down, up, down)

time: 110 us -> 109 us (level)
  blocking collectives: 15.2 us -> 13.7 us
  starting transfers between devices: 43.5 us -> 42.3 us
  waiting for transfers between devices: 31.2 us -> 32.4 us
    all_to_all x1, blocking collectives: 15.2 us -> 13.7 us  [on_device(): lax.all_to_all(jnp.broadcast_to(stats[None], (16, 8, TOK)), XY, 0, 0, til...]
    ppermute x6, starting transfers between devices: 11.6 us -> 10.4 us  [leg(): out.append(lax.ppermute(blocks[k], XYC, pairs))]
    ppermute x6, waiting for transfers between devices: 15.6 us -> 16.8 us  [leg(): out.append(lax.ppermute(blocks[k], XYC, pairs))]
  transfers between devices with their start and end apart: 22 -> 22, of which waited for: 10 -> 12; matrix products, arithmetic and copies ran while one was open for 2% -> 2% of each run, Pallas kernels for 7% -> 7%
where the time goes in v4:
time: 109 us; the launch traced here: 108 us
  starting transfers between devices  42.3 us (39%)
  waiting for transfers between devices  32.4 us (30%)
  Pallas kernels  16.1 us (15%)
  blocking collectives  13.7 us (13%)
  local copies, waits for them, and re-layouts  3.76 us (3%)
    ppermute x13, starting transfers between devices, shift(): return lax.ppermute(v, axis, [(s, (s + k) % n) for s in range(n)])  25.7 us
    ppermute x6, waiting for transfers between devices, leg(): out.append(lax.ppermute(blocks[k], XYC, pairs))  16.8 us
    all_to_all x1, blocking collectives, on_device(): lax.all_to_all(jnp.broadcast_to(stats[None], (16, 8, TOK)), XY, 0, 0, til...  13.7 us
    ppermute x13, waiting for transfers between devices, shift(): return lax.ppermute(v, axis, [(s, (s + k) % n) for s in range(n)])  11.9 us
    ppermute x6, starting transfers between devices, leg(): out.append(lax.ppermute(blocks[k], XYC, pairs))  10.4 us
    all_to_all x1, starting transfers between devices, on_device(): rows = lax.all_to_all(context.reshape(8, OWN, F), T, 0, 0, tiled=True)  6.14 us
    ppermute x2, waiting for transfers between devices, swap(): return lax.ppermute(v, 'c', [(0, 1), (1, 0)])  3.23 us
    pallas_call x1, Pallas kernels, make_probe(): pl.pallas_call(probe_kernel, grid=(8,), in_specs=[pl.BlockSpec(memory_spa...  3.21 us
  transfers between devices with their start and end apart: 22, of which 12 were waited for; matrix products, arithmetic and copies ran while one was open for 2% of the time, Pallas kernels for 7%

profile of v4, /device:TPU:32, one launch (start us, length us, event | category | flops | bytes accessed | tf_op | source)
XLA Modules:
  0.0 108.5 jit_solution(17618377443199858832)
XLA Ops:
  0.0 6.1 %all-to-all-start = ((bf16[8,32,384]{2,1,0:T(8,128)(2,1)}), bf16[8,32,384]{2,1,0:T(8,128)(2,1)S(1)}, u32[]{:S(2)}, u32[]{:S(2)}) async-start(bf16[8,32,384]{2,1,0:T(8,128)(2,1)} %bitcast.14), calls=%async_computation | async-start | bytes 393216 | tf_op jit(solution)/shard_map/all_to_all | solution.py:342
  6.2 2.0 %collective-permute-start.6 = (bf16[192,384]{1,0:T(8,128)(2,1)}, bf16[192,384]{1,0:T(8,128)(2,1)S(1)}, u32[]{:S(2)}, u32[]{:S(2)}) collective-permute-start(bf16[192,384]{1,0:T(8,128)(2,1)} %param.8), channel_id=1, source_target_pairs={{0,2},{2,4},{4,6},{6,32},{32,34},{34,36},{36,38},{38,0},{1,3},{3,5... | collective-permute-start | bytes 442376 | tf_op jit(solution)/shard_map/ppermute | solution.py:33
  11.7 1.2 %shard_map.64 = (bf16[4,32,3072]{2,1,0:T(8,128)(2,1)S(1)}, f32[384,1]{1,0:T(8,128)S(1)}) custom-call(s32[6]{0:T(128)S(1)} %concatenate.6.info, bf16[32,6144]{1,0:T(8,128)(2,1)S(1)} %copy-done, bf16[32,6144]{1,0:T(8,128)(2,1)S(1)} %copy-done.1, f32[32,192]{1,0:T(8,128)S(1)} %reshape.8.gains), custom_call_target="tpu_custom_call" | custom-call | bytes 1572864 | tf_op jit(solution)/shard_map/pallas_call | solution.py:96
  13.5 1.6 %collective-permute-start = (bf16[64,3072]{1,0:T(8,128)(2,1)S(1)}, bf16[64,3072]{1,0:T(8,128)(2,1)S(1)}, u32[]{:S(2)}, u32[]{:S(2)}) collective-permute-start(bf16[64,3072]{1,0:T(8,128)(2,1)S(1)} %get-tuple-element.54), channel_id=1, source_target_pairs={{0,64},{1,9},{8,72},{9,17},{16,80},{17,25},{24,88},{25,1},{64,128}... | collective-permute-start | bytes 1179656 | tf_op jit(solution)/shard_map/ppermute | solution.py:333
  15.0 1.7 %collective-permute-start.1 = (bf16[64,3072]{1,0:T(8,128)(2,1)S(1)}, bf16[64,3072]{1,0:T(8,128)(2,1)S(1)}, u32[]{:S(2)}, u32[]{:S(2)}) collective-permute-start(bf16[64,3072]{1,0:T(8,128)(2,1)S(1)} %get-tuple-element.55), channel_id=1, source_target_pairs={{0,192},{1,25},{8,200},{9,1},{16,208},{17,9},{24,216},{25,17},{64,... | collective-permute-start | bytes 1179656 | tf_op jit(solution)/shard_map/ppermute | solution.py:333
  16.8 1.8 %collective-permute-start.2 = (bf16[64,3072]{1,0:T(8,128)(2,1)S(1)}, bf16[64,3072]{1,0:T(8,128)(2,1)S(1)}, u32[]{:S(2)}, u32[]{:S(2)}) collective-permute-start(bf16[64,3072]{1,0:T(8,128)(2,1)S(1)} %get-tuple-element.56), channel_id=1, source_target_pairs={{0,128},{1,17},{8,136},{9,25},{16,144},{17,1},{24,152},{25,9},{64,... | collective-permute-start | bytes 1179656 | tf_op jit(solution)/shard_map/ppermute | solution.py:333
  18.7 5.5 %collective-permute-start.9 = (bf16[2,192,384]{2,1,0:T(8,128)(2,1)S(1)}, bf16[2,192,384]{2,1,0:T(8,128)(2,1)S(1)}, u32[]{:S(2)}, u32[]{:S(2)}) collective-permute-start(bf16[2,192,384]{2,1,0:T(8,128)(2,1)S(1)} %get-tuple-element.67), channel_id=1, source_target_pairs={{0,36},{2,38},{4,0},{6,2},{32,4},{34,6},{36,32},{38,34},{1,37},{3,... | collective-permute-start | bytes 884744 | tf_op jit(solution)/shard_map/ppermute | solution.py:33
  24.2 2.1 %collective-permute-done.1.refs_3_ = bf16[64,3072]{1,0:T(8,128)(2,1)S(1)} collective-permute-done((bf16[64,3072]{1,0:T(8,128)(2,1)S(1)}, bf16[64,3072]{1,0:T(8,128)(2,1)S(1)}, u32[]{:S(2)}, u32[]{:S(2)}) %collective-permute-start.1) | collective-permute-done | bytes 393248 | tf_op jit(solution)/shard_map/ppermute | solution.py:333
  26.3 1.4 %collective-permute-done.2.refs_2_ = bf16[64,3072]{1,0:T(8,128)(2,1)S(1)} collective-permute-done((bf16[64,3072]{1,0:T(8,128)(2,1)S(1)}, bf16[64,3072]{1,0:T(8,128)(2,1)S(1)}, u32[]{:S(2)}, u32[]{:S(2)}) %collective-permute-start.2) | collective-permute-done | bytes 393248 | tf_op jit(solution)/shard_map/ppermute | solution.py:333
  28.5 1.7 %collective-permute-start.3 = (bf16[4,32,3840]{2,1,0:T(8,128)(2,1)S(1)}, bf16[4,32,3840]{2,1,0:T(8,128)(2,1)S(1)}, u32[]{:S(2)}, u32[]{:S(2)}) collective-permute-start(bf16[4,32,3840]{2,1,0:T(8,128)(2,1)S(1)} %get-tuple-element.62), channel_id=1, source_target_pairs={{0,8},{1,65},{8,16},{9,73},{16,24},{17,81},{24,0},{25,89},{64,72},... | collective-permute-start | bytes 2949128 | tf_op jit(solution)/shard_map/ppermute | solution.py:333
  30.2 1.7 %collective-permute-start.4 = (bf16[4,32,3840]{2,1,0:T(8,128)(2,1)S(1)}, bf16[4,32,3840]{2,1,0:T(8,128)(2,1)S(1)}, u32[]{:S(2)}, u32[]{:S(2)}) collective-permute-start(bf16[4,32,3840]{2,1,0:T(8,128)(2,1)S(1)} %get-tuple-element.63), channel_id=1, source_target_pairs={{0,24},{1,193},{8,0},{9,201},{16,8},{17,209},{24,16},{25,217},{64,... | collective-permute-start | bytes 2949128 | tf_op jit(solution)/shard_map/ppermute | solution.py:333
  31.9 2.0 %collective-permute-start.5 = (bf16[4,32,3840]{2,1,0:T(8,128)(2,1)S(1)}, bf16[4,32,3840]{2,1,0:T(8,128)(2,1)S(1)}, u32[]{:S(2)}, u32[]{:S(2)}) collective-permute-start(bf16[4,32,3840]{2,1,0:T(8,128)(2,1)S(1)} %get-tuple-element.64), channel_id=1, source_target_pairs={{0,16},{1,129},{8,24},{9,137},{16,0},{17,145},{24,8},{25,153},{64,... | collective-permute-start | bytes 2949128 | tf_op jit(solution)/shard_map/ppermute | solution.py:333
  34.7 2.0 %collective-permute-start.10 = (bf16[192,384]{1,0:T(8,128)(2,1)S(1)}, bf16[192,384]{1,0:T(8,128)(2,1)S(1)}, u32[]{:S(2)}, u32[]{:S(2)}) collective-permute-start(bf16[192,384]{1,0:T(8,128)(2,1)S(1)} %slice_bitcast_fusion), channel_id=1, source_target_pairs={{0,38},{2,0},{4,2},{6,4},{32,6},{34,32},{36,34},{38,36},{1,39},{3,... | collective-permute-start | bytes 442376 | tf_op jit(solution)/shard_map/ppermute | solution.py:33
  36.7 2.3 %collective-permute-done.7 = bf16[2,192,384]{2,1,0:T(8,128)(2,1)S(1)} collective-permute-done((bf16[2,192,384]{2,1,0:T(8,128)(2,1)S(1)}, bf16[2,192,384]{2,1,0:T(8,128)(2,1)S(1)}, u32[]{:S(2)}, u32[]{:S(2)}) %collective-permute-start.7) | collective-permute-done | bytes 294944 | tf_op jit(solution)/shard_map/ppermute | solution.py:33
  39.0 3.2 %shard_map.67.refs_4_ = bf16[384,3072]{1,0:T(8,128)(2,1)S(1)} custom-call(s32[6]{0:T(128)S(1)} %concatenate.6.info), custom_call_target="tpu_custom_call" | custom-call | flops 16515072 | bytes 2359296 | tf_op jit(solution)/shard_map/pallas_call | solution.py:55
  42.4 1.5 %collective-permute-done.3.refs_1_ = bf16[4,32,3840]{2,1,0:T(8,128)(2,1)S(1)} collective-permute-done((bf16[4,32,3840]{2,1,0:T(8,128)(2,1)S(1)}, bf16[4,32,3840]{2,1,0:T(8,128)(2,1)S(1)}, u32[]{:S(2)}, u32[]{:S(2)}) %collective-permute-start.3) | collective-permute-done | bytes 983072 | tf_op jit(solution)/shard_map/ppermute | solution.py:333
  44.3 11.4 %collective-permute-done.5.refs_2_ = bf16[4,32,3840]{2,1,0:T(8,128)(2,1)S(1)} collective-permute-done((bf16[4,32,3840]{2,1,0:T(8,128)(2,1)S(1)}, bf16[4,32,3840]{2,1,0:T(8,128)(2,1)S(1)}, u32[]{:S(2)}, u32[]{:S(2)}) %collective-permute-start.5) | collective-permute-done | bytes 983072 | tf_op jit(solution)/shard_map/ppermute | solution.py:333
  55.7 2.4 %shard_map.68 = (bf16[512,3072]{1,0:T(8,128)(2,1)S(1)}, bf16[512,384]{1,0:T(8,128)(2,1)S(1)}, f32[384,512]{1,0:T(8,128)S(1)}, f32[384,512]{1,0:T(8,128)S(1)}) custom-call(s32[6]{0:T(128)S(1)} %concatenate.6.info, bf16[4,32,3840]{2,1,0:T(8,128)(2,1)S(1)} %get-tuple-element.70.refs_0_, bf16[4,32,3840]{2,1,0:T(8,128)(2,1)S(1)} %collective-permute-done.3.refs_1_, ...), custom_call_target="tpu_custom_call" | custom-call | flops 1207959552 | bytes 12582912 | tf_op jit(solution)/shard_map/pallas_call | solution.py:162
  58.5 2.9 %shard_map.69 = (f32[384,512]{1,0:T(8,128)S(1)}, f32[8,512]{1,0:T(8,128)S(1)}) custom-call(s32[6]{0:T(128)S(1)} %concatenate.6.info, bf16[8,192,384]{2,1,0:T(8,128)(2,1)S(1)} %constant_dynamic-update-slice_fusion.own, bf16[8,192,384]{2,1,0:T(8,128)(2,1)S(1)} %collective-permute-done.11.other, bf16[512,3072]{1,0:T(8,128)(2,1)S(1)} %get-tuple-element.76.context, ...), custom_call_target="tpu_custom_call" | custom-call | flops 1207959552 | bytes 12582912 | tf_op jit(solution)/shard_map/pallas_call | solution.py:198
  61.4 13.7 %all_to_all.10.stats = f32[16,8,512]{2,1,0:T(8,128)S(1)} all-to-all(f32[16,8,512]{2,1,0:T(8,128)S(1)} %broadcast_in_dim.5), channel_id=1, replica_groups=mesh['x'=4,'zh'=2,'y'=4,'zl'=4,'c'=2] {'x','y'}, dimensions={0} | all-to-all | bytes 524288 | tf_op jit(solution)/shard_map/all_to_all | solution.py:359
  75.1 2.3 %shard_map.70 = (bf16[384,512]{1,0:T(8,128)(2,1)S(1)}, bf16[8,192,384]{2,1,0:T(8,128)(2,1)S(1)}) custom-call(s32[6]{0:T(128)S(1)} %concatenate.6.info, f32[16,8,512]{2,1,0:T(8,128)S(1)} %all_to_all.10.stats, f32[384,512]{1,0:T(8,128)S(1)} %get-tuple-element.81.s, f32[384,512]{1,0:T(8,128)S(1)} %get-tuple-element.78.u_in.u, ...), custom_call_target="tpu_custom_call" | custom-call | flops 603979776 | bytes 12582912 | tf_op jit(solution)/shard_map/pallas_call | solution.py:244
  77.5 2.8 %collective-permute-done.12.received = bf16[8,192,384]{2,1,0:T(8,128)(2,1)S(1)} collective-permute-done((bf16[8,192,384]{2,1,0:T(8,128)(2,1)S(1)}, bf16[8,192,384]{2,1,0:T(8,128)(2,1)S(1)}, u32[]{:S(2)}, u32[]{:S(2)}) %collective-permute-start.12) | collective-permute-done | bytes 1179680 | tf_op jit(solution)/shard_map/ppermute | solution.py:317
  80.4 1.6 %shard_map.71 = (bf16[192,384]{1,0:T(8,128)(2,1)S(1)}, bf16[192,384]{1,0:T(8,128)(2,1)S(1)}, bf16[192,384]{1,0:T(8,128)(2,1)S(1)}, bf16[192,384]{1,0:T(8,128)(2,...) custom-call(s32[6]{0:T(128)S(1)} %concatenate.6.info, ...), custom_call_target="tpu_custom_call" | custom-call | flops 603979776 | bytes 12582912 | tf_op jit(solution)/shard_map/pallas_call | solution.py:271
  81.9 1.1 %collective-permute-start.15 = (bf16[192,384]{1,0:T(8,128)(2,1)S(1)}, bf16[192,384]{1,0:T(8,128)(2,1)S(1)}, u32[]{:S(2)}, u32[]{:S(2)}) collective-permute-start(bf16[192,384]{1,0:T(8,128)(2,1)S(1)} %get-tuple-element.87), channel_id=1, source_target_pairs={{0,2},{2,4},{4,6},{6,32},{32,34},{34,36},{36,38},{38,0},{1,3},{3,5... | collective-permute-start | bytes 442376 | tf_op jit(solution)/shard_map/ppermute | solution.py:33
  83.1 1.8 %collective-permute-start.16 = (bf16[192,384]{1,0:T(8,128)(2,1)S(1)}, bf16[192,384]{1,0:T(8,128)(2,1)S(1)}, u32[]{:S(2)}, u32[]{:S(2)}) collective-permute-start(bf16[192,384]{1,0:T(8,128)(2,1)S(1)} %get-tuple-element.88), channel_id=1, source_target_pairs={{0,38},{2,0},{4,2},{6,4},{32,6},{34,32},{36,34},{38,36},{1,39},{3,... | collective-permute-start | bytes 442376 | tf_op jit(solution)/shard_map/ppermute | solution.py:33
  84.9 2.5 %collective-permute-start.17 = (bf16[96,384]{1,0:T(8,128)(2,1)S(1)}, bf16[96,384]{1,0:T(8,128)(2,1)S(1)}, u32[]{:S(2)}, u32[]{:S(2)}) collective-permute-start(bf16[96,384]{1,0:T(8,128)(2,1)S(1)} %get-tuple-element.89), channel_id=1, source_target_pairs={{0,4},{2,6},{4,32},{6,34},{32,36},{34,38},{36,0},{38,2},{1,5},{3,7... | collective-permute-start | bytes 221192 | tf_op jit(solution)/shard_map/ppermute | solution.py:33
  87.3 2.1 %collective-permute-start.18 = (bf16[96,384]{1,0:T(8,128)(2,1)S(1)}, bf16[96,384]{1,0:T(8,128)(2,1)S(1)}, u32[]{:S(2)}, u32[]{:S(2)}) collective-permute-start(bf16[96,384]{1,0:T(8,128)(2,1)S(1)} %get-tuple-element.90), channel_id=1, source_target_pairs={{0,36},{2,38},{4,0},{6,2},{32,4},{34,6},{36,32},{38,34},{1,37},{3,... | collective-permute-start | bytes 221192 | tf_op jit(solution)/shard_map/ppermute | solution.py:33
  90.6 3.3 %collective-permute-done.17.four_up = bf16[96,384]{1,0:T(8,128)(2,1)S(1)} collective-permute-done((bf16[96,384]{1,0:T(8,128)(2,1)S(1)}, bf16[96,384]{1,0:T(8,128)(2,1)S(1)}, u32[]{:S(2)}, u32[]{:S(2)}) %collective-permute-start.17) | collective-permute-done | bytes 73760 | tf_op jit(solution)/shard_map/ppermute | solution.py:33
  93.9 3.3 %collective-permute-start.14 = (bf16[192,384]{1,0:T(8,128)(2,1)S(1)}, bf16[192,384]{1,0:T(8,128)(2,1)S(1)}, u32[]{:S(2)}, u32[]{:S(2)}) collective-permute-start(bf16[192,384]{1,0:T(8,128)(2,1)S(1)} %get-tuple-element.86), channel_id=1, source_target_pairs={{0,38},{2,0},{4,2},{6,4},{32,6},{34,32},{36,34},{38,36},{1,39},{3,... | collective-permute-start | bytes 442376 | tf_op jit(solution)/shard_map/ppermute | solution.py:33
  97.3 4.1 %collective-permute-start.20 = (bf16[192,384]{1,0:T(8,128)(2,1)S(1)}, bf16[192,384]{1,0:T(8,128)(2,1)S(1)}, u32[]{:S(2)}, u32[]{:S(2)}) collective-permute-start(bf16[192,384]{1,0:T(8,128)(2,1)S(1)} %get-tuple-element.92), channel_id=1, source_target_pairs={{0,36},{2,38},{4,0},{6,2},{32,4},{34,6},{36,32},{38,34},{1,37},{3,... | collective-permute-start | bytes 442376 | tf_op jit(solution)/shard_map/ppermute | solution.py:33
  101.5 5.5 %collective-permute-done.19.up = bf16[192,384]{1,0:T(8,128)(2,1)S(1)} collective-permute-done((bf16[192,384]{1,0:T(8,128)(2,1)S(1)}, bf16[192,384]{1,0:T(8,128)(2,1)S(1)}, u32[]{:S(2)}, u32[]{:S(2)}) %collective-permute-start.19) | collective-permute-done | bytes 147488 | tf_op jit(solution)/shard_map/ppermute | solution.py:33
  107.0 1.5 %shard_map.73 = f32[192,384]{1,0:T(8,128)} custom-call(s32[6]{0:T(128)S(1)} %concatenate.6.info, f32[3,192,384]{2,1,0:T(8,128)S(1)} %get-tuple-element.84.kept, bf16[192,384]{1,0:T(8,128)(2,1)S(1)} %collective-permute-done.13.a, bf16[192,384]{1,0:T(8,128)(2,1)S(1)} %collective-permute-done.14.b, bf16[192,384]{1,0:T(8,128)(2,1)S(1)} %collective-permute-done.19.up, ...), custom_call_target="tpu_custom_call" | custom-call | flops 1474560 | bytes 1474560 | tf_op jit(solution)/shard_map/pallas_call | solution.py:290
  (39 shorter events, 8.1 us)
Async XLA Ops:
  0.0 18.6 %copy-start.2 = (bf16[192,384]{1,0:T(8,128)(2,1)S(1)}, bf16[192,384]{1,0:T(8,128)(2,1)}, u32[]{:S(2)}) copy-start(bf16[192,384]{1,0:T(8,128)(2,1)} %param.8) | copy-start | bytes 442372
  0.0 13.3 %all-to-all-start = ((bf16[8,32,384]{2,1,0:T(8,128)(2,1)}), bf16[8,32,384]{2,1,0:T(8,128)(2,1)S(1)}, u32[]{:S(2)}, u32[]{:S(2)}) async-start(bf16[8,32,384]{2,1,0:T(8,128)(2,1)} %bitcast.14), calls=%async_computation | async-start | bytes 393216 | tf_op jit(solution)/shard_map/all_to_all | solution.py:342
  6.1 12.5 %collective-permute-start.8 = (bf16[192,384]{1,0:T(8,128)(2,1)}, bf16[192,384]{1,0:T(8,128)(2,1)S(1)}, u32[]{:S(2)}, u32[]{:S(2)}) collective-permute-start(bf16[192,384]{1,0:T(8,128)(2,1)} %param.8), channel_id=1, source_target_pairs={{0,38},{2,0},{4,2},{6,4},{32,6},{34,32},{36,34},{38,36},{1,39},{3,... | collective-permute-start | bytes 442376 | tf_op jit(solution)/shard_map/ppermute | solution.py:33
  6.2 12.4 %collective-permute-start.6 = (bf16[192,384]{1,0:T(8,128)(2,1)}, bf16[192,384]{1,0:T(8,128)(2,1)S(1)}, u32[]{:S(2)}, u32[]{:S(2)}) collective-permute-start(bf16[192,384]{1,0:T(8,128)(2,1)} %param.8), channel_id=1, source_target_pairs={{0,2},{2,4},{4,6},{6,32},{32,34},{34,36},{36,38},{38,0},{1,3},{3,5... | collective-permute-start | bytes 442376 | tf_op jit(solution)/shard_map/ppermute | solution.py:33
  9.7 1.0 copy-start
  10.7 1.0 copy-start.1
  13.5 10.7 %collective-permute-start = (bf16[64,3072]{1,0:T(8,128)(2,1)S(1)}, bf16[64,3072]{1,0:T(8,128)(2,1)S(1)}, u32[]{:S(2)}, u32[]{:S(2)}) collective-permute-start(bf16[64,3072]{1,0:T(8,128)(2,1)S(1)} %get-tuple-element.54), channel_id=1, source_target_pairs={{0,64},{1,9},{8,72},{9,17},{16,80},{17,25},{24,88},{25,1},{64,128}... | collective-permute-start | bytes 1179656 | tf_op jit(solution)/shard_map/ppermute | solution.py:333
  15.0 11.3 %collective-permute-start.1 = (bf16[64,3072]{1,0:T(8,128)(2,1)S(1)}, bf16[64,3072]{1,0:T(8,128)(2,1)S(1)}, u32[]{:S(2)}, u32[]{:S(2)}) collective-permute-start(bf16[64,3072]{1,0:T(8,128)(2,1)S(1)} %get-tuple-element.55), channel_id=1, source_target_pairs={{0,192},{1,25},{8,200},{9,1},{16,208},{17,9},{24,216},{25,17},{64,... | collective-permute-start | bytes 1179656 | tf_op jit(solution)/shard_map/ppermute | solution.py:333
  16.8 10.9 %collective-permute-start.2 = (bf16[64,3072]{1,0:T(8,128)(2,1)S(1)}, bf16[64,3072]{1,0:T(8,128)(2,1)S(1)}, u32[]{:S(2)}, u32[]{:S(2)}) collective-permute-start(bf16[64,3072]{1,0:T(8,128)(2,1)S(1)} %get-tuple-element.56), channel_id=1, source_target_pairs={{0,128},{1,17},{8,136},{9,25},{16,144},{17,1},{24,152},{25,9},{64,... | collective-permute-start | bytes 1179656 | tf_op jit(solution)/shard_map/ppermute | solution.py:333
  18.7 16.0 %collective-permute-start.9 = (bf16[2,192,384]{2,1,0:T(8,128)(2,1)S(1)}, bf16[2,192,384]{2,1,0:T(8,128)(2,1)S(1)}, u32[]{:S(2)}, u32[]{:S(2)}) collective-permute-start(bf16[2,192,384]{2,1,0:T(8,128)(2,1)S(1)} %get-tuple-element.67), channel_id=1, source_target_pairs={{0,36},{2,38},{4,0},{6,2},{32,4},{34,6},{36,32},{38,34},{1,37},{3,... | collective-permute-start | bytes 884744 | tf_op jit(solution)/shard_map/ppermute | solution.py:33
  24.2 14.8 %collective-permute-start.7 = (bf16[2,192,384]{2,1,0:T(8,128)(2,1)S(1)}, bf16[2,192,384]{2,1,0:T(8,128)(2,1)S(1)}, u32[]{:S(2)}, u32[]{:S(2)}) collective-permute-start(bf16[2,192,384]{2,1,0:T(8,128)(2,1)S(1)} %get-tuple-element.66), channel_id=1, source_target_pairs={{0,4},{2,6},{4,32},{6,34},{32,36},{34,38},{36,0},{38,2},{1,5},{3,7... | collective-permute-start | bytes 884744 | tf_op jit(solution)/shard_map/ppermute | solution.py:33
  28.5 15.4 %collective-permute-start.3 = (bf16[4,32,3840]{2,1,0:T(8,128)(2,1)S(1)}, bf16[4,32,3840]{2,1,0:T(8,128)(2,1)S(1)}, u32[]{:S(2)}, u32[]{:S(2)}) collective-permute-start(bf16[4,32,3840]{2,1,0:T(8,128)(2,1)S(1)} %get-tuple-element.62), channel_id=1, source_target_pairs={{0,8},{1,65},{8,16},{9,73},{16,24},{17,81},{24,0},{25,89},{64,72},... | collective-permute-start | bytes 2949128 | tf_op jit(solution)/shard_map/ppermute | solution.py:333
  30.2 14.1 %collective-permute-start.4 = (bf16[4,32,3840]{2,1,0:T(8,128)(2,1)S(1)}, bf16[4,32,3840]{2,1,0:T(8,128)(2,1)S(1)}, u32[]{:S(2)}, u32[]{:S(2)}) collective-permute-start(bf16[4,32,3840]{2,1,0:T(8,128)(2,1)S(1)} %get-tuple-element.63), channel_id=1, source_target_pairs={{0,24},{1,193},{8,0},{9,201},{16,8},{17,209},{24,16},{25,217},{64,... | collective-permute-start | bytes 2949128 | tf_op jit(solution)/shard_map/ppermute | solution.py:333
  31.9 23.8 %collective-permute-start.5 = (bf16[4,32,3840]{2,1,0:T(8,128)(2,1)S(1)}, bf16[4,32,3840]{2,1,0:T(8,128)(2,1)S(1)}, u32[]{:S(2)}, u32[]{:S(2)}) collective-permute-start(bf16[4,32,3840]{2,1,0:T(8,128)(2,1)S(1)} %get-tuple-element.64), channel_id=1, source_target_pairs={{0,16},{1,129},{8,24},{9,137},{16,0},{17,145},{24,8},{25,153},{64,... | collective-permute-start | bytes 2949128 | tf_op jit(solution)/shard_map/ppermute | solution.py:333
  34.7 7.6 %collective-permute-start.10 = (bf16[192,384]{1,0:T(8,128)(2,1)S(1)}, bf16[192,384]{1,0:T(8,128)(2,1)S(1)}, u32[]{:S(2)}, u32[]{:S(2)}) collective-permute-start(bf16[192,384]{1,0:T(8,128)(2,1)S(1)} %slice_bitcast_fusion), channel_id=1, source_target_pairs={{0,38},{2,0},{4,2},{6,4},{32,6},{34,32},{36,34},{38,36},{1,39},{3,... | collective-permute-start | bytes 442376 | tf_op jit(solution)/shard_map/ppermute | solution.py:33
  55.7 2.8 %collective-permute-start.11 = (bf16[8,192,384]{2,1,0:T(8,128)(2,1)S(1)}, bf16[8,192,384]{2,1,0:T(8,128)(2,1)S(1)}, u32[]{:S(2)}, u32[]{:S(2)}) collective-permute-start(bf16[8,192,384]{2,1,0:T(8,128)(2,1)S(1)} %constant_dynamic-update-slice_fusion.own), channel_id=1, source_target_pairs={{0,1},{1,0},{2,3},{3,2},{4,5},{5,4},{6,7},{7,6},{8,9},{9,8},{10,11... | collective-permute-start | bytes 3538952 | tf_op jit(solution)/shard_map/ppermute | solution.py:317
  77.4 2.9 %collective-permute-start.12 = (bf16[8,192,384]{2,1,0:T(8,128)(2,1)S(1)}, bf16[8,192,384]{2,1,0:T(8,128)(2,1)S(1)}, u32[]{:S(2)}, u32[]{:S(2)}) collective-permute-start(bf16[8,192,384]{2,1,0:T(8,128)(2,1)S(1)} %get-tuple-element.83), channel_id=1, source_target_pairs={{0,1},{1,0},{2,3},{3,2},{4,5},{5,4},{6,7},{7,6},{8,9},{9,8},{10,11... | collective-permute-start | bytes 3538952 | tf_op jit(solution)/shard_map/ppermute | solution.py:317
  81.9 15.2 %collective-permute-start.15 = (bf16[192,384]{1,0:T(8,128)(2,1)S(1)}, bf16[192,384]{1,0:T(8,128)(2,1)S(1)}, u32[]{:S(2)}, u32[]{:S(2)}) collective-permute-start(bf16[192,384]{1,0:T(8,128)(2,1)S(1)} %get-tuple-element.87), channel_id=1, source_target_pairs={{0,2},{2,4},{4,6},{6,32},{32,34},{34,36},{36,38},{38,0},{1,3},{3,5... | collective-permute-start | bytes 442376 | tf_op jit(solution)/shard_map/ppermute | solution.py:33
  83.1 14.1 %collective-permute-start.16 = (bf16[192,384]{1,0:T(8,128)(2,1)S(1)}, bf16[192,384]{1,0:T(8,128)(2,1)S(1)}, u32[]{:S(2)}, u32[]{:S(2)}) collective-permute-start(bf16[192,384]{1,0:T(8,128)(2,1)S(1)} %get-tuple-element.88), channel_id=1, source_target_pairs={{0,38},{2,0},{4,2},{6,4},{32,6},{34,32},{36,34},{38,36},{1,39},{3,... | collective-permute-start | bytes 442376 | tf_op jit(solution)/shard_map/ppermute | solution.py:33
  84.9 9.0 %collective-permute-start.17 = (bf16[96,384]{1,0:T(8,128)(2,1)S(1)}, bf16[96,384]{1,0:T(8,128)(2,1)S(1)}, u32[]{:S(2)}, u32[]{:S(2)}) collective-permute-start(bf16[96,384]{1,0:T(8,128)(2,1)S(1)} %get-tuple-element.89), channel_id=1, source_target_pairs={{0,4},{2,6},{4,32},{6,34},{32,36},{34,38},{36,0},{38,2},{1,5},{3,7... | collective-permute-start | bytes 221192 | tf_op jit(solution)/shard_map/ppermute | solution.py:33
  87.3 9.8 %collective-permute-start.18 = (bf16[96,384]{1,0:T(8,128)(2,1)S(1)}, bf16[96,384]{1,0:T(8,128)(2,1)S(1)}, u32[]{:S(2)}, u32[]{:S(2)}) collective-permute-start(bf16[96,384]{1,0:T(8,128)(2,1)S(1)} %get-tuple-element.90), channel_id=1, source_target_pairs={{0,36},{2,38},{4,0},{6,2},{32,4},{34,6},{36,32},{38,34},{1,37},{3,... | collective-permute-start | bytes 221192 | tf_op jit(solution)/shard_map/ppermute | solution.py:33
  89.5 12.0 %collective-permute-start.13 = (bf16[192,384]{1,0:T(8,128)(2,1)S(1)}, bf16[192,384]{1,0:T(8,128)(2,1)S(1)}, u32[]{:S(2)}, u32[]{:S(2)}) collective-permute-start(bf16[192,384]{1,0:T(8,128)(2,1)S(1)} %get-tuple-element.85), channel_id=1, source_target_pairs={{0,2},{2,4},{4,6},{6,32},{32,34},{34,36},{36,38},{38,0},{1,3},{3,5... | collective-permute-start | bytes 442376 | tf_op jit(solution)/shard_map/ppermute | solution.py:33
  93.9 7.6 %collective-permute-start.14 = (bf16[192,384]{1,0:T(8,128)(2,1)S(1)}, bf16[192,384]{1,0:T(8,128)(2,1)S(1)}, u32[]{:S(2)}, u32[]{:S(2)}) collective-permute-start(bf16[192,384]{1,0:T(8,128)(2,1)S(1)} %get-tuple-element.86), channel_id=1, source_target_pairs={{0,38},{2,0},{4,2},{6,4},{32,6},{34,32},{36,34},{38,36},{1,39},{3,... | collective-permute-start | bytes 442376 | tf_op jit(solution)/shard_map/ppermute | solution.py:33
  97.3 9.7 %collective-permute-start.19 = (bf16[192,384]{1,0:T(8,128)(2,1)S(1)}, bf16[192,384]{1,0:T(8,128)(2,1)S(1)}, u32[]{:S(2)}, u32[]{:S(2)}) collective-permute-start(bf16[192,384]{1,0:T(8,128)(2,1)S(1)} %get-tuple-element.91), channel_id=1, source_target_pairs={{0,4},{2,6},{4,32},{6,34},{32,36},{34,38},{36,0},{38,2},{1,5},{3,7... | collective-permute-start | bytes 442376 | tf_op jit(solution)/shard_map/ppermute | solution.py:33
  97.3 9.6 %collective-permute-start.20 = (bf16[192,384]{1,0:T(8,128)(2,1)S(1)}, bf16[192,384]{1,0:T(8,128)(2,1)S(1)}, u32[]{:S(2)}, u32[]{:S(2)}) collective-permute-start(bf16[192,384]{1,0:T(8,128)(2,1)S(1)} %get-tuple-element.92), channel_id=1, source_target_pairs={{0,36},{2,38},{4,0},{6,2},{32,4},{34,6},{36,32},{38,34},{1,37},{3,... | collective-permute-start | bytes 442376 | tf_op jit(solution)/shard_map/ppermute | solution.py:33

commit v5 on v3

--- a/solution.py
+++ b/solution.py
@@ -323,7 +323,7 @@
 
 def leg(blocks, axes):
     out = [blocks[0]]
-    for k in range(1, 4):
+    for k in (2, 1, 3):
         pairs = []
         for x in range(4):
             for y in range(4):
@@ -343,6 +343,7 @@
     rows, rest, gain = lax.optimization_barrier((rows, rest, gain))
 
     came = lax.optimization_barrier(leg(first_leg(rows, rest), "xy"))
+    came = [came[n] for n in (0, 2, 1, 3)]
     behind, ahead = shift(out_proj, Z, 1), shift(out_proj, Z, -1)
     two, ahead2 = after(jnp.stack([out_proj, behind]), rows), after(jnp.stack([out_proj, ahead]), rows)
     behind2, ahead2 = shift(two, Z, 2), shift(ahead2, Z, -2)
@@ -351,6 +352,7 @@
 
     probe = make_probe(after(info, *came))
     *pieces, probe, own = lax.optimization_barrier((*leg(second_leg(info, came), "yx"), probe, own))
+    pieces = [pieces[n] for n in (0, 2, 1, 3)]
     other = swap(own)
     rows, res, u, w = tangent_of(info, pieces, probe, gain)
     s, stats = stream_of(info, own, other, rows, res, u, w)
@@ -358,9 +360,10 @@
     grad, send = away(info, stats, s, u, w, rows)
     near_up, near_down, three_up, three_down, four_up, four_down, kept = home(info, grad, rows, swap(send))
 
+    four_up, four_down, three_up, three_down = lax.optimization_barrier(
+        (shift(four_up, Z, 2), shift(four_down, Z, -2), shift(three_up, Z, 1), shift(three_down, Z, -1))
+    )
     near_up, near_down = shift(near_up, Z, 1), shift(near_down, Z, -1)
-    three_up, three_down = shift(three_up, Z, 1), shift(three_down, Z, -1)
-    four_up, four_down = shift(four_up, Z, 2), shift(four_down, Z, -2)
     up, down = between(kept, three_up, three_down, four_up, four_down)
     up, down = shift(up, Z, 2), shift(down, Z, -2)
     return last(info, kept, near_up, near_down, up, down)

time: 110 us -> 109 us (level)
  waiting for transfers between devices: 31.2 us -> 29.4 us
    ppermute x6, waiting for transfers between devices: 15.6 us -> 12.7 us  [leg(): out.append(lax.ppermute(blocks[k], XYC, pairs))]
    ppermute x6, starting transfers between devices: 11.6 us -> 12.9 us  [leg(): out.append(lax.ppermute(blocks[k], XYC, pairs))]
    ppermute x13, waiting for transfers between devices: 11.9 us -> 13.1 us  [shift(): return lax.ppermute(v, axis, [(s, (s + k) % n) for s in range(n)])]
  transfers between devices with their start and end apart: 22 -> 22, of which waited for: 10 -> 12; matrix products, arithmetic and copies ran while one was open for 2% -> 2% of each run, Pallas kernels for 7% -> 7%
where the time goes in v5:
time: 109 us; the launch traced here: 108 us
  starting transfers between devices  44.2 us (41%)
  waiting for transfers between devices  29.4 us (27%)
  Pallas kernels  16.1 us (15%)
  blocking collectives  14.7 us (13%)
  local copies, waits for them, and re-layouts  3.76 us (3%)
    ppermute x13, starting transfers between devices, shift(): return lax.ppermute(v, axis, [(s, (s + k) % n) for s in range(n)])  25.1 us
    all_to_all x1, blocking collectives, on_device(): lax.all_to_all(jnp.broadcast_to(stats[None], (16, 8, TOK)), XY, 0, 0, til...  14.7 us
    ppermute x13, waiting for transfers between devices, shift(): return lax.ppermute(v, axis, [(s, (s + k) % n) for s in range(n)])  13.1 us
    ppermute x6, starting transfers between devices, leg(): out.append(lax.ppermute(blocks[k], XYC, pairs))  12.9 us
    ppermute x6, waiting for transfers between devices, leg(): out.append(lax.ppermute(blocks[k], XYC, pairs))  12.7 us
    all_to_all x1, starting transfers between devices, on_device(): rows = lax.all_to_all(context.reshape(8, OWN, F), T, 0, 0, tiled=True)  6.14 us
    ppermute x2, waiting for transfers between devices, swap(): return lax.ppermute(v, 'c', [(0, 1), (1, 0)])  3.23 us
    pallas_call x1, Pallas kernels, make_probe(): pl.pallas_call(probe_kernel, grid=(8,), in_specs=[pl.BlockSpec(memory_spa...  3.21 us
  transfers between devices with their start and end apart: 22, of which 12 were waited for; matrix products, arithmetic and copies ran while one was open for 2% of the time, Pallas kernels for 7%

profile of v5, /device:TPU:32, one launch (start us, length us, event | category | flops | bytes accessed | tf_op | source)
XLA Modules:
  0.0 108.4 jit_solution(4543919665731008793)
XLA Ops:
  0.0 6.1 %all-to-all-start = ((bf16[8,32,384]{2,1,0:T(8,128)(2,1)}), bf16[8,32,384]{2,1,0:T(8,128)(2,1)S(1)}, u32[]{:S(2)}, u32[]{:S(2)}) async-start(bf16[8,32,384]{2,1,0:T(8,128)(2,1)} %bitcast.14), calls=%async_computation | async-start | bytes 393216 | tf_op jit(solution)/shard_map/all_to_all | solution.py:342
  6.2 2.0 %collective-permute-start.6 = (bf16[192,384]{1,0:T(8,128)(2,1)}, bf16[192,384]{1,0:T(8,128)(2,1)S(1)}, u32[]{:S(2)}, u32[]{:S(2)}) collective-permute-start(bf16[192,384]{1,0:T(8,128)(2,1)} %param.8), channel_id=1, source_target_pairs={{0,2},{2,4},{4,6},{6,32},{32,34},{34,36},{36,38},{38,0},{1,3},{3,5... | collective-permute-start | bytes 442376 | tf_op jit(solution)/shard_map/ppermute | solution.py:33
  9.7 1.0 copy-done
  10.7 1.0 copy-done.1
  11.7 1.2 %shard_map.64 = (bf16[4,32,3072]{2,1,0:T(8,128)(2,1)S(1)}, f32[384,1]{1,0:T(8,128)S(1)}) custom-call(s32[6]{0:T(128)S(1)} %concatenate.6.info, bf16[32,6144]{1,0:T(8,128)(2,1)S(1)} %copy-done, bf16[32,6144]{1,0:T(8,128)(2,1)S(1)} %copy-done.1, f32[32,192]{1,0:T(8,128)S(1)} %reshape.8.gains), custom_call_target="tpu_custom_call" | custom-call | bytes 1572864 | tf_op jit(solution)/shard_map/pallas_call | solution.py:96
  13.5 3.1 %collective-permute-start = (bf16[64,3072]{1,0:T(8,128)(2,1)S(1)}, bf16[64,3072]{1,0:T(8,128)(2,1)S(1)}, u32[]{:S(2)}, u32[]{:S(2)}) collective-permute-start(bf16[64,3072]{1,0:T(8,128)(2,1)S(1)} %get-tuple-element.58), channel_id=1, source_target_pairs={{0,128},{1,17},{8,136},{9,25},{16,144},{17,1},{24,152},{25,9},{64,... | collective-permute-start | bytes 1179656 | tf_op jit(solution)/shard_map/ppermute | solution.py:333
  17.2 2.6 %collective-permute-start.2 = (bf16[64,3072]{1,0:T(8,128)(2,1)S(1)}, bf16[64,3072]{1,0:T(8,128)(2,1)S(1)}, u32[]{:S(2)}, u32[]{:S(2)}) collective-permute-start(bf16[64,3072]{1,0:T(8,128)(2,1)S(1)} %get-tuple-element.60), channel_id=1, source_target_pairs={{0,192},{1,25},{8,200},{9,1},{16,208},{17,9},{24,216},{25,17},{64,... | collective-permute-start | bytes 1179656 | tf_op jit(solution)/shard_map/ppermute | solution.py:333
  19.9 5.5 %collective-permute-start.9 = (bf16[2,192,384]{2,1,0:T(8,128)(2,1)S(1)}, bf16[2,192,384]{2,1,0:T(8,128)(2,1)S(1)}, u32[]{:S(2)}, u32[]{:S(2)}) collective-permute-start(bf16[2,192,384]{2,1,0:T(8,128)(2,1)S(1)} %get-tuple-element.71), channel_id=1, source_target_pairs={{0,36},{2,38},{4,0},{6,2},{32,4},{34,6},{36,32},{38,34},{1,37},{3,... | collective-permute-start | bytes 884744 | tf_op jit(solution)/shard_map/ppermute | solution.py:33
  25.4 1.6 %collective-permute-done.1.refs_1_ = bf16[64,3072]{1,0:T(8,128)(2,1)S(1)} collective-permute-done((bf16[64,3072]{1,0:T(8,128)(2,1)S(1)}, bf16[64,3072]{1,0:T(8,128)(2,1)S(1)}, u32[]{:S(2)}, u32[]{:S(2)}) %collective-permute-start.1) | collective-permute-done | bytes 393248 | tf_op jit(solution)/shard_map/ppermute | solution.py:333
  27.9 3.3 %collective-permute-start.3 = (bf16[4,32,3840]{2,1,0:T(8,128)(2,1)S(1)}, bf16[4,32,3840]{2,1,0:T(8,128)(2,1)S(1)}, u32[]{:S(2)}, u32[]{:S(2)}) collective-permute-start(bf16[4,32,3840]{2,1,0:T(8,128)(2,1)S(1)} %get-tuple-element.66), channel_id=1, source_target_pairs={{0,16},{1,129},{8,24},{9,137},{16,0},{17,145},{24,8},{25,153},{64,... | collective-permute-start | bytes 2949128 | tf_op jit(solution)/shard_map/ppermute | solution.py:333
  31.9 2.6 %collective-permute-start.5 = (bf16[4,32,3840]{2,1,0:T(8,128)(2,1)S(1)}, bf16[4,32,3840]{2,1,0:T(8,128)(2,1)S(1)}, u32[]{:S(2)}, u32[]{:S(2)}) collective-permute-start(bf16[4,32,3840]{2,1,0:T(8,128)(2,1)S(1)} %get-tuple-element.68), channel_id=1, source_target_pairs={{0,24},{1,193},{8,0},{9,201},{16,8},{17,209},{24,16},{25,217},{64,... | collective-permute-start | bytes 2949128 | tf_op jit(solution)/shard_map/ppermute | solution.py:333
  34.5 1.4 %collective-permute-done.9 = bf16[2,192,384]{2,1,0:T(8,128)(2,1)S(1)} collective-permute-done((bf16[2,192,384]{2,1,0:T(8,128)(2,1)S(1)}, bf16[2,192,384]{2,1,0:T(8,128)(2,1)S(1)}, u32[]{:S(2)}, u32[]{:S(2)}) %collective-permute-start.9) | collective-permute-done | bytes 294944 | tf_op jit(solution)/shard_map/ppermute | solution.py:33
  35.9 1.4 %collective-permute-start.10 = (bf16[192,384]{1,0:T(8,128)(2,1)S(1)}, bf16[192,384]{1,0:T(8,128)(2,1)S(1)}, u32[]{:S(2)}, u32[]{:S(2)}) collective-permute-start(bf16[192,384]{1,0:T(8,128)(2,1)S(1)} %slice_bitcast_fusion), channel_id=1, source_target_pairs={{0,38},{2,0},{4,2},{6,4},{32,6},{34,32},{36,34},{38,36},{1,39},{3,... | collective-permute-start | bytes 442376 | tf_op jit(solution)/shard_map/ppermute | solution.py:33
  37.3 2.9 %collective-permute-done.7 = bf16[2,192,384]{2,1,0:T(8,128)(2,1)S(1)} collective-permute-done((bf16[2,192,384]{2,1,0:T(8,128)(2,1)S(1)}, bf16[2,192,384]{2,1,0:T(8,128)(2,1)S(1)}, u32[]{:S(2)}, u32[]{:S(2)}) %collective-permute-start.7) | collective-permute-done | bytes 294944 | tf_op jit(solution)/shard_map/ppermute | solution.py:33
  40.3 3.2 %shard_map.67.refs_4_ = bf16[384,3072]{1,0:T(8,128)(2,1)S(1)} custom-call(s32[6]{0:T(128)S(1)} %concatenate.6.info), custom_call_target="tpu_custom_call" | custom-call | flops 16515072 | bytes 2359296 | tf_op jit(solution)/shard_map/pallas_call | solution.py:55
  43.7 10.4 %collective-permute-done.4.refs_1_ = bf16[4,32,3840]{2,1,0:T(8,128)(2,1)S(1)} collective-permute-done((bf16[4,32,3840]{2,1,0:T(8,128)(2,1)S(1)}, bf16[4,32,3840]{2,1,0:T(8,128)(2,1)S(1)}, u32[]{:S(2)}, u32[]{:S(2)}) %collective-permute-start.4) | collective-permute-done | bytes 983072 | tf_op jit(solution)/shard_map/ppermute | solution.py:333
  54.6 2.4 %shard_map.68 = (bf16[512,3072]{1,0:T(8,128)(2,1)S(1)}, bf16[512,384]{1,0:T(8,128)(2,1)S(1)}, f32[384,512]{1,0:T(8,128)S(1)}, f32[384,512]{1,0:T(8,128)S(1)}) custom-call(s32[6]{0:T(128)S(1)} %concatenate.6.info, bf16[4,32,3840]{2,1,0:T(8,128)(2,1)S(1)} %get-tuple-element.74.refs_0_, bf16[4,32,3840]{2,1,0:T(8,128)(2,1)S(1)} %collective-permute-done.4.refs_1_, ...), custom_call_target="tpu_custom_call" | custom-call | flops 1207959552 | bytes 12582912 | tf_op jit(solution)/shard_map/pallas_call | solution.py:162
  57.4 2.9 %shard_map.69 = (f32[384,512]{1,0:T(8,128)S(1)}, f32[8,512]{1,0:T(8,128)S(1)}) custom-call(s32[6]{0:T(128)S(1)} %concatenate.6.info, bf16[8,192,384]{2,1,0:T(8,128)(2,1)S(1)} %constant_dynamic-update-slice_fusion.own, bf16[8,192,384]{2,1,0:T(8,128)(2,1)S(1)} %collective-permute-done.11.other, bf16[512,3072]{1,0:T(8,128)(2,1)S(1)} %get-tuple-element.80.context, ...), custom_call_target="tpu_custom_call" | custom-call | flops 1207959552 | bytes 12582912 | tf_op jit(solution)/shard_map/pallas_call | solution.py:198
  60.3 14.7 %all_to_all.10.stats = f32[16,8,512]{2,1,0:T(8,128)S(1)} all-to-all(f32[16,8,512]{2,1,0:T(8,128)S(1)} %broadcast_in_dim.5), channel_id=1, replica_groups=mesh['x'=4,'zh'=2,'y'=4,'zl'=4,'c'=2] {'x','y'}, dimensions={0} | all-to-all | bytes 524288 | tf_op jit(solution)/shard_map/all_to_all | solution.py:359
  75.0 2.3 %shard_map.70 = (bf16[384,512]{1,0:T(8,128)(2,1)S(1)}, bf16[8,192,384]{2,1,0:T(8,128)(2,1)S(1)}) custom-call(s32[6]{0:T(128)S(1)} %concatenate.6.info, f32[16,8,512]{2,1,0:T(8,128)S(1)} %all_to_all.10.stats, f32[384,512]{1,0:T(8,128)S(1)} %get-tuple-element.85.s, f32[384,512]{1,0:T(8,128)S(1)} %get-tuple-element.82.u_in.u, ...), custom_call_target="tpu_custom_call" | custom-call | flops 603979776 | bytes 12582912 | tf_op jit(solution)/shard_map/pallas_call | solution.py:244
  77.5 2.8 %collective-permute-done.12.received = bf16[8,192,384]{2,1,0:T(8,128)(2,1)S(1)} collective-permute-done((bf16[8,192,384]{2,1,0:T(8,128)(2,1)S(1)}, bf16[8,192,384]{2,1,0:T(8,128)(2,1)S(1)}, u32[]{:S(2)}, u32[]{:S(2)}) %collective-permute-start.12) | collective-permute-done | bytes 1179680 | tf_op jit(solution)/shard_map/ppermute | solution.py:317
  80.3 1.6 %shard_map.71 = (bf16[192,384]{1,0:T(8,128)(2,1)S(1)}, bf16[192,384]{1,0:T(8,128)(2,1)S(1)}, bf16[192,384]{1,0:T(8,128)(2,1)S(1)}, bf16[192,384]{1,0:T(8,128)(2,...) custom-call(s32[6]{0:T(128)S(1)} %concatenate.6.info, ...), custom_call_target="tpu_custom_call" | custom-call | flops 603979776 | bytes 12582912 | tf_op jit(solution)/shard_map/pallas_call | solution.py:271
  81.9 1.1 %collective-permute-start.17 = (bf16[192,384]{1,0:T(8,128)(2,1)S(1)}, bf16[192,384]{1,0:T(8,128)(2,1)S(1)}, u32[]{:S(2)}, u32[]{:S(2)}) collective-permute-start(bf16[192,384]{1,0:T(8,128)(2,1)S(1)} %get-tuple-element.93), channel_id=1, source_target_pairs={{0,2},{2,4},{4,6},{6,32},{32,34},{34,36},{36,38},{38,0},{1,3},{3,5... | collective-permute-start | bytes 442376 | tf_op jit(solution)/shard_map/ppermute | solution.py:33
  83.0 1.8 %collective-permute-start.18 = (bf16[192,384]{1,0:T(8,128)(2,1)S(1)}, bf16[192,384]{1,0:T(8,128)(2,1)S(1)}, u32[]{:S(2)}, u32[]{:S(2)}) collective-permute-start(bf16[192,384]{1,0:T(8,128)(2,1)S(1)} %get-tuple-element.94), channel_id=1, source_target_pairs={{0,38},{2,0},{4,2},{6,4},{32,6},{34,32},{36,34},{38,36},{1,39},{3,... | collective-permute-start | bytes 442376 | tf_op jit(solution)/shard_map/ppermute | solution.py:33
  84.7 2.5 %collective-permute-start.15 = (bf16[96,384]{1,0:T(8,128)(2,1)S(1)}, bf16[96,384]{1,0:T(8,128)(2,1)S(1)}, u32[]{:S(2)}, u32[]{:S(2)}) collective-permute-start(bf16[96,384]{1,0:T(8,128)(2,1)S(1)} %get-tuple-element.91), channel_id=1, source_target_pairs={{0,4},{2,6},{4,32},{6,34},{32,36},{34,38},{36,0},{38,2},{1,5},{3,7... | collective-permute-start | bytes 221192 | tf_op jit(solution)/shard_map/ppermute | solution.py:33
  87.2 2.1 %collective-permute-start.16 = (bf16[96,384]{1,0:T(8,128)(2,1)S(1)}, bf16[96,384]{1,0:T(8,128)(2,1)S(1)}, u32[]{:S(2)}, u32[]{:S(2)}) collective-permute-start(bf16[96,384]{1,0:T(8,128)(2,1)S(1)} %get-tuple-element.92), channel_id=1, source_target_pairs={{0,36},{2,38},{4,0},{6,2},{32,4},{34,6},{36,32},{38,34},{1,37},{3,... | collective-permute-start | bytes 221192 | tf_op jit(solution)/shard_map/ppermute | solution.py:33
  89.4 1.1 %collective-permute-start.13 = (bf16[192,384]{1,0:T(8,128)(2,1)S(1)}, bf16[192,384]{1,0:T(8,128)(2,1)S(1)}, u32[]{:S(2)}, u32[]{:S(2)}) collective-permute-start(bf16[192,384]{1,0:T(8,128)(2,1)S(1)} %get-tuple-element.89), channel_id=1, source_target_pairs={{0,2},{2,4},{4,6},{6,32},{32,34},{34,36},{36,38},{38,0},{1,3},{3,5... | collective-permute-start | bytes 442376 | tf_op jit(solution)/shard_map/ppermute | solution.py:33
  90.5 3.3 %collective-permute-done.15.four_up = bf16[96,384]{1,0:T(8,128)(2,1)S(1)} collective-permute-done((bf16[96,384]{1,0:T(8,128)(2,1)S(1)}, bf16[96,384]{1,0:T(8,128)(2,1)S(1)}, u32[]{:S(2)}, u32[]{:S(2)}) %collective-permute-start.15) | collective-permute-done | bytes 73760 | tf_op jit(solution)/shard_map/ppermute | solution.py:33
  93.8 3.3 %collective-permute-start.14 = (bf16[192,384]{1,0:T(8,128)(2,1)S(1)}, bf16[192,384]{1,0:T(8,128)(2,1)S(1)}, u32[]{:S(2)}, u32[]{:S(2)}) collective-permute-start(bf16[192,384]{1,0:T(8,128)(2,1)S(1)} %get-tuple-element.90), channel_id=1, source_target_pairs={{0,38},{2,0},{4,2},{6,4},{32,6},{34,32},{36,34},{38,36},{1,39},{3,... | collective-permute-start | bytes 442376 | tf_op jit(solution)/shard_map/ppermute | solution.py:33
  97.2 4.1 %collective-permute-start.20 = (bf16[192,384]{1,0:T(8,128)(2,1)S(1)}, bf16[192,384]{1,0:T(8,128)(2,1)S(1)}, u32[]{:S(2)}, u32[]{:S(2)}) collective-permute-start(bf16[192,384]{1,0:T(8,128)(2,1)S(1)} %get-tuple-element.100), channel_id=1, source_target_pairs={{0,36},{2,38},{4,0},{6,2},{32,4},{34,6},{36,32},{38,34},{1,37},{3,... | collective-permute-start | bytes 442376 | tf_op jit(solution)/shard_map/ppermute | solution.py:33
  101.4 5.5 %collective-permute-done.19.up = bf16[192,384]{1,0:T(8,128)(2,1)S(1)} collective-permute-done((bf16[192,384]{1,0:T(8,128)(2,1)S(1)}, bf16[192,384]{1,0:T(8,128)(2,1)S(1)}, u32[]{:S(2)}, u32[]{:S(2)}) %collective-permute-start.19) | collective-permute-done | bytes 147488 | tf_op jit(solution)/shard_map/ppermute | solution.py:33
  106.9 1.5 %shard_map.73 = f32[192,384]{1,0:T(8,128)} custom-call(s32[6]{0:T(128)S(1)} %concatenate.6.info, f32[3,192,384]{2,1,0:T(8,128)S(1)} %get-tuple-element.88.kept, bf16[192,384]{1,0:T(8,128)(2,1)S(1)} %collective-permute-done.13.a, bf16[192,384]{1,0:T(8,128)(2,1)S(1)} %collective-permute-done.14.b, bf16[192,384]{1,0:T(8,128)(2,1)S(1)} %collective-permute-done.19.up, ...), custom_call_target="tpu_custom_call" | custom-call | flops 1474560 | bytes 1474560 | tf_op jit(solution)/shard_map/pallas_call | solution.py:290
  (39 shorter events, 5.7 us)
Async XLA Ops:
  0.0 19.8 %copy-start.2 = (bf16[192,384]{1,0:T(8,128)(2,1)S(1)}, bf16[192,384]{1,0:T(8,128)(2,1)}, u32[]{:S(2)}) copy-start(bf16[192,384]{1,0:T(8,128)(2,1)} %param.8) | copy-start | bytes 442372
  0.0 13.3 %all-to-all-start = ((bf16[8,32,384]{2,1,0:T(8,128)(2,1)}), bf16[8,32,384]{2,1,0:T(8,128)(2,1)S(1)}, u32[]{:S(2)}, u32[]{:S(2)}) async-start(bf16[8,32,384]{2,1,0:T(8,128)(2,1)} %bitcast.14), calls=%async_computation | async-start | bytes 393216 | tf_op jit(solution)/shard_map/all_to_all | solution.py:342
  6.1 13.7 %collective-permute-start.8 = (bf16[192,384]{1,0:T(8,128)(2,1)}, bf16[192,384]{1,0:T(8,128)(2,1)S(1)}, u32[]{:S(2)}, u32[]{:S(2)}) collective-permute-start(bf16[192,384]{1,0:T(8,128)(2,1)} %param.8), channel_id=1, source_target_pairs={{0,38},{2,0},{4,2},{6,4},{32,6},{34,32},{36,34},{38,36},{1,39},{3,... | collective-permute-start | bytes 442376 | tf_op jit(solution)/shard_map/ppermute | solution.py:33
  6.2 13.6 %collective-permute-start.6 = (bf16[192,384]{1,0:T(8,128)(2,1)}, bf16[192,384]{1,0:T(8,128)(2,1)S(1)}, u32[]{:S(2)}, u32[]{:S(2)}) collective-permute-start(bf16[192,384]{1,0:T(8,128)(2,1)} %param.8), channel_id=1, source_target_pairs={{0,2},{2,4},{4,6},{6,32},{32,34},{34,36},{36,38},{38,0},{1,3},{3,5... | collective-permute-start | bytes 442376 | tf_op jit(solution)/shard_map/ppermute | solution.py:33
  9.7 1.0 copy-start
  10.7 1.0 copy-start.1
  13.5 11.9 %collective-permute-start = (bf16[64,3072]{1,0:T(8,128)(2,1)S(1)}, bf16[64,3072]{1,0:T(8,128)(2,1)S(1)}, u32[]{:S(2)}, u32[]{:S(2)}) collective-permute-start(bf16[64,3072]{1,0:T(8,128)(2,1)S(1)} %get-tuple-element.58), channel_id=1, source_target_pairs={{0,128},{1,17},{8,136},{9,25},{16,144},{17,1},{24,152},{25,9},{64,... | collective-permute-start | bytes 1179656 | tf_op jit(solution)/shard_map/ppermute | solution.py:333
  16.6 10.5 %collective-permute-start.1 = (bf16[64,3072]{1,0:T(8,128)(2,1)S(1)}, bf16[64,3072]{1,0:T(8,128)(2,1)S(1)}, u32[]{:S(2)}, u32[]{:S(2)}) collective-permute-start(bf16[64,3072]{1,0:T(8,128)(2,1)S(1)} %get-tuple-element.59), channel_id=1, source_target_pairs={{0,64},{1,9},{8,72},{9,17},{16,80},{17,25},{24,88},{25,1},{64,128}... | collective-permute-start | bytes 1179656 | tf_op jit(solution)/shard_map/ppermute | solution.py:333
  17.2 10.0 %collective-permute-start.2 = (bf16[64,3072]{1,0:T(8,128)(2,1)S(1)}, bf16[64,3072]{1,0:T(8,128)(2,1)S(1)}, u32[]{:S(2)}, u32[]{:S(2)}) collective-permute-start(bf16[64,3072]{1,0:T(8,128)(2,1)S(1)} %get-tuple-element.60), channel_id=1, source_target_pairs={{0,192},{1,25},{8,200},{9,1},{16,208},{17,9},{24,216},{25,17},{64,... | collective-permute-start | bytes 1179656 | tf_op jit(solution)/shard_map/ppermute | solution.py:333
  19.9 16.0 %collective-permute-start.9 = (bf16[2,192,384]{2,1,0:T(8,128)(2,1)S(1)}, bf16[2,192,384]{2,1,0:T(8,128)(2,1)S(1)}, u32[]{:S(2)}, u32[]{:S(2)}) collective-permute-start(bf16[2,192,384]{2,1,0:T(8,128)(2,1)S(1)} %get-tuple-element.71), channel_id=1, source_target_pairs={{0,36},{2,38},{4,0},{6,2},{32,4},{34,6},{36,32},{38,34},{1,37},{3,... | collective-permute-start | bytes 884744 | tf_op jit(solution)/shard_map/ppermute | solution.py:33
  25.4 14.8 %collective-permute-start.7 = (bf16[2,192,384]{2,1,0:T(8,128)(2,1)S(1)}, bf16[2,192,384]{2,1,0:T(8,128)(2,1)S(1)}, u32[]{:S(2)}, u32[]{:S(2)}) collective-permute-start(bf16[2,192,384]{2,1,0:T(8,128)(2,1)S(1)} %get-tuple-element.70), channel_id=1, source_target_pairs={{0,4},{2,6},{4,32},{6,34},{32,36},{34,38},{36,0},{38,2},{1,5},{3,7... | collective-permute-start | bytes 884744 | tf_op jit(solution)/shard_map/ppermute | solution.py:33
  27.9 15.8 %collective-permute-start.3 = (bf16[4,32,3840]{2,1,0:T(8,128)(2,1)S(1)}, bf16[4,32,3840]{2,1,0:T(8,128)(2,1)S(1)}, u32[]{:S(2)}, u32[]{:S(2)}) collective-permute-start(bf16[4,32,3840]{2,1,0:T(8,128)(2,1)S(1)} %get-tuple-element.66), channel_id=1, source_target_pairs={{0,16},{1,129},{8,24},{9,137},{16,0},{17,145},{24,8},{25,153},{64,... | collective-permute-start | bytes 2949128 | tf_op jit(solution)/shard_map/ppermute | solution.py:333
  31.2 22.9 %collective-permute-start.4 = (bf16[4,32,3840]{2,1,0:T(8,128)(2,1)S(1)}, bf16[4,32,3840]{2,1,0:T(8,128)(2,1)S(1)}, u32[]{:S(2)}, u32[]{:S(2)}) collective-permute-start(bf16[4,32,3840]{2,1,0:T(8,128)(2,1)S(1)} %get-tuple-element.67), channel_id=1, source_target_pairs={{0,8},{1,65},{8,16},{9,73},{16,24},{17,81},{24,0},{25,89},{64,72},... | collective-permute-start | bytes 2949128 | tf_op jit(solution)/shard_map/ppermute | solution.py:333
  31.9 22.6 %collective-permute-start.5 = (bf16[4,32,3840]{2,1,0:T(8,128)(2,1)S(1)}, bf16[4,32,3840]{2,1,0:T(8,128)(2,1)S(1)}, u32[]{:S(2)}, u32[]{:S(2)}) collective-permute-start(bf16[4,32,3840]{2,1,0:T(8,128)(2,1)S(1)} %get-tuple-element.68), channel_id=1, source_target_pairs={{0,24},{1,193},{8,0},{9,201},{16,8},{17,209},{24,16},{25,217},{64,... | collective-permute-start | bytes 2949128 | tf_op jit(solution)/shard_map/ppermute | solution.py:333
  35.9 7.6 %collective-permute-start.10 = (bf16[192,384]{1,0:T(8,128)(2,1)S(1)}, bf16[192,384]{1,0:T(8,128)(2,1)S(1)}, u32[]{:S(2)}, u32[]{:S(2)}) collective-permute-start(bf16[192,384]{1,0:T(8,128)(2,1)S(1)} %slice_bitcast_fusion), channel_id=1, source_target_pairs={{0,38},{2,0},{4,2},{6,4},{32,6},{34,32},{36,34},{38,36},{1,39},{3,... | collective-permute-start | bytes 442376 | tf_op jit(solution)/shard_map/ppermute | solution.py:33
  54.5 2.8 %collective-permute-start.11 = (bf16[8,192,384]{2,1,0:T(8,128)(2,1)S(1)}, bf16[8,192,384]{2,1,0:T(8,128)(2,1)S(1)}, u32[]{:S(2)}, u32[]{:S(2)}) collective-permute-start(bf16[8,192,384]{2,1,0:T(8,128)(2,1)S(1)} %constant_dynamic-update-slice_fusion.own), channel_id=1, source_target_pairs={{0,1},{1,0},{2,3},{3,2},{4,5},{5,4},{6,7},{7,6},{8,9},{9,8},{10,11... | collective-permute-start | bytes 3538952 | tf_op jit(solution)/shard_map/ppermute | solution.py:317
  77.4 2.9 %collective-permute-start.12 = (bf16[8,192,384]{2,1,0:T(8,128)(2,1)S(1)}, bf16[8,192,384]{2,1,0:T(8,128)(2,1)S(1)}, u32[]{:S(2)}, u32[]{:S(2)}) collective-permute-start(bf16[8,192,384]{2,1,0:T(8,128)(2,1)S(1)} %get-tuple-element.87), channel_id=1, source_target_pairs={{0,1},{1,0},{2,3},{3,2},{4,5},{5,4},{6,7},{7,6},{8,9},{9,8},{10,11... | collective-permute-start | bytes 3538952 | tf_op jit(solution)/shard_map/ppermute | solution.py:317
  81.9 15.2 %collective-permute-start.17 = (bf16[192,384]{1,0:T(8,128)(2,1)S(1)}, bf16[192,384]{1,0:T(8,128)(2,1)S(1)}, u32[]{:S(2)}, u32[]{:S(2)}) collective-permute-start(bf16[192,384]{1,0:T(8,128)(2,1)S(1)} %get-tuple-element.93), channel_id=1, source_target_pairs={{0,2},{2,4},{4,6},{6,32},{32,34},{34,36},{36,38},{38,0},{1,3},{3,5... | collective-permute-start | bytes 442376 | tf_op jit(solution)/shard_map/ppermute | solution.py:33
  83.0 14.1 %collective-permute-start.18 = (bf16[192,384]{1,0:T(8,128)(2,1)S(1)}, bf16[192,384]{1,0:T(8,128)(2,1)S(1)}, u32[]{:S(2)}, u32[]{:S(2)}) collective-permute-start(bf16[192,384]{1,0:T(8,128)(2,1)S(1)} %get-tuple-element.94), channel_id=1, source_target_pairs={{0,38},{2,0},{4,2},{6,4},{32,6},{34,32},{36,34},{38,36},{1,39},{3,... | collective-permute-start | bytes 442376 | tf_op jit(solution)/shard_map/ppermute | solution.py:33
  84.7 9.0 %collective-permute-start.15 = (bf16[96,384]{1,0:T(8,128)(2,1)S(1)}, bf16[96,384]{1,0:T(8,128)(2,1)S(1)}, u32[]{:S(2)}, u32[]{:S(2)}) collective-permute-start(bf16[96,384]{1,0:T(8,128)(2,1)S(1)} %get-tuple-element.91), channel_id=1, source_target_pairs={{0,4},{2,6},{4,32},{6,34},{32,36},{34,38},{36,0},{38,2},{1,5},{3,7... | collective-permute-start | bytes 221192 | tf_op jit(solution)/shard_map/ppermute | solution.py:33
  87.2 9.8 %collective-permute-start.16 = (bf16[96,384]{1,0:T(8,128)(2,1)S(1)}, bf16[96,384]{1,0:T(8,128)(2,1)S(1)}, u32[]{:S(2)}, u32[]{:S(2)}) collective-permute-start(bf16[96,384]{1,0:T(8,128)(2,1)S(1)} %get-tuple-element.92), channel_id=1, source_target_pairs={{0,36},{2,38},{4,0},{6,2},{32,4},{34,6},{36,32},{38,34},{1,37},{3,... | collective-permute-start | bytes 221192 | tf_op jit(solution)/shard_map/ppermute | solution.py:33
  89.4 12.0 %collective-permute-start.13 = (bf16[192,384]{1,0:T(8,128)(2,1)S(1)}, bf16[192,384]{1,0:T(8,128)(2,1)S(1)}, u32[]{:S(2)}, u32[]{:S(2)}) collective-permute-start(bf16[192,384]{1,0:T(8,128)(2,1)S(1)} %get-tuple-element.89), channel_id=1, source_target_pairs={{0,2},{2,4},{4,6},{6,32},{32,34},{34,36},{36,38},{38,0},{1,3},{3,5... | collective-permute-start | bytes 442376 | tf_op jit(solution)/shard_map/ppermute | solution.py:33
  93.8 7.6 %collective-permute-start.14 = (bf16[192,384]{1,0:T(8,128)(2,1)S(1)}, bf16[192,384]{1,0:T(8,128)(2,1)S(1)}, u32[]{:S(2)}, u32[]{:S(2)}) collective-permute-start(bf16[192,384]{1,0:T(8,128)(2,1)S(1)} %get-tuple-element.90), channel_id=1, source_target_pairs={{0,38},{2,0},{4,2},{6,4},{32,6},{34,32},{36,34},{38,36},{1,39},{3,... | collective-permute-start | bytes 442376 | tf_op jit(solution)/shard_map/ppermute | solution.py:33
  97.2 9.7 %collective-permute-start.19 = (bf16[192,384]{1,0:T(8,128)(2,1)S(1)}, bf16[192,384]{1,0:T(8,128)(2,1)S(1)}, u32[]{:S(2)}, u32[]{:S(2)}) collective-permute-start(bf16[192,384]{1,0:T(8,128)(2,1)S(1)} %get-tuple-element.99), channel_id=1, source_target_pairs={{0,4},{2,6},{4,32},{6,34},{32,36},{34,38},{36,0},{38,2},{1,5},{3,7... | collective-permute-start | bytes 442376 | tf_op jit(solution)/shard_map/ppermute | solution.py:33
  97.2 9.6 %collective-permute-start.20 = (bf16[192,384]{1,0:T(8,128)(2,1)S(1)}, bf16[192,384]{1,0:T(8,128)(2,1)S(1)}, u32[]{:S(2)}, u32[]{:S(2)}) collective-permute-start(bf16[192,384]{1,0:T(8,128)(2,1)S(1)} %get-tuple-element.100), channel_id=1, source_target_pairs={{0,36},{2,38},{4,0},{6,2},{32,4},{34,6},{36,32},{38,34},{1,37},{3,... | collective-permute-start | bytes 442376 | tf_op jit(solution)/shard_map/ppermute | solution.py:33

commit v6 on v5

--- a/solution.py
+++ b/solution.py
@@ -139,7 +139,7 @@
 
 
 def tangent_kernel(info, *refs):
-    pieces, (probe, gain), (context, residual, u_out, w_out), cotangent = refs[:4], refs[4:6], refs[6:10], refs[10]
+    pieces, (probe, gain), (context, r_out, u_out, w_out), (residual, cotangent) = refs[:4], refs[4:6], refs[6:10], refs[10:]
     x, y, c = info[0], info[1], info[3]
     for j in range(4):
         for k in range(4):
@@ -151,6 +151,7 @@
             cotangent[row, :] = pieces[j][k, :, W + D :]
     u_out[...] = lax.dot_general(probe[...], context[...], NT, preferred_element_type=F32)
     w_out[...] = turned(cotangent[...]) * gain[...]
+    r_out[...] = turned(residual[...])
 
 
 def turned(v):
@@ -162,9 +163,8 @@
     return pl.pallas_call(
         tangent_kernel,
         in_specs=[pl.BlockSpec(memory_space=pltpu.SMEM)] + [pl.BlockSpec(memory_space=pltpu.VMEM)] * 6,
-        out_shape=[jax.ShapeDtypeStruct((TOK, W), BF16), jax.ShapeDtypeStruct((TOK, D), BF16)]
-        + [jax.ShapeDtypeStruct((D, TOK), F32)] * 2,
-        scratch_shapes=[pltpu.VMEM((TOK, D), BF16)],
+        out_shape=[jax.ShapeDtypeStruct((TOK, W), BF16)] + [jax.ShapeDtypeStruct((D, TOK), F32)] * 3,
+        scratch_shapes=[pltpu.VMEM((TOK, D), BF16)] * 2,
         compiler_params=pltpu.CompilerParams(vmem_limit_bytes=16 * MIB),
         cost_estimate=pl.CostEstimate(flops=2 * D * TOK * W, bytes_accessed=8 * TOK * W, transcendentals=0),
     )(info, *pieces, probe, gain)
@@ -178,7 +178,7 @@
             rows = slice(zh * R, (zh + 1) * R)
             weight[rows, pl.ds(pl.multiple_of((zl * 2 + c) * F, F), F)] = own[at]
             weight[rows, pl.ds(pl.multiple_of((zl * 2 + 1 - c) * F, F), F)] = other[at]
-    s = turned(residual[...]) + lax.dot_general(weight[...], context[...], NT, preferred_element_type=F32)
+    s = residual[...] + lax.dot_general(weight[...], context[...], NT, preferred_element_type=F32)
     s_out[...] = s
     u, w = u_in[...], w_in[...]
     mean = lambda v: jnp.sum(v, axis=0, keepdims=True) * (1.0 / D)

time: 109 us -> 109 us (level)
  no operation moved by 1% of the time
where the time goes in v6:
time: 109 us; the launch traced here: 108 us
  starting transfers between devices  44.2 us (41%)
  waiting for transfers between devices  29.2 us (27%)
  Pallas kernels  16 us (15%)
  blocking collectives  14.9 us (14%)
  local copies, waits for them, and re-layouts  3.76 us (3%)
    ppermute x13, starting transfers between devices, shift(): return lax.ppermute(v, axis, [(s, (s + k) % n) for s in range(n)])  25.1 us
    all_to_all x1, blocking collectives, on_device(): lax.all_to_all(jnp.broadcast_to(stats[None], (16, 8, TOK)), XY, 0, 0, til...  14.9 us
    ppermute x13, waiting for transfers between devices, shift(): return lax.ppermute(v, axis, [(s, (s + k) % n) for s in range(n)])  13.1 us
    ppermute x6, starting transfers between devices, leg(): out.append(lax.ppermute(blocks[k], XYC, pairs))  12.9 us
    ppermute x6, waiting for transfers between devices, leg(): out.append(lax.ppermute(blocks[k], XYC, pairs))  12.7 us
    all_to_all x1, starting transfers between devices, on_device(): rows = lax.all_to_all(context.reshape(8, OWN, F), T, 0, 0, tiled=True)  6.14 us
    pallas_call x1, Pallas kernels, make_probe(): pl.pallas_call(probe_kernel, grid=(8,), in_specs=[pl.BlockSpec(memory_spa...  3.21 us
    ppermute x2, waiting for transfers between devices, swap(): return lax.ppermute(v, 'c', [(0, 1), (1, 0)])  3.05 us
  transfers between devices with their start and end apart: 22, of which 12 were waited for; matrix products, arithmetic and copies ran while one was open for 2% of the time, Pallas kernels for 7%

profile of v6, /device:TPU:32, one launch (start us, length us, event | category | flops | bytes accessed | tf_op | source)
XLA Modules:
  0.0 108.3 jit_solution(1785321038458022710)
XLA Ops:
  0.0 6.1 %all-to-all-start = ((bf16[8,32,384]{2,1,0:T(8,128)(2,1)}), bf16[8,32,384]{2,1,0:T(8,128)(2,1)S(1)}, u32[]{:S(2)}, u32[]{:S(2)}) async-start(bf16[8,32,384]{2,1,0:T(8,128)(2,1)} %bitcast.14), calls=%async_computation | async-start | bytes 393216 | tf_op jit(solution)/shard_map/all_to_all | solution.py:342
  6.2 2.0 %collective-permute-start.6 = (bf16[192,384]{1,0:T(8,128)(2,1)}, bf16[192,384]{1,0:T(8,128)(2,1)S(1)}, u32[]{:S(2)}, u32[]{:S(2)}) collective-permute-start(bf16[192,384]{1,0:T(8,128)(2,1)} %param.8), channel_id=1, source_target_pairs={{0,2},{2,4},{4,6},{6,32},{32,34},{34,36},{36,38},{38,0},{1,3},{3,5... | collective-permute-start | bytes 442376 | tf_op jit(solution)/shard_map/ppermute | solution.py:33
  9.7 1.0 copy-done
  10.7 1.0 copy-done.1
  11.7 1.2 %shard_map.64 = (bf16[4,32,3072]{2,1,0:T(8,128)(2,1)S(1)}, f32[384,1]{1,0:T(8,128)S(1)}) custom-call(s32[6]{0:T(128)S(1)} %concatenate.6.info, bf16[32,6144]{1,0:T(8,128)(2,1)S(1)} %copy-done, bf16[32,6144]{1,0:T(8,128)(2,1)S(1)} %copy-done.1, f32[32,192]{1,0:T(8,128)S(1)} %reshape.8.gains), custom_call_target="tpu_custom_call" | custom-call | bytes 1572864 | tf_op jit(solution)/shard_map/pallas_call | solution.py:96
  13.5 3.1 %collective-permute-start = (bf16[64,3072]{1,0:T(8,128)(2,1)S(1)}, bf16[64,3072]{1,0:T(8,128)(2,1)S(1)}, u32[]{:S(2)}, u32[]{:S(2)}) collective-permute-start(bf16[64,3072]{1,0:T(8,128)(2,1)S(1)} %get-tuple-element.58), channel_id=1, source_target_pairs={{0,128},{1,17},{8,136},{9,25},{16,144},{17,1},{24,152},{25,9},{64,... | collective-permute-start | bytes 1179656 | tf_op jit(solution)/shard_map/ppermute | solution.py:333
  17.2 2.6 %collective-permute-start.2 = (bf16[64,3072]{1,0:T(8,128)(2,1)S(1)}, bf16[64,3072]{1,0:T(8,128)(2,1)S(1)}, u32[]{:S(2)}, u32[]{:S(2)}) collective-permute-start(bf16[64,3072]{1,0:T(8,128)(2,1)S(1)} %get-tuple-element.60), channel_id=1, source_target_pairs={{0,192},{1,25},{8,200},{9,1},{16,208},{17,9},{24,216},{25,17},{64,... | collective-permute-start | bytes 1179656 | tf_op jit(solution)/shard_map/ppermute | solution.py:333
  19.9 5.5 %collective-permute-start.9 = (bf16[2,192,384]{2,1,0:T(8,128)(2,1)S(1)}, bf16[2,192,384]{2,1,0:T(8,128)(2,1)S(1)}, u32[]{:S(2)}, u32[]{:S(2)}) collective-permute-start(bf16[2,192,384]{2,1,0:T(8,128)(2,1)S(1)} %get-tuple-element.71), channel_id=1, source_target_pairs={{0,36},{2,38},{4,0},{6,2},{32,4},{34,6},{36,32},{38,34},{1,37},{3,... | collective-permute-start | bytes 884744 | tf_op jit(solution)/shard_map/ppermute | solution.py:33
  25.4 1.6 %collective-permute-done.1.refs_1_ = bf16[64,3072]{1,0:T(8,128)(2,1)S(1)} collective-permute-done((bf16[64,3072]{1,0:T(8,128)(2,1)S(1)}, bf16[64,3072]{1,0:T(8,128)(2,1)S(1)}, u32[]{:S(2)}, u32[]{:S(2)}) %collective-permute-start.1) | collective-permute-done | bytes 393248 | tf_op jit(solution)/shard_map/ppermute | solution.py:333
  27.9 3.3 %collective-permute-start.3 = (bf16[4,32,3840]{2,1,0:T(8,128)(2,1)S(1)}, bf16[4,32,3840]{2,1,0:T(8,128)(2,1)S(1)}, u32[]{:S(2)}, u32[]{:S(2)}) collective-permute-start(bf16[4,32,3840]{2,1,0:T(8,128)(2,1)S(1)} %get-tuple-element.66), channel_id=1, source_target_pairs={{0,16},{1,129},{8,24},{9,137},{16,0},{17,145},{24,8},{25,153},{64,... | collective-permute-start | bytes 2949128 | tf_op jit(solution)/shard_map/ppermute | solution.py:333
  31.9 2.6 %collective-permute-start.5 = (bf16[4,32,3840]{2,1,0:T(8,128)(2,1)S(1)}, bf16[4,32,3840]{2,1,0:T(8,128)(2,1)S(1)}, u32[]{:S(2)}, u32[]{:S(2)}) collective-permute-start(bf16[4,32,3840]{2,1,0:T(8,128)(2,1)S(1)} %get-tuple-element.68), channel_id=1, source_target_pairs={{0,24},{1,193},{8,0},{9,201},{16,8},{17,209},{24,16},{25,217},{64,... | collective-permute-start | bytes 2949128 | tf_op jit(solution)/shard_map/ppermute | solution.py:333
  34.5 1.4 %collective-permute-done.9 = bf16[2,192,384]{2,1,0:T(8,128)(2,1)S(1)} collective-permute-done((bf16[2,192,384]{2,1,0:T(8,128)(2,1)S(1)}, bf16[2,192,384]{2,1,0:T(8,128)(2,1)S(1)}, u32[]{:S(2)}, u32[]{:S(2)}) %collective-permute-start.9) | collective-permute-done | bytes 294944 | tf_op jit(solution)/shard_map/ppermute | solution.py:33
  35.9 1.4 %collective-permute-start.10 = (bf16[192,384]{1,0:T(8,128)(2,1)S(1)}, bf16[192,384]{1,0:T(8,128)(2,1)S(1)}, u32[]{:S(2)}, u32[]{:S(2)}) collective-permute-start(bf16[192,384]{1,0:T(8,128)(2,1)S(1)} %slice_bitcast_fusion), channel_id=1, source_target_pairs={{0,38},{2,0},{4,2},{6,4},{32,6},{34,32},{36,34},{38,36},{1,39},{3,... | collective-permute-start | bytes 442376 | tf_op jit(solution)/shard_map/ppermute | solution.py:33
  37.3 2.9 %collective-permute-done.7 = bf16[2,192,384]{2,1,0:T(8,128)(2,1)S(1)} collective-permute-done((bf16[2,192,384]{2,1,0:T(8,128)(2,1)S(1)}, bf16[2,192,384]{2,1,0:T(8,128)(2,1)S(1)}, u32[]{:S(2)}, u32[]{:S(2)}) %collective-permute-start.7) | collective-permute-done | bytes 294944 | tf_op jit(solution)/shard_map/ppermute | solution.py:33
  40.3 3.2 %shard_map.67.refs_4_ = bf16[384,3072]{1,0:T(8,128)(2,1)S(1)} custom-call(s32[6]{0:T(128)S(1)} %concatenate.6.info), custom_call_target="tpu_custom_call" | custom-call | flops 16515072 | bytes 2359296 | tf_op jit(solution)/shard_map/pallas_call | solution.py:55
  43.7 10.4 %collective-permute-done.4.refs_1_ = bf16[4,32,3840]{2,1,0:T(8,128)(2,1)S(1)} collective-permute-done((bf16[4,32,3840]{2,1,0:T(8,128)(2,1)S(1)}, bf16[4,32,3840]{2,1,0:T(8,128)(2,1)S(1)}, u32[]{:S(2)}, u32[]{:S(2)}) %collective-permute-start.4) | collective-permute-done | bytes 983072 | tf_op jit(solution)/shard_map/ppermute | solution.py:333
  54.6 2.6 %shard_map.68 = (bf16[512,3072]{1,0:T(8,128)(2,1)S(1)}, f32[384,512]{1,0:T(8,128)S(1)}, f32[384,512]{1,0:T(8,128)S(1)}, f32[384,512]{1,0:T(8,128)S(1)}) custom-call(s32[6]{0:T(128)S(1)} %concatenate.6.info, bf16[4,32,3840]{2,1,0:T(8,128)(2,1)S(1)} %get-tuple-element.74.refs_0_, bf16[4,32,3840]{2,1,0:T(8,128)(2,1)S(1)} %collective-permute-done.4.refs_1_, ...), custom_call_target="tpu_custom_call" | custom-call | flops 1207959552 | bytes 12582912 | tf_op jit(solution)/shard_map/pallas_call | solution.py:163
  57.4 2.7 %shard_map.69 = (f32[384,512]{1,0:T(8,128)S(1)}, f32[8,512]{1,0:T(8,128)S(1)}) custom-call(s32[6]{0:T(128)S(1)} %concatenate.6.info, bf16[8,192,384]{2,1,0:T(8,128)(2,1)S(1)} %constant_dynamic-update-slice_fusion.own, bf16[8,192,384]{2,1,0:T(8,128)(2,1)S(1)} %collective-permute-done.11.other, bf16[512,3072]{1,0:T(8,128)(2,1)S(1)} %get-tuple-element.80.context, ...), custom_call_target="tpu_custom_call" | custom-call | flops 1207959552 | bytes 12582912 | tf_op jit(solution)/shard_map/pallas_call | solution.py:198
  60.1 14.9 %all_to_all.10.stats = f32[16,8,512]{2,1,0:T(8,128)S(1)} all-to-all(f32[16,8,512]{2,1,0:T(8,128)S(1)} %broadcast_in_dim.5), channel_id=1, replica_groups=mesh['x'=4,'zh'=2,'y'=4,'zl'=4,'c'=2] {'x','y'}, dimensions={0} | all-to-all | bytes 524288 | tf_op jit(solution)/shard_map/all_to_all | solution.py:359
  75.0 2.3 %shard_map.70 = (bf16[384,512]{1,0:T(8,128)(2,1)S(1)}, bf16[8,192,384]{2,1,0:T(8,128)(2,1)S(1)}) custom-call(s32[6]{0:T(128)S(1)} %concatenate.6.info, f32[16,8,512]{2,1,0:T(8,128)S(1)} %all_to_all.10.stats, f32[384,512]{1,0:T(8,128)S(1)} %get-tuple-element.85.s, f32[384,512]{1,0:T(8,128)S(1)} %get-tuple-element.82.u_in.u, ...), custom_call_target="tpu_custom_call" | custom-call | flops 603979776 | bytes 12582912 | tf_op jit(solution)/shard_map/pallas_call | solution.py:244
  77.4 2.8 %collective-permute-done.12.received = bf16[8,192,384]{2,1,0:T(8,128)(2,1)S(1)} collective-permute-done((bf16[8,192,384]{2,1,0:T(8,128)(2,1)S(1)}, bf16[8,192,384]{2,1,0:T(8,128)(2,1)S(1)}, u32[]{:S(2)}, u32[]{:S(2)}) %collective-permute-start.12) | collective-permute-done | bytes 1179680 | tf_op jit(solution)/shard_map/ppermute | solution.py:317
  80.3 1.6 %shard_map.71 = (bf16[192,384]{1,0:T(8,128)(2,1)S(1)}, bf16[192,384]{1,0:T(8,128)(2,1)S(1)}, bf16[192,384]{1,0:T(8,128)(2,1)S(1)}, bf16[192,384]{1,0:T(8,128)(2,...) custom-call(s32[6]{0:T(128)S(1)} %concatenate.6.info, ...), custom_call_target="tpu_custom_call" | custom-call | flops 603979776 | bytes 12582912 | tf_op jit(solution)/shard_map/pallas_call | solution.py:271
  81.8 1.1 %collective-permute-start.17 = (bf16[192,384]{1,0:T(8,128)(2,1)S(1)}, bf16[192,384]{1,0:T(8,128)(2,1)S(1)}, u32[]{:S(2)}, u32[]{:S(2)}) collective-permute-start(bf16[192,384]{1,0:T(8,128)(2,1)S(1)} %get-tuple-element.93), channel_id=1, source_target_pairs={{0,2},{2,4},{4,6},{6,32},{32,34},{34,36},{36,38},{38,0},{1,3},{3,5... | collective-permute-start | bytes 442376 | tf_op jit(solution)/shard_map/ppermute | solution.py:33
  82.9 1.8 %collective-permute-start.18 = (bf16[192,384]{1,0:T(8,128)(2,1)S(1)}, bf16[192,384]{1,0:T(8,128)(2,1)S(1)}, u32[]{:S(2)}, u32[]{:S(2)}) collective-permute-start(bf16[192,384]{1,0:T(8,128)(2,1)S(1)} %get-tuple-element.94), channel_id=1, source_target_pairs={{0,38},{2,0},{4,2},{6,4},{32,6},{34,32},{36,34},{38,36},{1,39},{3,... | collective-permute-start | bytes 442376 | tf_op jit(solution)/shard_map/ppermute | solution.py:33
  84.7 2.5 %collective-permute-start.15 = (bf16[96,384]{1,0:T(8,128)(2,1)S(1)}, bf16[96,384]{1,0:T(8,128)(2,1)S(1)}, u32[]{:S(2)}, u32[]{:S(2)}) collective-permute-start(bf16[96,384]{1,0:T(8,128)(2,1)S(1)} %get-tuple-element.91), channel_id=1, source_target_pairs={{0,4},{2,6},{4,32},{6,34},{32,36},{34,38},{36,0},{38,2},{1,5},{3,7... | collective-permute-start | bytes 221192 | tf_op jit(solution)/shard_map/ppermute | solution.py:33
  87.2 2.1 %collective-permute-start.16 = (bf16[96,384]{1,0:T(8,128)(2,1)S(1)}, bf16[96,384]{1,0:T(8,128)(2,1)S(1)}, u32[]{:S(2)}, u32[]{:S(2)}) collective-permute-start(bf16[96,384]{1,0:T(8,128)(2,1)S(1)} %get-tuple-element.92), channel_id=1, source_target_pairs={{0,36},{2,38},{4,0},{6,2},{32,4},{34,6},{36,32},{38,34},{1,37},{3,... | collective-permute-start | bytes 221192 | tf_op jit(solution)/shard_map/ppermute | solution.py:33
  89.3 1.1 %collective-permute-start.13 = (bf16[192,384]{1,0:T(8,128)(2,1)S(1)}, bf16[192,384]{1,0:T(8,128)(2,1)S(1)}, u32[]{:S(2)}, u32[]{:S(2)}) collective-permute-start(bf16[192,384]{1,0:T(8,128)(2,1)S(1)} %get-tuple-element.89), channel_id=1, source_target_pairs={{0,2},{2,4},{4,6},{6,32},{32,34},{34,36},{36,38},{38,0},{1,3},{3,5... | collective-permute-start | bytes 442376 | tf_op jit(solution)/shard_map/ppermute | solution.py:33
  90.4 3.3 %collective-permute-done.15.four_up = bf16[96,384]{1,0:T(8,128)(2,1)S(1)} collective-permute-done((bf16[96,384]{1,0:T(8,128)(2,1)S(1)}, bf16[96,384]{1,0:T(8,128)(2,1)S(1)}, u32[]{:S(2)}, u32[]{:S(2)}) %collective-permute-start.15) | collective-permute-done | bytes 73760 | tf_op jit(solution)/shard_map/ppermute | solution.py:33
  93.8 3.3 %collective-permute-start.14 = (bf16[192,384]{1,0:T(8,128)(2,1)S(1)}, bf16[192,384]{1,0:T(8,128)(2,1)S(1)}, u32[]{:S(2)}, u32[]{:S(2)}) collective-permute-start(bf16[192,384]{1,0:T(8,128)(2,1)S(1)} %get-tuple-element.90), channel_id=1, source_target_pairs={{0,38},{2,0},{4,2},{6,4},{32,6},{34,32},{36,34},{38,36},{1,39},{3,... | collective-permute-start | bytes 442376 | tf_op jit(solution)/shard_map/ppermute | solution.py:33
  97.2 4.1 %collective-permute-start.20 = (bf16[192,384]{1,0:T(8,128)(2,1)S(1)}, bf16[192,384]{1,0:T(8,128)(2,1)S(1)}, u32[]{:S(2)}, u32[]{:S(2)}) collective-permute-start(bf16[192,384]{1,0:T(8,128)(2,1)S(1)} %get-tuple-element.100), channel_id=1, source_target_pairs={{0,36},{2,38},{4,0},{6,2},{32,4},{34,6},{36,32},{38,34},{1,37},{3,... | collective-permute-start | bytes 442376 | tf_op jit(solution)/shard_map/ppermute | solution.py:33
  101.3 5.5 %collective-permute-done.19.up = bf16[192,384]{1,0:T(8,128)(2,1)S(1)} collective-permute-done((bf16[192,384]{1,0:T(8,128)(2,1)S(1)}, bf16[192,384]{1,0:T(8,128)(2,1)S(1)}, u32[]{:S(2)}, u32[]{:S(2)}) %collective-permute-start.19) | collective-permute-done | bytes 147488 | tf_op jit(solution)/shard_map/ppermute | solution.py:33
  106.9 1.5 %shard_map.73 = f32[192,384]{1,0:T(8,128)} custom-call(s32[6]{0:T(128)S(1)} %concatenate.6.info, f32[3,192,384]{2,1,0:T(8,128)S(1)} %get-tuple-element.88.kept, bf16[192,384]{1,0:T(8,128)(2,1)S(1)} %collective-permute-done.13.a, bf16[192,384]{1,0:T(8,128)(2,1)S(1)} %collective-permute-done.14.b, bf16[192,384]{1,0:T(8,128)(2,1)S(1)} %collective-permute-done.19.up, ...), custom_call_target="tpu_custom_call" | custom-call | flops 1474560 | bytes 1474560 | tf_op jit(solution)/shard_map/pallas_call | solution.py:290
  (39 shorter events, 5.6 us)
Async XLA Ops:
  0.0 19.8 %copy-start.2 = (bf16[192,384]{1,0:T(8,128)(2,1)S(1)}, bf16[192,384]{1,0:T(8,128)(2,1)}, u32[]{:S(2)}) copy-start(bf16[192,384]{1,0:T(8,128)(2,1)} %param.8) | copy-start | bytes 442372
  0.0 13.3 %all-to-all-start = ((bf16[8,32,384]{2,1,0:T(8,128)(2,1)}), bf16[8,32,384]{2,1,0:T(8,128)(2,1)S(1)}, u32[]{:S(2)}, u32[]{:S(2)}) async-start(bf16[8,32,384]{2,1,0:T(8,128)(2,1)} %bitcast.14), calls=%async_computation | async-start | bytes 393216 | tf_op jit(solution)/shard_map/all_to_all | solution.py:342
  6.1 13.7 %collective-permute-start.8 = (bf16[192,384]{1,0:T(8,128)(2,1)}, bf16[192,384]{1,0:T(8,128)(2,1)S(1)}, u32[]{:S(2)}, u32[]{:S(2)}) collective-permute-start(bf16[192,384]{1,0:T(8,128)(2,1)} %param.8), channel_id=1, source_target_pairs={{0,38},{2,0},{4,2},{6,4},{32,6},{34,32},{36,34},{38,36},{1,39},{3,... | collective-permute-start | bytes 442376 | tf_op jit(solution)/shard_map/ppermute | solution.py:33
  6.2 13.6 %collective-permute-start.6 = (bf16[192,384]{1,0:T(8,128)(2,1)}, bf16[192,384]{1,0:T(8,128)(2,1)S(1)}, u32[]{:S(2)}, u32[]{:S(2)}) collective-permute-start(bf16[192,384]{1,0:T(8,128)(2,1)} %param.8), channel_id=1, source_target_pairs={{0,2},{2,4},{4,6},{6,32},{32,34},{34,36},{36,38},{38,0},{1,3},{3,5... | collective-permute-start | bytes 442376 | tf_op jit(solution)/shard_map/ppermute | solution.py:33
  9.7 1.0 copy-start
  10.7 1.0 copy-start.1
  13.5 11.9 %collective-permute-start = (bf16[64,3072]{1,0:T(8,128)(2,1)S(1)}, bf16[64,3072]{1,0:T(8,128)(2,1)S(1)}, u32[]{:S(2)}, u32[]{:S(2)}) collective-permute-start(bf16[64,3072]{1,0:T(8,128)(2,1)S(1)} %get-tuple-element.58), channel_id=1, source_target_pairs={{0,128},{1,17},{8,136},{9,25},{16,144},{17,1},{24,152},{25,9},{64,... | collective-permute-start | bytes 1179656 | tf_op jit(solution)/shard_map/ppermute | solution.py:333
  16.6 10.5 %collective-permute-start.1 = (bf16[64,3072]{1,0:T(8,128)(2,1)S(1)}, bf16[64,3072]{1,0:T(8,128)(2,1)S(1)}, u32[]{:S(2)}, u32[]{:S(2)}) collective-permute-start(bf16[64,3072]{1,0:T(8,128)(2,1)S(1)} %get-tuple-element.59), channel_id=1, source_target_pairs={{0,64},{1,9},{8,72},{9,17},{16,80},{17,25},{24,88},{25,1},{64,128}... | collective-permute-start | bytes 1179656 | tf_op jit(solution)/shard_map/ppermute | solution.py:333
  17.2 10.0 %collective-permute-start.2 = (bf16[64,3072]{1,0:T(8,128)(2,1)S(1)}, bf16[64,3072]{1,0:T(8,128)(2,1)S(1)}, u32[]{:S(2)}, u32[]{:S(2)}) collective-permute-start(bf16[64,3072]{1,0:T(8,128)(2,1)S(1)} %get-tuple-element.60), channel_id=1, source_target_pairs={{0,192},{1,25},{8,200},{9,1},{16,208},{17,9},{24,216},{25,17},{64,... | collective-permute-start | bytes 1179656 | tf_op jit(solution)/shard_map/ppermute | solution.py:333
  19.9 16.0 %collective-permute-start.9 = (bf16[2,192,384]{2,1,0:T(8,128)(2,1)S(1)}, bf16[2,192,384]{2,1,0:T(8,128)(2,1)S(1)}, u32[]{:S(2)}, u32[]{:S(2)}) collective-permute-start(bf16[2,192,384]{2,1,0:T(8,128)(2,1)S(1)} %get-tuple-element.71), channel_id=1, source_target_pairs={{0,36},{2,38},{4,0},{6,2},{32,4},{34,6},{36,32},{38,34},{1,37},{3,... | collective-permute-start | bytes 884744 | tf_op jit(solution)/shard_map/ppermute | solution.py:33
  25.4 14.8 %collective-permute-start.7 = (bf16[2,192,384]{2,1,0:T(8,128)(2,1)S(1)}, bf16[2,192,384]{2,1,0:T(8,128)(2,1)S(1)}, u32[]{:S(2)}, u32[]{:S(2)}) collective-permute-start(bf16[2,192,384]{2,1,0:T(8,128)(2,1)S(1)} %get-tuple-element.70), channel_id=1, source_target_pairs={{0,4},{2,6},{4,32},{6,34},{32,36},{34,38},{36,0},{38,2},{1,5},{3,7... | collective-permute-start | bytes 884744 | tf_op jit(solution)/shard_map/ppermute | solution.py:33
  27.9 15.8 %collective-permute-start.3 = (bf16[4,32,3840]{2,1,0:T(8,128)(2,1)S(1)}, bf16[4,32,3840]{2,1,0:T(8,128)(2,1)S(1)}, u32[]{:S(2)}, u32[]{:S(2)}) collective-permute-start(bf16[4,32,3840]{2,1,0:T(8,128)(2,1)S(1)} %get-tuple-element.66), channel_id=1, source_target_pairs={{0,16},{1,129},{8,24},{9,137},{16,0},{17,145},{24,8},{25,153},{64,... | collective-permute-start | bytes 2949128 | tf_op jit(solution)/shard_map/ppermute | solution.py:333
  31.2 22.9 %collective-permute-start.4 = (bf16[4,32,3840]{2,1,0:T(8,128)(2,1)S(1)}, bf16[4,32,3840]{2,1,0:T(8,128)(2,1)S(1)}, u32[]{:S(2)}, u32[]{:S(2)}) collective-permute-start(bf16[4,32,3840]{2,1,0:T(8,128)(2,1)S(1)} %get-tuple-element.67), channel_id=1, source_target_pairs={{0,8},{1,65},{8,16},{9,73},{16,24},{17,81},{24,0},{25,89},{64,72},... | collective-permute-start | bytes 2949128 | tf_op jit(solution)/shard_map/ppermute | solution.py:333
  31.9 22.6 %collective-permute-start.5 = (bf16[4,32,3840]{2,1,0:T(8,128)(2,1)S(1)}, bf16[4,32,3840]{2,1,0:T(8,128)(2,1)S(1)}, u32[]{:S(2)}, u32[]{:S(2)}) collective-permute-start(bf16[4,32,3840]{2,1,0:T(8,128)(2,1)S(1)} %get-tuple-element.68), channel_id=1, source_target_pairs={{0,24},{1,193},{8,0},{9,201},{16,8},{17,209},{24,16},{25,217},{64,... | collective-permute-start | bytes 2949128 | tf_op jit(solution)/shard_map/ppermute | solution.py:333
  35.9 7.6 %collective-permute-start.10 = (bf16[192,384]{1,0:T(8,128)(2,1)S(1)}, bf16[192,384]{1,0:T(8,128)(2,1)S(1)}, u32[]{:S(2)}, u32[]{:S(2)}) collective-permute-start(bf16[192,384]{1,0:T(8,128)(2,1)S(1)} %slice_bitcast_fusion), channel_id=1, source_target_pairs={{0,38},{2,0},{4,2},{6,4},{32,6},{34,32},{36,34},{38,36},{1,39},{3,... | collective-permute-start | bytes 442376 | tf_op jit(solution)/shard_map/ppermute | solution.py:33
  54.5 2.8 %collective-permute-start.11 = (bf16[8,192,384]{2,1,0:T(8,128)(2,1)S(1)}, bf16[8,192,384]{2,1,0:T(8,128)(2,1)S(1)}, u32[]{:S(2)}, u32[]{:S(2)}) collective-permute-start(bf16[8,192,384]{2,1,0:T(8,128)(2,1)S(1)} %constant_dynamic-update-slice_fusion.own), channel_id=1, source_target_pairs={{0,1},{1,0},{2,3},{3,2},{4,5},{5,4},{6,7},{7,6},{8,9},{9,8},{10,11... | collective-permute-start | bytes 3538952 | tf_op jit(solution)/shard_map/ppermute | solution.py:317
  77.3 2.9 %collective-permute-start.12 = (bf16[8,192,384]{2,1,0:T(8,128)(2,1)S(1)}, bf16[8,192,384]{2,1,0:T(8,128)(2,1)S(1)}, u32[]{:S(2)}, u32[]{:S(2)}) collective-permute-start(bf16[8,192,384]{2,1,0:T(8,128)(2,1)S(1)} %get-tuple-element.87), channel_id=1, source_target_pairs={{0,1},{1,0},{2,3},{3,2},{4,5},{5,4},{6,7},{7,6},{8,9},{9,8},{10,11... | collective-permute-start | bytes 3538952 | tf_op jit(solution)/shard_map/ppermute | solution.py:317
  81.8 15.2 %collective-permute-start.17 = (bf16[192,384]{1,0:T(8,128)(2,1)S(1)}, bf16[192,384]{1,0:T(8,128)(2,1)S(1)}, u32[]{:S(2)}, u32[]{:S(2)}) collective-permute-start(bf16[192,384]{1,0:T(8,128)(2,1)S(1)} %get-tuple-element.93), channel_id=1, source_target_pairs={{0,2},{2,4},{4,6},{6,32},{32,34},{34,36},{36,38},{38,0},{1,3},{3,5... | collective-permute-start | bytes 442376 | tf_op jit(solution)/shard_map/ppermute | solution.py:33
  82.9 14.1 %collective-permute-start.18 = (bf16[192,384]{1,0:T(8,128)(2,1)S(1)}, bf16[192,384]{1,0:T(8,128)(2,1)S(1)}, u32[]{:S(2)}, u32[]{:S(2)}) collective-permute-start(bf16[192,384]{1,0:T(8,128)(2,1)S(1)} %get-tuple-element.94), channel_id=1, source_target_pairs={{0,38},{2,0},{4,2},{6,4},{32,6},{34,32},{36,34},{38,36},{1,39},{3,... | collective-permute-start | bytes 442376 | tf_op jit(solution)/shard_map/ppermute | solution.py:33
  84.7 9.0 %collective-permute-start.15 = (bf16[96,384]{1,0:T(8,128)(2,1)S(1)}, bf16[96,384]{1,0:T(8,128)(2,1)S(1)}, u32[]{:S(2)}, u32[]{:S(2)}) collective-permute-start(bf16[96,384]{1,0:T(8,128)(2,1)S(1)} %get-tuple-element.91), channel_id=1, source_target_pairs={{0,4},{2,6},{4,32},{6,34},{32,36},{34,38},{36,0},{38,2},{1,5},{3,7... | collective-permute-start | bytes 221192 | tf_op jit(solution)/shard_map/ppermute | solution.py:33
  87.2 9.8 %collective-permute-start.16 = (bf16[96,384]{1,0:T(8,128)(2,1)S(1)}, bf16[96,384]{1,0:T(8,128)(2,1)S(1)}, u32[]{:S(2)}, u32[]{:S(2)}) collective-permute-start(bf16[96,384]{1,0:T(8,128)(2,1)S(1)} %get-tuple-element.92), channel_id=1, source_target_pairs={{0,36},{2,38},{4,0},{6,2},{32,4},{34,6},{36,32},{38,34},{1,37},{3,... | collective-permute-start | bytes 221192 | tf_op jit(solution)/shard_map/ppermute | solution.py:33
  89.3 12.0 %collective-permute-start.13 = (bf16[192,384]{1,0:T(8,128)(2,1)S(1)}, bf16[192,384]{1,0:T(8,128)(2,1)S(1)}, u32[]{:S(2)}, u32[]{:S(2)}) collective-permute-start(bf16[192,384]{1,0:T(8,128)(2,1)S(1)} %get-tuple-element.89), channel_id=1, source_target_pairs={{0,2},{2,4},{4,6},{6,32},{32,34},{34,36},{36,38},{38,0},{1,3},{3,5... | collective-permute-start | bytes 442376 | tf_op jit(solution)/shard_map/ppermute | solution.py:33
  93.8 7.6 %collective-permute-start.14 = (bf16[192,384]{1,0:T(8,128)(2,1)S(1)}, bf16[192,384]{1,0:T(8,128)(2,1)S(1)}, u32[]{:S(2)}, u32[]{:S(2)}) collective-permute-start(bf16[192,384]{1,0:T(8,128)(2,1)S(1)} %get-tuple-element.90), channel_id=1, source_target_pairs={{0,38},{2,0},{4,2},{6,4},{32,6},{34,32},{36,34},{38,36},{1,39},{3,... | collective-permute-start | bytes 442376 | tf_op jit(solution)/shard_map/ppermute | solution.py:33
  97.1 9.7 %collective-permute-start.19 = (bf16[192,384]{1,0:T(8,128)(2,1)S(1)}, bf16[192,384]{1,0:T(8,128)(2,1)S(1)}, u32[]{:S(2)}, u32[]{:S(2)}) collective-permute-start(bf16[192,384]{1,0:T(8,128)(2,1)S(1)} %get-tuple-element.99), channel_id=1, source_target_pairs={{0,4},{2,6},{4,32},{6,34},{32,36},{34,38},{36,0},{38,2},{1,5},{3,7... | collective-permute-start | bytes 442376 | tf_op jit(solution)/shard_map/ppermute | solution.py:33
  97.2 9.6 %collective-permute-start.20 = (bf16[192,384]{1,0:T(8,128)(2,1)S(1)}, bf16[192,384]{1,0:T(8,128)(2,1)S(1)}, u32[]{:S(2)}, u32[]{:S(2)}) collective-permute-start(bf16[192,384]{1,0:T(8,128)(2,1)S(1)} %get-tuple-element.100), channel_id=1, source_target_pairs={{0,36},{2,38},{4,0},{6,2},{32,4},{34,6},{36,32},{38,34},{1,37},{3,... | collective-permute-start | bytes 442376 | tf_op jit(solution)/shard_map/ppermute | solution.py:33
